TPU v7x, 32 devices: a whole 2x2x4 slice. The times are simulated.
32 devices in a mesh: seq: 8 (over z, y), head: 4 (over x, core).
Axes of the slice: x: 2, y: 2, z: 4, core: 2. Of those that a mesh axis runs over, the one named last changes fastest.
Arguments:
- query_rows: bfloat16 [1024, 2048], P('seq', 'head'), may hold values from -6 to 6
- key_rows: bfloat16 [1024, 2048], P('seq', 'head'), may hold values from -0.52734375 to 0.52734375
- value_rows: bfloat16 [1024, 2048], P('seq', 'head'), may hold values from -6 to 6
- ridge_reg: float32 [16], P('head'), may hold values from 0.5 to 4
- out_weight: bfloat16 [2048, 2048], P('head'), may hold values from -0.125 to 0.125
- out_grad: bfloat16 [1024, 2048], P('seq', 'head'), may hold values from -8 to 8
- doc_ids: int32 [1024], P('seq'), may hold values from 0 to 3, never falling along the last dimension, each value on 1 to 512 neighbouring positions
Outputs:
- layer_out: bfloat16 [1024, 2048], P('seq', 'head')
- grad_queries: bfloat16 [1024, 2048], P('seq', 'head')
- grad_keys: bfloat16 [1024, 2048], P('seq', 'head')
- grad_values: bfloat16 [1024, 2048], P('seq', 'head')
- grad_weight: float32 [2048, 2048], P('seq', 'head')
Inputs may be any that keep to these rules, and one draw needn't show every extreme that they name: `doc_ids`: document numbers never fall along the tokens; every number occurs, each document has 1 to 512 tokens and one has exactly 512.
All inputs are finite; a program needn't handle non-finite values.
Results may differ from a plain program's by a relative error of at most 0.018.
Values may be sent and summed in bfloat16 or wider, within the bound.
No kernel may reach another device: no remote copies, remote signals or barrier semaphores. Data moves between devices by JAX's collectives and lax.ppermute only.
A program may use at most 128 MiB of HBM per device.

v0:
```python
import jax
import jax.numpy as jnp
from jax import lax
from jax.sharding import PartitionSpec as P

CG_STEPS = 4


epsilon = 1e-06


def shortened(value):
    return jax.tree.map(lambda a: a.astype(jnp.bfloat16) if a.dtype == jnp.float32 else a, value)


def shifted(value, axis, by):
    devices = lax.axis_size(axis)
    pairs = [(i, i + by) for i in range(devices) if 0 <= i + by < devices]
    return lax.ppermute(value, axis, pairs)


def matmul_high(left_side, right_side):
    return jnp.dot(
        left_side, right_side, precision=lax.Precision.HIGHEST, preferred_element_type=jnp.float32
    )


def causal_mask(labels):
    length = labels.shape[0]
    row_idx = lax.broadcasted_iota(jnp.int32, (length, length), 0)
    col_idx = lax.broadcasted_iota(jnp.int32, (length, length), 1)
    return ((labels[:, None] == labels[None, :]) & (col_idx <= row_idx)).astype(jnp.float32)


def conj_solve(target, key_rows, same_doc, carried, gram_in, ridge_reg):
    solution = jnp.zeros_like(target)
    residual = target
    direction = target
    res_sq = jnp.sum(residual * residual, axis=1, keepdims=True)
    for number in range(CG_STEPS):
        scores = matmul_high(direction, key_rows.T) * same_doc
        applied = (
            carried[:, None] * matmul_high(direction, gram_in)
            + matmul_high(scores, key_rows)
            + ridge_reg * direction
        )
        step_size = res_sq / (jnp.sum(direction * applied, axis=1, keepdims=True) + epsilon)
        solution = solution + step_size * direction
        residual = residual - step_size * applied
        new_sq = jnp.sum(residual * residual, axis=1, keepdims=True)
        direction = residual + new_sq / (res_sq + epsilon) * direction
        res_sq = new_sq
    return solution


def head_forward(query_rows, key_rows, value_rows, same_doc, carried, gram_in, value_in, ridge_reg):
    solution = conj_solve(query_rows, key_rows, same_doc, carried, gram_in, ridge_reg)
    score_one = matmul_high(solution, key_rows.T) * same_doc
    output = carried[:, None] * matmul_high(solution, value_in.T) + matmul_high(
        score_one, value_rows
    )
    return (solution, output)


def head_dual(
    key_rows,
    value_rows,
    same_doc,
    carried,
    head_rows,
    gram_in,
    value_in,
    ridge_reg,
    solution,
    out_cot,
):
    score_two = matmul_high(out_cot, value_rows.T) * same_doc
    target = carried[:, None] * matmul_high(out_cot, value_in) + matmul_high(score_two, key_rows)
    dual_sol = conj_solve(target, key_rows, same_doc, carried, gram_in, ridge_reg)
    state_part = matmul_high(out_cot.T, head_rows[:, None] * solution)
    cross_sum = matmul_high(dual_sol.T, head_rows[:, None] * solution)
    return (dual_sol, state_part, cross_sum + cross_sum.T, score_two)


def head_grads(
    key_rows,
    value_rows,
    same_doc,
    later_rows,
    solution,
    out_cot,
    dual_sol,
    score_two,
    grad_state,
    gram_grad,
):
    score_one = matmul_high(solution, key_rows.T) * same_doc
    score_three = matmul_high(dual_sol, key_rows.T) * same_doc
    grad_v = later_rows[:, None] * matmul_high(key_rows, grad_state.T) + matmul_high(
        score_one.T, out_cot
    )
    grad_k = later_rows[:, None] * (
        matmul_high(value_rows, grad_state) - matmul_high(key_rows, gram_grad)
    )
    grad_k = (
        grad_k
        + matmul_high(score_two.T, solution)
        - matmul_high(score_one.T, dual_sol)
        - matmul_high(score_three.T, solution)
    )
    return (grad_k, grad_v)


def link_states(earlier, later):
    broken_a, label_a, gram_a, value_a = earlier
    broken_b, label_b, gram_b, value_b = later
    same_label = (label_a == label_b) | (label_a == 0) | (label_b == 0)
    broken = jnp.maximum(jnp.maximum(broken_a, broken_b), 1 - same_label.astype(jnp.int32))
    joined = (broken_b == 0) & same_label
    gram_sum = jnp.where(joined, gram_a + gram_b, gram_b)
    value_sum = jnp.where(joined, value_a + value_b, value_b)
    doc_label = jnp.where(label_b == 0, label_a, label_b)
    return (broken, doc_label, gram_sum, value_sum)


def forward_doubling(element):
    running = element
    stride = 1
    axis_count = lax.axis_size("seq")
    while stride < axis_count:
        moved_state = shifted(
            (
                shortened(running[0]),
                shortened(running[1]),
                shortened(running[2]),
                shortened(running[3]),
            ),
            "seq",
            stride,
        )
        running = link_states(moved_state, running)
        stride = stride * 2
    return shifted(
        (
            shortened(running[0]),
            shortened(running[1]),
            shortened(running[2]),
            shortened(running[3]),
        ),
        "seq",
        1,
    )


def backward_doubling(element):
    running = element
    stride = 1
    axis_count = lax.axis_size("seq")
    while stride < axis_count:
        moved_state = shifted(
            (
                shortened(running[0]),
                shortened(running[1]),
                shortened(running[2]),
                shortened(running[3]),
            ),
            "seq",
            -stride,
        )
        running = link_states(moved_state, running)
        stride = stride * 2
    return shifted(
        (
            shortened(running[0]),
            shortened(running[1]),
            shortened(running[2]),
            shortened(running[3]),
        ),
        "seq",
        -1,
    )


def to_heads(array, heads_here):
    return array.astype(jnp.float32).reshape(array.shape[0], heads_here, -1).transpose(1, 0, 2)


def from_heads(array):
    return array.transpose(1, 0, 2).reshape(array.shape[1], -1)


def per_device(query_rows, key_rows, value_rows, ridge_reg, out_weight, out_grad, doc_ids):
    heads_here = ridge_reg.shape[0]
    query_h = to_heads(query_rows, heads_here)
    key_h = to_heads(key_rows, heads_here)
    value_h = to_heads(value_rows, heads_here)
    same_doc = causal_mask(doc_ids)
    broken_here = (doc_ids[0] != doc_ids[-1]).astype(jnp.int32)
    tail_rows = (doc_ids == doc_ids[-1]).astype(jnp.float32)[None, :, None]
    gram_tail = jnp.einsum(
        "hpk,hpl->hkl",
        key_h * tail_rows,
        key_h,
        precision=lax.Precision.HIGHEST,
        preferred_element_type=jnp.float32,
    )
    value_tail = jnp.einsum(
        "hpv,hpk->hvk",
        value_h * tail_rows,
        key_h,
        precision=lax.Precision.HIGHEST,
        preferred_element_type=jnp.float32,
    )
    element = (broken_here, doc_ids[-1] + 1, gram_tail, value_tail)
    incoming = forward_doubling(element)
    label_in = incoming[1] - 1
    gram_in = incoming[2]
    value_in = incoming[3]
    carried = (doc_ids == label_in).astype(jnp.float32)
    solution, output = jax.vmap(head_forward, in_axes=(0, 0, 0, None, None, 0, 0, 0))(
        query_h, key_h, value_h, same_doc, carried, gram_in, value_in, ridge_reg
    )
    mixed = from_heads(output).astype(jnp.bfloat16)
    partial_out = jnp.dot(mixed, out_weight, preferred_element_type=jnp.float32)
    layer_out = lax.psum_scatter(
        partial_out.astype(jnp.bfloat16), "head", scatter_dimension=1, tiled=True
    )
    cot_full = lax.all_gather(out_grad, "head", axis=1, tiled=True)
    out_cot = to_heads(
        jnp.dot(cot_full, out_weight.T, preferred_element_type=jnp.float32), heads_here
    )
    grad_weight = lax.psum_scatter(
        lax.dot_general(
            cot_full, mixed, (((0,), (0,)), ((), ())), preferred_element_type=jnp.float32
        ),
        "seq",
        scatter_dimension=0,
        tiled=True,
    )
    head_rows = (doc_ids == doc_ids[0]).astype(jnp.float32)
    dual_sol, state_part, gram_part, score_two = jax.vmap(
        head_dual, in_axes=(0, 0, None, None, None, 0, 0, 0, 0, 0)
    )(key_h, value_h, same_doc, carried, head_rows, gram_in, value_in, ridge_reg, solution, out_cot)
    back_element = (broken_here, doc_ids[0] + 1, state_part, gram_part)
    from_later = backward_doubling(back_element)
    later_rows = (doc_ids == from_later[1] - 1).astype(jnp.float32)
    grad_k, grad_v = jax.vmap(head_grads, in_axes=(0, 0, None, None, 0, 0, 0, 0, 0, 0))(
        key_h,
        value_h,
        same_doc,
        later_rows,
        solution,
        out_cot,
        dual_sol,
        score_two,
        from_later[2],
        from_later[3],
    )
    grad_queries = from_heads(dual_sol).astype(jnp.bfloat16)
    grad_keys = from_heads(grad_k).astype(jnp.bfloat16)
    grad_values = from_heads(grad_v).astype(jnp.bfloat16)
    return (layer_out, grad_queries, grad_keys, grad_values, grad_weight)


def solution(mesh):
    in_specs = (
        P("seq", "head"),
        P("seq", "head"),
        P("seq", "head"),
        P("head"),
        P("head", None),
        P("seq", "head"),
        P("seq"),
    )
    out_specs = (
        P("seq", "head"),
        P("seq", "head"),
        P("seq", "head"),
        P("seq", "head"),
        P("seq", "head"),
    )
    return jax.shard_map(
        per_device, mesh=mesh, in_specs=in_specs, out_specs=out_specs, check_vma=False
    )
```

profile of v0, /device:TPU:0, one launch (start us, length us, event | category | flops | bytes accessed | tf_op | source)
XLA Modules:
  0.0 265.5 jit_solution(17588269281264026734)
XLA Ops:
  7.2 1.4 fusion.118
  9.9 6.2 %collective-permute-start.4 = (s32[]{:T(128)}, s32[]{:T(128)}, u32[]{:S(2)}, u32[]{:S(2)}) collective-permute-start(s32[]{:T(128)} %convert_element_type.152), channel_id=1, source_target_pairs={{0,4},{4,8},{8,12},{12,16},{16,20},{20,24},{24,28},{1,5},{5,9},{9,... | collective-permute-start | bytes 20 | tf_op jit(solution)/shard_map/ppermute | solution.py:19
  16.7 1.3 collective-permute-start.14
  18.7 7.1 %collective-permute-start = (s32[]{:T(128)}, s32[]{:T(128)}, u32[]{:S(2)}, u32[]{:S(2)}) collective-permute-start(s32[]{:T(128)} %add.324), channel_id=1, source_target_pairs={{0,4},{4,8},{8,12},{12,16},{16,20},{20,24},{24,28},{1,5},{5,9},{9,... | collective-permute-start | bytes 20 | tf_op jit(solution)/shard_map/ppermute | solution.py:19
  29.7 7.5 %all_gather.3 = bf16[128,2048]{1,0:T(8,128)(2,1)S(1)} all-gather(bf16[128,512]{1,0:T(8,128)(2,1)} %param.12), channel_id=1, replica_groups=mesh['seq'=8,'head'=4] {'head'}, dimensions={1}, use_global_device_ids=true | all-gather | bytes 655360 | tf_op jit(solution)/shard_map/all_gather | solution.py:228
  40.4 1.3 collective-permute-start.15
  42.3 7.1 %collective-permute-start.1 = (s32[]{:T(128)}, s32[]{:T(128)}, u32[]{:S(2)}, u32[]{:S(2)}) collective-permute-start(s32[]{:T(128)} %select_n.81), channel_id=1, source_target_pairs={{0,8},{4,12},{8,16},{12,20},{16,24},{20,28},{1,9},{5,13},{9,17},{1... | collective-permute-start | bytes 20 | tf_op jit(solution)/shard_map/ppermute | solution.py:19
  51.3 4.8 %collective-permute-start.5 = (s32[]{:T(128)}, s32[]{:T(128)}, u32[]{:S(2)}, u32[]{:S(2)}) collective-permute-start(s32[]{:T(128)} %max.25), channel_id=1, source_target_pairs={{0,8},{4,12},{8,16},{12,20},{16,24},{20,28},{1,9},{5,13},{9,17},{1... | collective-permute-start | bytes 20 | tf_op jit(solution)/shard_map/ppermute | solution.py:19
  56.7 1.3 collective-permute-start.16
  58.6 8.0 %collective-permute-start.2 = (s32[]{:T(128)}, s32[]{:T(128)}, u32[]{:S(2)}, u32[]{:S(2)}) collective-permute-start(s32[]{:T(128)} %select_n.82), channel_id=1, source_target_pairs={{0,16},{4,20},{8,24},{12,28},{1,17},{5,21},{9,25},{13,29},{2,18},{... | collective-permute-start | bytes 20 | tf_op jit(solution)/shard_map/ppermute | solution.py:19
  69.2 1.3 collective-permute-start.17
  72.2 7.5 %collective-permute-start.3 = (s32[]{:T(128)}, s32[]{:T(128)}, u32[]{:S(2)}, u32[]{:S(2)}) collective-permute-start(s32[]{:T(128)} %select_n.83), channel_id=1, source_target_pairs={{0,4},{4,8},{8,12},{12,16},{16,20},{20,24},{24,28},{1,5},{5,9},{9,... | collective-permute-start | bytes 20 | tf_op jit(solution)/shard_map/ppermute | solution.py:19
  80.8 1.8 compare_convert_fusion.1
  82.9 4.8 %collective-permute-start.10 = (bf16[4,128,128]{2,1,0:T(8,128)(2,1)S(1)}, bf16[4,128,128]{2,1,0:T(8,128)(2,1)S(1)}, u32[]{:S(2)}, u32[]{:S(2)}) collective-permute-start(bf16[4,128,128]{2,1,0:T(8,128)(2,1)S(1)} %get-tuple-element.33), channel_id=1, source_target_pairs={{0,4},{4,8},{8,12},{12,16},{16,20},{20,24},{24,28},{1,5},{5,9},{9,... | collective-permute-start | bytes 393224 | tf_op jit(solution)/shard_map/ppermute | solution.py:19
  88.0 4.6 %collective-permute-start.6 = (bf16[4,128,128]{2,1,0:T(8,128)(2,1)S(1)}, bf16[4,128,128]{2,1,0:T(8,128)(2,1)S(1)}, u32[]{:S(2)}, u32[]{:S(2)}) collective-permute-start(bf16[4,128,128]{2,1,0:T(8,128)(2,1)S(1)} %get-tuple-element.35), channel_id=1, source_target_pairs={{0,4},{4,8},{8,12},{12,16},{16,20},{20,24},{24,28},{1,5},{5,9},{9,... | collective-permute-start | bytes 393224 | tf_op jit(solution)/shard_map/ppermute | solution.py:19
  92.6 4.1 %collective-permute-start.11 = (bf16[4,128,128]{2,1,0:T(8,128)(2,1)S(1)}, bf16[4,128,128]{2,1,0:T(8,128)(2,1)S(1)}, u32[]{:S(2)}, u32[]{:S(2)}) collective-permute-start(bf16[4,128,128]{2,1,0:T(8,128)(2,1)S(1)} %fusion.65), channel_id=1, source_target_pairs={{0,8},{4,12},{8,16},{12,20},{16,24},{20,28},{1,9},{5,13},{9,17},{1... | collective-permute-start | bytes 393224 | tf_op jit(solution)/shard_map/ppermute | solution.py:19
  96.8 4.0 %collective-permute-start.7 = (bf16[4,128,128]{2,1,0:T(8,128)(2,1)S(1)}, bf16[4,128,128]{2,1,0:T(8,128)(2,1)S(1)}, u32[]{:S(2)}, u32[]{:S(2)}) collective-permute-start(bf16[4,128,128]{2,1,0:T(8,128)(2,1)S(1)} %fusion.64), channel_id=1, source_target_pairs={{0,8},{4,12},{8,16},{12,20},{16,24},{20,28},{1,9},{5,13},{9,17},{1... | collective-permute-start | bytes 393224 | tf_op jit(solution)/shard_map/ppermute | solution.py:19
  100.9 7.0 %collective-permute-start.12 = (bf16[4,128,128]{2,1,0:T(8,128)(2,1)S(1)}, bf16[4,128,128]{2,1,0:T(8,128)(2,1)S(1)}, u32[]{:S(2)}, u32[]{:S(2)}) collective-permute-start(bf16[4,128,128]{2,1,0:T(8,128)(2,1)S(1)} %fusion.97), channel_id=1, source_target_pairs={{0,16},{4,20},{8,24},{12,28},{1,17},{5,21},{9,25},{13,29},{2,18},{... | collective-permute-start | bytes 393224 | tf_op jit(solution)/shard_map/ppermute | solution.py:19
  108.0 1.3 collective-permute-start.8
  110.5 1.9 collective-permute-start.13
  112.5 2.1 collective-permute-start.9
  121.0 1.5 multiply_reduce_fusion
  127.7 1.4 fusion.68
  129.4 2.7 convolution_bitcast_fusion
  132.2 1.3 collective-permute-start.18
  134.7 3.3 %collective-permute-done.18 = s32[]{:T(128)} collective-permute-done((s32[]{:T(128)}, s32[]{:T(128)}, u32[]{:S(2)}, u32[]{:S(2)}) %collective-permute-start.18) | collective-permute-done | bytes 36 | tf_op jit(solution)/shard_map/ppermute | solution.py:19
  138.7 1.3 collective-permute-start.19
  141.3 6.2 %collective-permute-done.19 = s32[]{:T(128)} collective-permute-done((s32[]{:T(128)}, s32[]{:T(128)}, u32[]{:S(2)}, u32[]{:S(2)}) %collective-permute-start.19) | collective-permute-done | bytes 36 | tf_op jit(solution)/shard_map/ppermute | solution.py:19
  149.5 1.4 convolution_multiply_fusion.2
  151.3 1.5 fusion.25
  153.9 1.7 copy.57
  159.4 1.7 fusion.117
  162.4 1.3 fusion.121
  163.7 1.5 collective-permute-start.20
  165.2 2.0 convolution_bitcast_fusion.4
  167.2 2.0 convolution_bitcast_fusion.1
  169.3 1.3 convolution_convert_fusion
  175.6 1.4 collective-permute-start.25
  177.1 14.1 %collective-permute-done.21 = bf16[4,128,128]{2,1,0:T(8,128)(2,1)S(1)} collective-permute-done((bf16[4,128,128]{2,1,0:T(8,128)(2,1)S(1)}, bf16[4,128,128]{2,1,0:T(8,128)(2,1)S(1)}, u32[]{:S(2)}, u32[]{:S(2)}) %collective-permute-start.21) | collective-permute-done | bytes 131104 | tf_op jit(solution)/shard_map/ppermute | solution.py:19
  195.8 5.8 %collective-permute-done.22 = bf16[4,128,128]{2,1,0:T(8,128)(2,1)S(1)} collective-permute-done((bf16[4,128,128]{2,1,0:T(8,128)(2,1)S(1)}, bf16[4,128,128]{2,1,0:T(8,128)(2,1)S(1)}, u32[]{:S(2)}, u32[]{:S(2)}) %collective-permute-start.22) | collective-permute-done | bytes 131104 | tf_op jit(solution)/shard_map/ppermute | solution.py:19
  202.5 1.4 collective-permute-start.23
  204.3 1.7 fusion.30
  207.2 3.7 %collective-permute-done.23 = bf16[4,128,128]{2,1,0:T(8,128)(2,1)S(1)} collective-permute-done((bf16[4,128,128]{2,1,0:T(8,128)(2,1)S(1)}, bf16[4,128,128]{2,1,0:T(8,128)(2,1)S(1)}, u32[]{:S(2)}, u32[]{:S(2)}) %collective-permute-start.23) | collective-permute-done | bytes 131104 | tf_op jit(solution)/shard_map/ppermute | solution.py:19
  211.9 2.9 %collective-permute-done.27 = bf16[4,128,128]{2,1,0:T(8,128)(2,1)} collective-permute-done((bf16[4,128,128]{2,1,0:T(8,128)(2,1)}, bf16[4,128,128]{2,1,0:T(8,128)(2,1)}, u32[]{:S(2)}, u32[]{:S(2)}) %collective-permute-start.27) | collective-permute-done | bytes 131104 | tf_op jit(solution)/shard_map/ppermute | solution.py:19
  217.2 1.3 fusion.3
  219.7 14.5 %reduce-scatter.5.cloned.1.call-done = f32[256,512]{0,1:T(8,128)} async-done(((f32[2048,512]{0,1:T(8,128)}), f32[256,512]{0,1:T(8,128)}) %reduce-scatter.5.cloned.1.call-update) | async-done | bytes 524304 | tf_op jit(solution)/shard_map/reduce_scatter | solution.py:232
  234.1 2.0 copy.60
  236.2 22.5 %reduce-scatter.3.cloned.1.call-done = bf16[128,512]{1,0:T(8,128)(2,1)} async-done(((bf16[128,2048]{1,0:T(8,128)(2,1)}), bf16[128,512]{1,0:T(8,128)(2,1)}) %reduce-scatter.3.cloned.1.call-update) | async-done | bytes 131088 | tf_op jit(solution)/shard_map/reduce_scatter | solution.py:225
  (187 shorter events, 43.3 us)
Async XLA Ops:
  7.2 30.1 %copy-start = (bf16[512,2048]{1,0:T(8,128)(2,1)S(1)}, bf16[512,2048]{1,0:T(8,128)(2,1)}, u32[]{:S(2)}) copy-start(bf16[512,2048]{1,0:T(8,128)(2,1)} %param.11) | copy-start | bytes 6291460
  7.2 226.9 %reduce-scatter.5.cloned.1.call-start = ((), (), s32[]{:S(2)}) async-start(), calls=%async_computation.3 | async-start | bytes 4718592 | tf_op jit(solution)/shard_map/reduce_scatter | solution.py:232
  9.9 40.8 %collective-permute-start.4 = (s32[]{:T(128)}, s32[]{:T(128)}, u32[]{:S(2)}, u32[]{:S(2)}) collective-permute-start(s32[]{:T(128)} %convert_element_type.152), channel_id=1, source_target_pairs={{0,4},{4,8},{8,12},{12,16},{16,20},{20,24},{24,28},{1,5},{5,9},{9,... | collective-permute-start | bytes 20 | tf_op jit(solution)/shard_map/ppermute | solution.py:19
  16.7 23.0 %collective-permute-start.14 = (s32[]{:T(128)}, s32[]{:T(128)}, u32[]{:S(2)}, u32[]{:S(2)}) collective-permute-start(s32[]{:T(128)} %add.387), channel_id=1, source_target_pairs={{4,0},{8,4},{12,8},{16,12},{20,16},{24,20},{28,24},{5,1},{9,5},{13... | collective-permute-start | bytes 20 | tf_op jit(solution)/shard_map/ppermute | solution.py:19
  18.7 23.0 %collective-permute-start = (s32[]{:T(128)}, s32[]{:T(128)}, u32[]{:S(2)}, u32[]{:S(2)}) collective-permute-start(s32[]{:T(128)} %add.324), channel_id=1, source_target_pairs={{0,4},{4,8},{8,12},{12,16},{16,20},{20,24},{24,28},{1,5},{5,9},{9,... | collective-permute-start | bytes 20 | tf_op jit(solution)/shard_map/ppermute | solution.py:19
  26.6 98.7 %copy-start.2 = (f32[128,128]{1,0:T(8,128)}, f32[128,128]{1,0:T(8,128)S(1)}, u32[]{:S(2)}) copy-start(f32[128,128]{1,0:T(8,128)S(1)} %fusion.101) | copy-start | bytes 196612
  37.3 43.6 %copy-start.36 = (s32[128]{0:T(128)S(1)}, s32[128]{0:T(128)}, u32[]{:S(2)}) copy-start(s32[128]{0:T(128)} %param.13) | copy-start | bytes 1540
  38.0 76.9 %copy-start.6 = (f32[128,512]{0,1:T(8,128)}, f32[128,512]{0,1:T(8,128)S(1)}, u32[]{:S(2)}) copy-start(f32[128,512]{0,1:T(8,128)S(1)} %fusion.123) | copy-start | bytes 786436
  38.4 44.5 %copy-start.16 = (f32[4,128,128]{2,1,0:T(8,128)}, f32[4,128,128]{2,1,0:T(8,128)S(1)}, u32[]{:S(2)}) copy-start(f32[4,128,128]{2,1,0:T(8,128)S(1)} %convolution_multiply_fusion.10) | copy-start | bytes 786436
  40.4 15.7 %collective-permute-start.15 = (s32[]{:T(128)}, s32[]{:T(128)}, u32[]{:S(2)}, u32[]{:S(2)}) collective-permute-start(s32[]{:T(128)} %select_n.93), channel_id=1, source_target_pairs={{8,0},{12,4},{16,8},{20,12},{24,16},{28,20},{9,1},{13,5},{17,9},{2... | collective-permute-start | bytes 20 | tf_op jit(solution)/shard_map/ppermute | solution.py:19
  42.3 15.7 %collective-permute-start.1 = (s32[]{:T(128)}, s32[]{:T(128)}, u32[]{:S(2)}, u32[]{:S(2)}) collective-permute-start(s32[]{:T(128)} %select_n.81), channel_id=1, source_target_pairs={{0,8},{4,12},{8,16},{12,20},{16,24},{20,28},{1,9},{5,13},{9,17},{1... | collective-permute-start | bytes 20 | tf_op jit(solution)/shard_map/ppermute | solution.py:19
  51.3 16.6 %collective-permute-start.5 = (s32[]{:T(128)}, s32[]{:T(128)}, u32[]{:S(2)}, u32[]{:S(2)}) collective-permute-start(s32[]{:T(128)} %max.25), channel_id=1, source_target_pairs={{0,8},{4,12},{8,16},{12,20},{16,24},{20,28},{1,9},{5,13},{9,17},{1... | collective-permute-start | bytes 20 | tf_op jit(solution)/shard_map/ppermute | solution.py:19
  56.7 11.9 %collective-permute-start.16 = (s32[]{:T(128)}, s32[]{:T(128)}, u32[]{:S(2)}, u32[]{:S(2)}) collective-permute-start(s32[]{:T(128)} %select_n.94), channel_id=1, source_target_pairs={{16,0},{20,4},{24,8},{28,12},{17,1},{21,5},{25,9},{29,13},{18,2},{... | collective-permute-start | bytes 20 | tf_op jit(solution)/shard_map/ppermute | solution.py:19
  58.6 11.9 %collective-permute-start.2 = (s32[]{:T(128)}, s32[]{:T(128)}, u32[]{:S(2)}, u32[]{:S(2)}) collective-permute-start(s32[]{:T(128)} %select_n.82), channel_id=1, source_target_pairs={{0,16},{4,20},{8,24},{12,28},{1,17},{5,21},{9,25},{13,29},{2,18},{... | collective-permute-start | bytes 20 | tf_op jit(solution)/shard_map/ppermute | solution.py:19
  69.2 10.5 %collective-permute-start.17 = (s32[]{:T(128)}, s32[]{:T(128)}, u32[]{:S(2)}, u32[]{:S(2)}) collective-permute-start(s32[]{:T(128)} %select_n.95), channel_id=1, source_target_pairs={{4,0},{8,4},{12,8},{16,12},{20,16},{24,20},{28,24},{5,1},{9,5},{13... | collective-permute-start | bytes 20 | tf_op jit(solution)/shard_map/ppermute | solution.py:19
  72.2 8.1 %collective-permute-start.3 = (s32[]{:T(128)}, s32[]{:T(128)}, u32[]{:S(2)}, u32[]{:S(2)}) collective-permute-start(s32[]{:T(128)} %select_n.83), channel_id=1, source_target_pairs={{0,4},{4,8},{8,12},{12,16},{16,20},{20,24},{24,28},{1,5},{5,9},{9,... | collective-permute-start | bytes 20 | tf_op jit(solution)/shard_map/ppermute | solution.py:19
  82.9 9.7 %collective-permute-start.10 = (bf16[4,128,128]{2,1,0:T(8,128)(2,1)S(1)}, bf16[4,128,128]{2,1,0:T(8,128)(2,1)S(1)}, u32[]{:S(2)}, u32[]{:S(2)}) collective-permute-start(bf16[4,128,128]{2,1,0:T(8,128)(2,1)S(1)} %get-tuple-element.33), channel_id=1, source_target_pairs={{0,4},{4,8},{8,12},{12,16},{16,20},{20,24},{24,28},{1,5},{5,9},{9,... | collective-permute-start | bytes 393224 | tf_op jit(solution)/shard_map/ppermute | solution.py:19
  88.0 8.7 %collective-permute-start.6 = (bf16[4,128,128]{2,1,0:T(8,128)(2,1)S(1)}, bf16[4,128,128]{2,1,0:T(8,128)(2,1)S(1)}, u32[]{:S(2)}, u32[]{:S(2)}) collective-permute-start(bf16[4,128,128]{2,1,0:T(8,128)(2,1)S(1)} %get-tuple-element.35), channel_id=1, source_target_pairs={{0,4},{4,8},{8,12},{12,16},{16,20},{20,24},{24,28},{1,5},{5,9},{9,... | collective-permute-start | bytes 393224 | tf_op jit(solution)/shard_map/ppermute | solution.py:19
  92.6 8.2 %collective-permute-start.11 = (bf16[4,128,128]{2,1,0:T(8,128)(2,1)S(1)}, bf16[4,128,128]{2,1,0:T(8,128)(2,1)S(1)}, u32[]{:S(2)}, u32[]{:S(2)}) collective-permute-start(bf16[4,128,128]{2,1,0:T(8,128)(2,1)S(1)} %fusion.65), channel_id=1, source_target_pairs={{0,8},{4,12},{8,16},{12,20},{16,24},{20,28},{1,9},{5,13},{9,17},{1... | collective-permute-start | bytes 393224 | tf_op jit(solution)/shard_map/ppermute | solution.py:19
  96.8 11.1 %collective-permute-start.7 = (bf16[4,128,128]{2,1,0:T(8,128)(2,1)S(1)}, bf16[4,128,128]{2,1,0:T(8,128)(2,1)S(1)}, u32[]{:S(2)}, u32[]{:S(2)}) collective-permute-start(bf16[4,128,128]{2,1,0:T(8,128)(2,1)S(1)} %fusion.64), channel_id=1, source_target_pairs={{0,8},{4,12},{8,16},{12,20},{16,24},{20,28},{1,9},{5,13},{9,17},{1... | collective-permute-start | bytes 393224 | tf_op jit(solution)/shard_map/ppermute | solution.py:19
  100.9 9.5 %collective-permute-start.12 = (bf16[4,128,128]{2,1,0:T(8,128)(2,1)S(1)}, bf16[4,128,128]{2,1,0:T(8,128)(2,1)S(1)}, u32[]{:S(2)}, u32[]{:S(2)}) collective-permute-start(bf16[4,128,128]{2,1,0:T(8,128)(2,1)S(1)} %fusion.97), channel_id=1, source_target_pairs={{0,16},{4,20},{8,24},{12,28},{1,17},{5,21},{9,25},{13,29},{2,18},{... | collective-permute-start | bytes 393224 | tf_op jit(solution)/shard_map/ppermute | solution.py:19
  108.0 8.9 %copy-start.26 = (f32[4]{0:T(128)S(1)}, f32[4]{0:T(128)}, u32[]{:S(2)}) copy-start(f32[4]{0:T(128)} %param.10) | copy-start | bytes 52
  108.0 4.4 %collective-permute-start.8 = (bf16[4,128,128]{2,1,0:T(8,128)(2,1)S(1)}, bf16[4,128,128]{2,1,0:T(8,128)(2,1)S(1)}, u32[]{:S(2)}, u32[]{:S(2)}) collective-permute-start(bf16[4,128,128]{2,1,0:T(8,128)(2,1)S(1)} %fusion.96), channel_id=1, source_target_pairs={{0,16},{4,20},{8,24},{12,28},{1,17},{5,21},{9,25},{13,29},{2,18},{... | collective-permute-start | bytes 393224 | tf_op jit(solution)/shard_map/ppermute | solution.py:19
  110.5 4.4 %collective-permute-start.13 = (bf16[4,128,128]{2,1,0:T(8,128)(2,1)S(1)}, bf16[4,128,128]{2,1,0:T(8,128)(2,1)S(1)}, u32[]{:S(2)}, u32[]{:S(2)}) collective-permute-start(bf16[4,128,128]{2,1,0:T(8,128)(2,1)S(1)} %fusion.28), channel_id=1, source_target_pairs={{0,4},{4,8},{8,12},{12,16},{16,20},{20,24},{24,28},{1,5},{5,9},{9,... | collective-permute-start | bytes 393224 | tf_op jit(solution)/shard_map/ppermute | solution.py:19
  112.5 4.4 %collective-permute-start.9 = (bf16[4,128,128]{2,1,0:T(8,128)(2,1)S(1)}, bf16[4,128,128]{2,1,0:T(8,128)(2,1)S(1)}, u32[]{:S(2)}, u32[]{:S(2)}) collective-permute-start(bf16[4,128,128]{2,1,0:T(8,128)(2,1)S(1)} %fusion.27), channel_id=1, source_target_pairs={{0,4},{4,8},{8,12},{12,16},{16,20},{20,24},{24,28},{1,5},{5,9},{9,... | collective-permute-start | bytes 393224 | tf_op jit(solution)/shard_map/ppermute | solution.py:19
  116.9 9.2 %copy-start.5 = (bf16[4,128,128]{2,1,0:T(8,128)(2,1)}, bf16[4,128,128]{2,1,0:T(8,128)(2,1)S(1)}, u32[]{:S(2)}) copy-start(bf16[4,128,128]{2,1,0:T(8,128)(2,1)S(1)} %collective-permute-done.9) | copy-start | bytes 393220
  132.1 17.4 %copy-start.30 = (f32[4,128]{1,0:T(4,128)S(1)}, f32[4,128]{1,0:T(4,128)}, u32[]{:S(2)}) copy-start(f32[4,128]{1,0:T(4,128)} %copy-done.29) | copy-start | bytes 6148
  132.1 17.4 %copy-start.35 = (f32[4,128]{1,0:T(4,128)S(1)}, f32[4,128]{1,0:T(4,128)}, u32[]{:S(2)}) copy-start(f32[4,128]{1,0:T(4,128)} %get-tuple-element.17) | copy-start | bytes 6148
  132.1 17.4 %copy-start.4 = (f32[128,128]{1,0:T(8,128)S(1)}, f32[128,128]{1,0:T(8,128)}, u32[]{:S(2)}) copy-start(f32[128,128]{1,0:T(8,128)} %copy-done.2) | copy-start | bytes 196612
  132.1 20.7 %copy-start.28 = (f32[4,128]{1,0:T(4,128)S(1)}, f32[4,128]{1,0:T(4,128)}, u32[]{:S(2)}) copy-start(f32[4,128]{1,0:T(4,128)} %copy-done.27) | copy-start | bytes 6148
  132.1 20.7 %copy-start.32 = (f32[4,128]{1,0:T(4,128)S(1)}, f32[4,128]{1,0:T(4,128)}, u32[]{:S(2)}) copy-start(f32[4,128]{1,0:T(4,128)} %copy-done.31) | copy-start | bytes 6148
  132.1 20.7 %copy-start.34 = (f32[4,128]{1,0:T(4,128)S(1)}, f32[4,128]{1,0:T(4,128)}, u32[]{:S(2)}) copy-start(f32[4,128]{1,0:T(4,128)} %copy-done.33) | copy-start | bytes 6148
  132.1 126.5 %reduce-scatter.3.cloned.1.call-start = ((), (), s32[]{:S(2)}) async-start(), calls=%async_computation.2 | async-start | bytes 655360 | tf_op jit(solution)/shard_map/reduce_scatter | solution.py:225
  132.2 5.8 %collective-permute-start.18 = (s32[]{:T(128)}, s32[]{:T(128)}, u32[]{:S(2)}, u32[]{:S(2)}) collective-permute-start(s32[]{:T(128)} %convert_element_type.152), channel_id=1, source_target_pairs={{4,0},{8,4},{12,8},{16,12},{20,16},{24,20},{28,24},{5,1},{9,5},{13... | collective-permute-start | bytes 20 | tf_op jit(solution)/shard_map/ppermute | solution.py:19
  138.7 8.8 %collective-permute-start.19 = (s32[]{:T(128)}, s32[]{:T(128)}, u32[]{:S(2)}, u32[]{:S(2)}) collective-permute-start(s32[]{:T(128)} %max.29), channel_id=1, source_target_pairs={{8,0},{12,4},{16,8},{20,12},{24,16},{28,20},{9,1},{13,5},{17,9},{2... | collective-permute-start | bytes 20 | tf_op jit(solution)/shard_map/ppermute | solution.py:19
  159.4 9.9 %copy-start.22 = (bf16[4,128,128]{1,2,0:T(8,128)(2,1)S(1)}, bf16[4,128,128]{1,2,0:T(8,128)(2,1)}, u32[]{:S(2)}) copy-start(bf16[4,128,128]{1,2,0:T(8,128)(2,1)} %copy-done.21) | copy-start | bytes 393220
  161.1 13.6 %collective-permute-start.24 = (bf16[4,128,128]{2,1,0:T(8,128)(2,1)}, bf16[4,128,128]{2,1,0:T(8,128)(2,1)}, u32[]{:S(2)}, u32[]{:S(2)}) collective-permute-start(bf16[4,128,128]{2,1,0:T(8,128)(2,1)} %get-tuple-element.15), channel_id=1, source_target_pairs={{4,0},{8,4},{12,8},{16,12},{20,16},{24,20},{28,24},{5,1},{9,5},{13... | collective-permute-start | bytes 393224 | tf_op jit(solution)/shard_map/ppermute | solution.py:19
  163.7 8.7 %collective-permute-start.20 = (bf16[4,128,128]{2,1,0:T(8,128)(2,1)}, bf16[4,128,128]{2,1,0:T(8,128)(2,1)}, u32[]{:S(2)}, u32[]{:S(2)}) collective-permute-start(bf16[4,128,128]{2,1,0:T(8,128)(2,1)} %get-tuple-element.45), channel_id=1, source_target_pairs={{4,0},{8,4},{12,8},{16,12},{20,16},{24,20},{28,24},{5,1},{9,5},{13... | collective-permute-start | bytes 393224 | tf_op jit(solution)/shard_map/ppermute | solution.py:19
  171.7 39.2 %copy-start.23 = (f32[128,4,128]{0,2,1:T(8,128)S(1)}, f32[128,4,128]{0,2,1:T(8,128)}, u32[]{:S(2)}) copy-start(f32[128,4,128]{0,2,1:T(8,128)} %convolution_bitcast_fusion.1) | copy-start | bytes 786436
  171.7 39.2 %copy-start.37 = (f32[128]{0:T(128)S(1)}, f32[128]{0:T(128)}, u32[]{:S(2)}) copy-start(f32[128]{0:T(128)} %get-tuple-element.25) | copy-start | bytes 1540
  173.4 17.8 %collective-permute-start.21 = (bf16[4,128,128]{2,1,0:T(8,128)(2,1)S(1)}, bf16[4,128,128]{2,1,0:T(8,128)(2,1)S(1)}, u32[]{:S(2)}, u32[]{:S(2)}) collective-permute-start(bf16[4,128,128]{2,1,0:T(8,128)(2,1)S(1)} %fusion.66), channel_id=1, source_target_pairs={{8,0},{12,4},{16,8},{20,12},{24,16},{28,20},{9,1},{13,5},{17,9},{2... | collective-permute-start | bytes 393224 | tf_op jit(solution)/shard_map/ppermute | solution.py:19
  175.6 40.3 %copy-start.20 = (bf16[128,512]{1,0:T(8,128)(2,1)S(1)}, bf16[128,512]{1,0:T(8,128)(2,1)}, u32[]{:S(2)}) copy-start(bf16[128,512]{1,0:T(8,128)(2,1)} %param.9) | copy-start | bytes 393220
  175.6 17.8 %collective-permute-start.25 = (bf16[4,128,128]{2,1,0:T(8,128)(2,1)S(1)}, bf16[4,128,128]{2,1,0:T(8,128)(2,1)S(1)}, u32[]{:S(2)}, u32[]{:S(2)}) collective-permute-start(bf16[4,128,128]{2,1,0:T(8,128)(2,1)S(1)} %fusion.67), channel_id=1, source_target_pairs={{8,0},{12,4},{16,8},{20,12},{24,16},{28,20},{9,1},{13,5},{17,9},{2... | collective-permute-start | bytes 393224 | tf_op jit(solution)/shard_map/ppermute | solution.py:19
  192.2 9.4 %collective-permute-start.22 = (bf16[4,128,128]{2,1,0:T(8,128)(2,1)S(1)}, bf16[4,128,128]{2,1,0:T(8,128)(2,1)S(1)}, u32[]{:S(2)}, u32[]{:S(2)}) collective-permute-start(bf16[4,128,128]{2,1,0:T(8,128)(2,1)S(1)} %fusion.98), channel_id=1, source_target_pairs={{16,0},{20,4},{24,8},{28,12},{17,1},{21,5},{25,9},{29,13},{18,2},{... | collective-permute-start | bytes 393224 | tf_op jit(solution)/shard_map/ppermute | solution.py:19
  194.5 9.8 %collective-permute-start.26 = (bf16[4,128,128]{2,1,0:T(8,128)(2,1)S(1)}, bf16[4,128,128]{2,1,0:T(8,128)(2,1)S(1)}, u32[]{:S(2)}, u32[]{:S(2)}) collective-permute-start(bf16[4,128,128]{2,1,0:T(8,128)(2,1)S(1)} %fusion.99), channel_id=1, source_target_pairs={{16,0},{20,4},{24,8},{28,12},{17,1},{21,5},{25,9},{29,13},{18,2},{... | collective-permute-start | bytes 393224 | tf_op jit(solution)/shard_map/ppermute | solution.py:19
  202.5 16.0 %copy-start.24 = (f32[4,128,128]{2,1,0:T(8,128)S(1)}, f32[4,128,128]{2,1,0:T(8,128)}, u32[]{:S(2)}) copy-start(f32[4,128,128]{2,1,0:T(8,128)} %convolution_multiply_fusion.1) | copy-start | bytes 786436
  202.5 8.3 %collective-permute-start.23 = (bf16[4,128,128]{2,1,0:T(8,128)(2,1)S(1)}, bf16[4,128,128]{2,1,0:T(8,128)(2,1)S(1)}, u32[]{:S(2)}, u32[]{:S(2)}) collective-permute-start(bf16[4,128,128]{2,1,0:T(8,128)(2,1)S(1)} %fusion.29), channel_id=1, source_target_pairs={{4,0},{8,4},{12,8},{16,12},{20,16},{24,20},{28,24},{5,1},{9,5},{13... | collective-permute-start | bytes 393224 | tf_op jit(solution)/shard_map/ppermute | solution.py:19
  205.9 8.9 %collective-permute-start.27 = (bf16[4,128,128]{2,1,0:T(8,128)(2,1)}, bf16[4,128,128]{2,1,0:T(8,128)(2,1)}, u32[]{:S(2)}, u32[]{:S(2)}) collective-permute-start(bf16[4,128,128]{2,1,0:T(8,128)(2,1)} %fusion.30), channel_id=1, source_target_pairs={{4,0},{8,4},{12,8},{16,12},{20,16},{24,20},{28,24},{5,1},{9,5},{13... | collective-permute-start | bytes 393224 | tf_op jit(solution)/shard_map/ppermute | solution.py:19
  (21 other events, 61.6 us)
Sparse Core Ops, SparseCore 0:
  132.2 101.8 reduce-scatter.4
  237.3 21.2 reduce-scatter.2
where the time goes:
time: 267 us; the launch traced here: 265 us
  starting transfers between devices  89.1 us (33%)
  waiting for transfers between devices  76.3 us (29%)
  matrix products  33.1 us (12%)
  between operations  32.5 us (12%)
  other arithmetic  15.6 us (6%)
  local copies, waits for them, and re-layouts  11.4 us (4%)
  blocking collectives  7.52 us (3%)
    ppermute x28, starting transfers between devices, shifted(): return lax.ppermute(value, axis, pairs)  89 us
    ppermute x28, waiting for transfers between devices, shifted(): return lax.ppermute(value, axis, pairs)  39.3 us
    dot_general x40, matrix products, matmul_high(): jnp.dot(left_side, right_side, precision=lax.Precision.HIGHEST, preferred...  27.9 us
    reduce_scatter x1, waiting for transfers between devices, per_device(): lax.psum_scatter(partial_out.astype(jnp.bfloat16), 'head', scatter_dimens...  22.5 us
    reduce_scatter x1, waiting for transfers between devices, per_device(): lax.psum_scatter(lax.dot_general(cot_full, mixed, (((0,), (0,)), ((), ())...  14.5 us
    convert_element_type x13, other arithmetic, shortened(): a.astype(jnp.bfloat16)  8.62 us
    all_gather x1, blocking collectives, per_device(): cot_full = lax.all_gather(out_grad, 'head', axis=1, tiled=True)  7.52 us
    unnamed x83, local copies, waits for them, and re-layouts  7.17 us
  transfers between devices with their start and end apart: 30, of which 13 were waited for; matrix products, arithmetic and copies ran while one was open for 15% of the time, Pallas kernels for 0%

commit v1 on v0

v1 whole, which is shorter than its diff:
```python
import functools

import jax
import jax.numpy as jnp
from jax import lax
from jax.experimental import pallas as pl
from jax.experimental.pallas import tpu as pltpu
from jax.sharding import PartitionSpec as P

CG_STEPS = 4
EPSILON = 1e-06
LABEL_ROWS = 16
F32 = jnp.float32
BF16 = jnp.bfloat16
VMEM_LIMIT = 48 * 1024 * 1024


def mm(a, b):
    return lax.dot_general(a, b, (((1,), (0,)), ((), ())), preferred_element_type=F32)


def mm_nt(a, b):
    return lax.dot_general(a, b, (((1,), (1,)), ((), ())), preferred_element_type=F32)


def mm_tn(a, b):
    return lax.dot_general(a, b, (((0,), (0,)), ((), ())), preferred_element_type=F32)


def kernel_call(body, out_shape, operands, flops, name, smem=()):
    in_specs = [
        pl.BlockSpec(memory_space=pltpu.SMEM if i in smem else pltpu.VMEM)
        for i in range(len(operands))
    ]
    nbytes = sum(o.size * o.dtype.itemsize for o in operands)
    nbytes += sum(o.size * o.dtype.itemsize for o in out_shape)
    return pl.pallas_call(
        body,
        out_shape=out_shape,
        in_specs=in_specs,
        out_specs=[pl.BlockSpec(memory_space=pltpu.VMEM)] * len(out_shape),
        compiler_params=pltpu.CompilerParams(vmem_limit_bytes=VMEM_LIMIT),
        cost_estimate=pl.CostEstimate(flops=flops, bytes_accessed=nbytes, transcendentals=0),
        name=name,
    )(*operands)


def label_grids(doc_ref, piece):
    across = jnp.broadcast_to(doc_ref[...], (piece, piece))
    return across, across.T


def document_mask(across, down):
    row = lax.broadcasted_iota(jnp.int32, across.shape, 0)
    col = lax.broadcasted_iota(jnp.int32, across.shape, 1)
    return (across == down) & (col <= row)


def tail_body(heads, width, doc_ref, key_ref, value_ref, out_ref):
    piece = key_ref.shape[0]
    across, down = label_grids(doc_ref, piece)
    last = jnp.max(across, axis=1, keepdims=True)
    tail = (down == last).astype(F32).astype(BF16)
    states = heads * width
    for h in range(heads):
        cols = slice(h * width, (h + 1) * width)
        key_h = key_ref[:, cols]
        masked = key_h * tail[:, :width]
        out_ref[h * width : (h + 1) * width, :] = mm_tn(key_h, masked).astype(BF16)
        out_ref[states + h * width : states + (h + 1) * width, :] = mm_tn(
            value_ref[:, cols], masked
        ).astype(BF16)
    label = (last[:LABEL_ROWS] + 1).astype(F32)
    out_ref[2 * states :, :] = jnp.broadcast_to(label, (LABEL_ROWS, width)).astype(BF16)


def cot_body(count, shard, place_ref, *refs):
    cots, weight_ref, cot_ref, full_ref = refs[:count], refs[count], refs[count + 1], refs[count + 2]
    me = place_ref[1]
    total = None
    for b in range(count):
        owner = jnp.bitwise_xor(me, b)
        cols = pl.ds(pl.multiple_of(owner * shard, shard), shard)
        block = cots[b][...]
        full_ref[:, cols] = block
        part = mm_nt(block, weight_ref[:, cols])
        total = part if total is None else total + part
    cot_ref[...] = total.astype(BF16)


def project_body(count, shard, place_ref, mixed_ref, weight_ref, own_ref, *send_refs):
    me = place_ref[1]
    mixed = mixed_ref[...]
    for b in range(count):
        owner = jnp.bitwise_xor(me, b)
        cols = pl.ds(pl.multiple_of(owner * shard, shard), shard)
        part = mm(mixed, weight_ref[:, cols])
        if b == 0:
            own_ref[...] = part
        else:
            send_refs[b - 1][...] = part.astype(BF16)


def solve_body(
    heads,
    width,
    ridge_ref,
    doc_ref,
    query_ref,
    key_ref,
    value_ref,
    cot_ref,
    near_ref,
    far_ref,
    sol_ref,
    dual_ref,
    mixed_ref,
    out_ref,
):
    piece = key_ref.shape[0]
    states = heads * width
    across, down = label_grids(doc_ref, piece)
    same = document_mask(across, down).astype(F32)
    same_two = jnp.concatenate([same, same], axis=0)
    first = jnp.min(across, axis=1, keepdims=True)
    head_rows = (down == first)[:, :width].astype(F32)
    near_label = near_ref[2 * states : 2 * states + LABEL_ROWS, :].astype(F32)[0:1, :]
    far_label = far_ref[2 * states : 2 * states + LABEL_ROWS, :].astype(F32)[0:1, :]
    joined = jnp.broadcast_to((near_label == far_label).astype(F32), (width, width))
    carried = ((down + 1).astype(F32)[:, :width] == near_label).astype(F32)
    carried_two = jnp.concatenate([carried, carried], axis=0)

    def state(index):
        rows = slice(index * width, (index + 1) * width)
        return (near_ref[rows, :].astype(F32) + joined * far_ref[rows, :].astype(F32)).astype(BF16)

    keys, rhs_keys, values, grams, solutions, residuals, directions, squares = ([] for _ in range(8))
    value_states = []
    for h in range(heads):
        cols = slice(h * width, (h + 1) * width)
        key_h = key_ref[:, cols]
        value_h = value_ref[:, cols]
        value_state = state(heads + h)
        cot_h = cot_ref[:, cols]
        both = mm(cot_h, jnp.concatenate([value_h.T, value_state], axis=1))
        scores = (both[:, :piece] * same).astype(BF16)
        target = carried * both[:, piece:] + mm(scores, key_h)
        start = jnp.concatenate([query_ref[:, cols].astype(F32), target], axis=0)
        keys.append(key_h)
        values.append(value_h)
        value_states.append(value_state)
        rhs_keys.append(jnp.concatenate([key_h.T, state(h)], axis=1))
        solutions.append(jnp.zeros_like(start))
        residuals.append(start)
        directions.append(start)
        squares.append(jnp.sum(start * start, axis=1, keepdims=True))
    for step in range(CG_STEPS):
        for h in range(heads):
            p = directions[h]
            both = mm(p.astype(BF16), rhs_keys[h])
            scores = (both[:, :piece] * same_two).astype(BF16)
            applied = carried_two * both[:, piece:] + mm(scores, keys[h]) + ridge_ref[h] * p
            size = squares[h] / (jnp.sum(p * applied, axis=1, keepdims=True) + EPSILON)
            solutions[h] = solutions[h] + size * p
            if step + 1 < CG_STEPS:
                residuals[h] = residuals[h] - size * applied
                new_sq = jnp.sum(residuals[h] * residuals[h], axis=1, keepdims=True)
                directions[h] = residuals[h] + new_sq / (squares[h] + EPSILON) * p
                squares[h] = new_sq
    for h in range(heads):
        cols = slice(h * width, (h + 1) * width)
        sol = solutions[h][:piece]
        sol_b = sol.astype(BF16)
        dual_b = solutions[h][piece:].astype(BF16)
        both = mm(sol_b, jnp.concatenate([rhs_keys[h][:, :piece], value_states[h].T], axis=1))
        scores = (both[:, :piece] * same).astype(BF16)
        output = carried * both[:, piece:] + mm(scores, values[h])
        mixed_ref[:, cols] = output.astype(BF16)
        sol_ref[:, cols] = sol_b
        dual_ref[:, cols] = dual_b
        masked = (head_rows * sol).astype(BF16)
        out_ref[h * width : (h + 1) * width, :] = mm_tn(cot_ref[:, cols], masked).astype(BF16)
        cross = mm_tn(dual_b, masked)
        out_ref[states + h * width : states + (h + 1) * width, :] = (cross + cross.T).astype(BF16)
    label = (first[:LABEL_ROWS] + 1).astype(F32)
    out_ref[2 * states :, :] = jnp.broadcast_to(label, (LABEL_ROWS, width)).astype(BF16)


def local_grads_body(
    heads, width, doc_ref, key_ref, value_ref, cot_ref, sol_ref, dual_ref, grad_k_ref, grad_v_ref
):
    piece = key_ref.shape[0]
    across, down = label_grids(doc_ref, piece)
    same = document_mask(across, down).astype(F32)
    same_two = jnp.concatenate([same, same], axis=0)
    for h in range(heads):
        cols = slice(h * width, (h + 1) * width)
        key_h, value_h, cot_h = key_ref[:, cols], value_ref[:, cols], cot_ref[:, cols]
        sol, dual = sol_ref[:, cols], dual_ref[:, cols]
        score_two = (mm_nt(cot_h, value_h) * same).astype(BF16)
        pair = (mm_nt(jnp.concatenate([sol, dual], axis=0), key_h) * same_two).astype(BF16)
        score_one, score_three = pair[:piece], pair[piece:]
        grad_v_ref[:, cols] = mm_tn(score_one, cot_h)
        grad_k_ref[:, cols] = mm_tn(
            jnp.concatenate([score_two, -score_three, -score_one], axis=0),
            jnp.concatenate([sol, sol, dual], axis=0),
        )


def final_grads_body(
    heads,
    width,
    doc_ref,
    key_ref,
    value_ref,
    near_ref,
    far_ref,
    local_k_ref,
    local_v_ref,
    grad_k_ref,
    grad_v_ref,
):
    piece = key_ref.shape[0]
    states = heads * width
    _, down = label_grids(doc_ref, piece)
    near_label = near_ref[2 * states : 2 * states + LABEL_ROWS, :].astype(F32)[0:1, :]
    far_label = far_ref[2 * states : 2 * states + LABEL_ROWS, :].astype(F32)[0:1, :]
    joined = jnp.broadcast_to((near_label == far_label).astype(F32), (width, width))
    later = ((down + 1).astype(F32)[:, :width] == near_label).astype(F32)

    def state(index):
        rows = slice(index * width, (index + 1) * width)
        return (near_ref[rows, :].astype(F32) + joined * far_ref[rows, :].astype(F32)).astype(BF16)

    for h in range(heads):
        cols = slice(h * width, (h + 1) * width)
        key_h, value_h = key_ref[:, cols], value_ref[:, cols]
        grad_state, gram_grad = state(h), state(heads + h)
        grad_v = local_v_ref[:, cols] + later * mm_nt(key_h, grad_state)
        grad_k = local_k_ref[:, cols] + later * (mm(value_h, grad_state) - mm(key_h, gram_grad))
        grad_v_ref[:, cols] = grad_v.astype(BF16)
        grad_k_ref[:, cols] = grad_k.astype(BF16)


def rotated(value, by):
    devices = lax.axis_size("seq")
    return lax.ppermute(value, "seq", [(i, (i + by) % devices) for i in range(devices)])


def swapped(value, axis, mask):
    devices = lax.axis_size(axis)
    return lax.ppermute(value, axis, [(i, i ^ mask) for i in range(devices)])


def joined_states(near, far, states):
    rows = lax.broadcasted_iota(jnp.int32, near.shape, 0)
    matches = (near[states:, :] == far[states:, :])[0:1, :]
    total = near.astype(F32) + far.astype(F32)
    return jnp.where((rows < states) & matches, total, near.astype(F32)).astype(BF16)


def scan_states(element, states, sign):
    window = lax.axis_size("seq") // 2
    near, far, reach = rotated(element, sign), rotated(element, 2 * sign), 2
    while reach < window:
        near = joined_states(near, far, states)
        far = rotated(near, sign * reach)
        reach *= 2
    return near, far


def per_device(query_rows, key_rows, value_rows, ridge_reg, out_weight, out_grad, doc_ids):
    heads = ridge_reg.shape[0]
    piece, features = key_rows.shape
    width = features // heads
    states = 2 * heads * width
    seq_size, head_size = lax.axis_size("seq"), lax.axis_size("head")
    seq_at, head_at = lax.axis_index("seq"), lax.axis_index("head")
    place = jnp.stack([seq_at, head_at]).astype(jnp.int32)
    model = out_weight.shape[1]
    shard = model // head_size
    doc_row = doc_ids.reshape(1, piece)
    payload = jax.ShapeDtypeStruct((states + LABEL_ROWS, width), BF16)
    rows_bf16 = jax.ShapeDtypeStruct((piece, features), BF16)
    rows_f32 = jax.ShapeDtypeStruct((piece, features), F32)

    (element,) = kernel_call(
        functools.partial(tail_body, heads, width),
        [payload],
        (doc_row, key_rows, value_rows),
        4 * piece * features * width,
        "tail_states",
    )
    near, far = scan_states(element, states, 1)

    cots = [out_grad] + [swapped(out_grad, "head", b) for b in range(1, head_size)]
    out_cot, cot_full = kernel_call(
        functools.partial(cot_body, head_size, shard),
        [rows_bf16, jax.ShapeDtypeStruct((piece, model), BF16)],
        (place, *cots, out_weight),
        2 * piece * features * model,
        "cotangent",
        smem=(0,),
    )

    sol, dual, mixed, back = kernel_call(
        functools.partial(solve_body, heads, width),
        [rows_bf16, rows_bf16, rows_bf16, payload],
        (ridge_reg, doc_row, query_rows, key_rows, value_rows, out_cot, near, far),
        60 * piece * features * width,
        "solve",
        smem=(0,),
    )
    later_near, later_far = scan_states(back, states, -1)

    own, *sends = kernel_call(
        functools.partial(project_body, head_size, shard),
        [jax.ShapeDtypeStruct((piece, shard), F32)]
        + [jax.ShapeDtypeStruct((piece, shard), BF16)] * (head_size - 1),
        (place, mixed, out_weight),
        2 * piece * features * model,
        "project",
        smem=(0,),
    )
    total = own
    for b in range(1, head_size):
        total = total + swapped(sends[b - 1], "head", b).astype(F32)
    layer_out = total.astype(BF16)

    pair_rows = 2 * (model // seq_size)
    pairs = seq_size // 2
    pair_at = seq_at // 2
    cot_blocks, mixed_blocks = [], []
    for c in range(pairs):
        start = jnp.bitwise_xor(pair_at, c) * pair_rows
        block = lax.dynamic_slice_in_dim(cot_full, start, pair_rows, 1)
        cot_blocks.append(block if c == 0 else swapped(block, "seq", 2 * c))
        if c == 0:
            mixed_blocks.append(mixed)
        else:
            low = c & -c
            rest = mixed_blocks[c ^ low]
            mixed_blocks.append(swapped(rest, "seq", 2 * low))
    pair_grad = lax.dot_general(
        jnp.concatenate(cot_blocks, axis=0),
        jnp.concatenate(mixed_blocks, axis=0),
        (((0,), (0,)), ((), ())),
        preferred_element_type=F32,
    )
    halves = pair_grad.reshape(2, pair_rows // 2, features)
    kept = lax.dynamic_index_in_dim(halves, seq_at % 2, 0, False)
    given = lax.dynamic_index_in_dim(halves, 1 - seq_at % 2, 0, False).astype(BF16)
    grad_weight = kept + swapped(given, "seq", 1).astype(F32)

    local_k, local_v = kernel_call(
        functools.partial(local_grads_body, heads, width),
        [rows_f32, rows_f32],
        (doc_row, key_rows, value_rows, out_cot, sol, dual),
        14 * piece * features * width,
        "local_grads",
    )
    grad_keys, grad_values = kernel_call(
        functools.partial(final_grads_body, heads, width),
        [rows_bf16, rows_bf16],
        (doc_row, key_rows, value_rows, later_near, later_far, local_k, local_v),
        6 * piece * features * width,
        "final_grads",
    )
    return (layer_out, dual, grad_keys, grad_values, grad_weight)


def solution(mesh):
    rows = P("seq", "head")
    in_specs = (rows, rows, rows, P("head"), P("head", None), rows, P("seq"))
    return jax.shard_map(
        per_device, mesh=mesh, in_specs=in_specs, out_specs=(rows,) * 5, check_vma=False
    )
```

time: 267 us -> 89.3 us (0.33)
  starting transfers between devices: 89.1 us -> 29.1 us
  waiting for transfers between devices: 76.3 us -> 38 us
  between operations: 32.5 us -> 0.83 us
  matrix products: 33.1 us -> 1.68 us
  other arithmetic: 15.6 us -> 2.2 us
  Pallas kernels: 0 us -> 9.93 us
  blocking collectives: 7.52 us -> 0 us
  local copies, waits for them, and re-layouts: 11.4 us -> 7.42 us
    ppermute x28 -> x19, starting transfers between devices: 89 us -> 29.1 us  [the longest x6 17.3 us: rotated(): lax.ppermute(value, 'seq', [(i, (i + by) % devices) for i in range(device...]
    reduce_scatter x2 -> x0, waiting for transfers between devices: 37 us -> none  [the longest x1 22.5 us: per_device(): lax.psum_scatter(partial_out.astype(jnp.bfloat16), 'head', scatter_dimens...]
    dot_general x44 -> x1, matrix products: 32.4 us -> 1.68 us  [per_device(): lax.dot_general(jnp.concatenate(cot_blocks, axis=0), jnp.concatenate(mixe...]
    convert_element_type x16 -> x3, other arithmetic: 12.2 us -> 1.24 us  [the longest x1 0.73 us: per_device(): layer_out = total.astype(BF16)]
    pallas_call x0 -> x6, Pallas kernels: none -> 9.93 us  [kernel_call(): pl.pallas_call(body, out_shape=out_shape, in_specs=in_specs, out_specs=[p...]
    all_gather x1 -> x0, blocking collectives: 7.52 us -> none  [per_device(): cot_full = lax.all_gather(out_grad, 'head', axis=1, tiled=True)]
    ppermute x28 -> x19, waiting for transfers between devices: 39.3 us -> 38 us  [the longest x6 22.8 us: rotated(): lax.ppermute(value, 'seq', [(i, (i + by) % devices) for i in range(device...]
    unnamed x83 -> x32, local copies, waits for them, and re-layouts: 7.17 us -> 6.64 us
  transfers between devices with their start and end apart: 30 -> 19, of which waited for: 13 -> 9; matrix products, arithmetic and copies ran while one was open for 15% -> 5% of each run, Pallas kernels for 0% -> 4%
where the time goes in v1:
time: 89.3 us; the launch traced here: 89.1 us
  waiting for transfers between devices  38 us (43%)
  starting transfers between devices  29.1 us (33%)
  Pallas kernels  9.93 us (11%)
  local copies, waits for them, and re-layouts  7.42 us (8%)
  other arithmetic  2.2 us (2%)
  matrix products  1.68 us (2%)
    ppermute x6, waiting for transfers between devices, rotated(): lax.ppermute(value, 'seq', [(i, (i + by) % devices) for i in range(device...  22.8 us
    ppermute x6, starting transfers between devices, rotated(): lax.ppermute(value, 'seq', [(i, (i + by) % devices) for i in range(device...  17.3 us
    ppermute x13, waiting for transfers between devices, swapped(): return lax.ppermute(value, axis, [(i, i ^ mask) for i in range(devices)])  15.2 us
    ppermute x13, starting transfers between devices, swapped(): return lax.ppermute(value, axis, [(i, i ^ mask) for i in range(devices)])  11.7 us
    pallas_call x6, Pallas kernels, kernel_call(): pl.pallas_call(body, out_shape=out_shape, in_specs=in_specs, out_specs=[p...  9.93 us
    unnamed x32, local copies, waits for them, and re-layouts  6.64 us
  transfers between devices with their start and end apart: 19, of which 9 were waited for; matrix products, arithmetic and copies ran while one was open for 5% of the time, Pallas kernels for 4%

profile of v1, /device:TPU:0, one launch (start us, length us, event | category | flops | bytes accessed | tf_op | source)
XLA Modules:
  0.0 89.1 jit_solution(5903607234369016019)
XLA Ops:
  0.7 0.9 %copy-done.2 = bf16[128,512]{1,0:T(8,128)(2,1)S(1)} copy-done((bf16[128,512]{1,0:T(8,128)(2,1)S(1)}, bf16[128,512]{1,0:T(8,128)(2,1)}, u32[]{:S(2)}) %copy-start.2) | copy-done | bytes 131096
  1.6 0.9 %copy-done.4 = bf16[128,512]{1,0:T(8,128)(2,1)S(1)} copy-done((bf16[128,512]{1,0:T(8,128)(2,1)S(1)}, bf16[128,512]{1,0:T(8,128)(2,1)}, u32[]{:S(2)}) %copy-start.4) | copy-done | bytes 131096
  2.5 0.7 copy-done.8
  3.1 0.4 tail_states.1
  3.5 3.1 %collective-permute-start.4 = (bf16[1040,128]{1,0:T(8,128)(2,1)S(1)}, bf16[1040,128]{1,0:T(8,128)(2,1)S(1)}, u32[]{:S(2)}, u32[]{:S(2)}) collective-permute-start(bf16[1040,128]{1,0:T(8,128)(2,1)S(1)} %tail_states.1), channel_id=1, source_target_pairs={{0,8},{4,12},{8,16},{12,20},{16,24},{20,28},{24,0},{28,4},{1,9},{5... | collective-permute-start | bytes 798728 | tf_op jit(solution)/shard_map/ppermute | solution.py:247
  6.6 1.5 %collective-permute-start.3 = (bf16[1040,128]{1,0:T(8,128)(2,1)S(1)}, bf16[1040,128]{1,0:T(8,128)(2,1)S(1)}, u32[]{:S(2)}, u32[]{:S(2)}) collective-permute-start(bf16[1040,128]{1,0:T(8,128)(2,1)S(1)} %tail_states.1), channel_id=1, source_target_pairs={{0,4},{4,8},{8,12},{12,16},{16,20},{20,24},{24,28},{28,0},{1,5},{5... | collective-permute-start | bytes 798728 | tf_op jit(solution)/shard_map/ppermute | solution.py:247
  8.1 6.9 %collective-permute-done.4 = bf16[1040,128]{1,0:T(8,128)(2,1)S(1)} collective-permute-done((bf16[1040,128]{1,0:T(8,128)(2,1)S(1)}, bf16[1040,128]{1,0:T(8,128)(2,1)S(1)}, u32[]{:S(2)}, u32[]{:S(2)}) %collective-permute-start.4) | collective-permute-done | bytes 266272 | tf_op jit(solution)/shard_map/ppermute | solution.py:247
  15.0 6.7 %collective-permute-done.3 = bf16[1040,128]{1,0:T(8,128)(2,1)S(1)} collective-permute-done((bf16[1040,128]{1,0:T(8,128)(2,1)S(1)}, bf16[1040,128]{1,0:T(8,128)(2,1)S(1)}, u32[]{:S(2)}, u32[]{:S(2)}) %collective-permute-start.3) | collective-permute-done | bytes 266272 | tf_op jit(solution)/shard_map/ppermute | solution.py:247
  21.7 0.3 fusion.near_ref
  22.0 0.1 collective-permute-start.5
  22.0 0.1 collective-permute-start
  22.1 1.6 %collective-permute-start.1 = (bf16[128,512]{1,0:T(8,128)(2,1)}, bf16[128,512]{1,0:T(8,128)(2,1)S(1)}, u32[]{:S(2)}, u32[]{:S(2)}) collective-permute-start(bf16[128,512]{1,0:T(8,128)(2,1)} %refs_0_.1), channel_id=1, source_target_pairs={{0,2},{1,3},{2,0},{3,1},{4,6},{5,7},{6,4},{7,5},{8,10},{9,11},{10,... | collective-permute-start | bytes 393224 | tf_op jit(solution)/shard_map/ppermute | solution.py:252
  23.7 0.3 collective-permute-start.2
  24.0 0.1 pad_add_fusion.place_ref
  24.0 4.6 %collective-permute-done.1.refs_2_ = bf16[128,512]{1,0:T(8,128)(2,1)S(1)} collective-permute-done((bf16[128,512]{1,0:T(8,128)(2,1)}, bf16[128,512]{1,0:T(8,128)(2,1)S(1)}, u32[]{:S(2)}, u32[]{:S(2)}) %collective-permute-start.1) | collective-permute-done | bytes 131104 | tf_op jit(solution)/shard_map/ppermute | solution.py:252
  28.7 1.9 %collective-permute-done.2.refs_3_ = bf16[128,512]{1,0:T(8,128)(2,1)S(1)} collective-permute-done((bf16[128,512]{1,0:T(8,128)(2,1)}, bf16[128,512]{1,0:T(8,128)(2,1)S(1)}, u32[]{:S(2)}, u32[]{:S(2)}) %collective-permute-start.2) | collective-permute-done | bytes 131104 | tf_op jit(solution)/shard_map/ppermute | solution.py:252
  30.6 1.6 %copy-done = bf16[512,2048]{1,0:T(8,128)(2,1)S(1)} copy-done((bf16[512,2048]{1,0:T(8,128)(2,1)S(1)}, bf16[512,2048]{1,0:T(8,128)(2,1)}, u32[]{:S(2)}) %copy-start) | copy-done | bytes 2097176
  32.2 0.9 %copy-done.6 = bf16[128,512]{1,0:T(8,128)(2,1)S(1)} copy-done((bf16[128,512]{1,0:T(8,128)(2,1)S(1)}, bf16[128,512]{1,0:T(8,128)(2,1)}, u32[]{:S(2)}) %copy-start.6) | copy-done | bytes 131096
  33.1 1.4 %cotangent.1 = (bf16[128,512]{1,0:T(8,128)(2,1)S(1)}, bf16[128,2048]{1,0:T(8,128)(2,1)S(1)}) custom-call(s32[2]{0:T(128)S(1)} %pad_add_fusion.place_ref, bf16[128,512]{1,0:T(8,128)(2,1)S(1)} %copy-done.6, bf16[128,512]{1,0:T(8,128)(2,1)S(1)} %collective-permute-done.refs_1_, bf16[128,512]{1,0:T(8,128)(2,1)S(1)} %collective-permute-done.1.refs_2_, ...), custom_call_target="tpu_custom_call" | custom-call | flops 268435456 | bytes 3276808 | tf_op jit(solution)/shard_map/cotangent/pallas_call | solution.py:37
  34.5 0.0 copy-start.1
  34.5 0.0 copy-start.10
  34.5 0.7 copy-done.10
  35.2 0.9 %copy-done.11 = bf16[1040,128]{1,0:T(8,128)(2,1)S(1)} copy-done((bf16[1040,128]{1,0:T(8,128)(2,1)S(1)}, bf16[1040,128]{1,0:T(8,128)(2,1)}, u32[]{:S(2)}) %copy-start.11) | copy-done | bytes 266264
  36.2 5.1 %solve.1 = (bf16[128,512]{1,0:T(8,128)(2,1)S(1)}, bf16[128,512]{1,0:T(8,128)(2,1)}, bf16[128,512]{1,0:T(8,128)(2,1)S(1)}, bf16[1040,128]{1,0:T(8,128)(2,1)S(1)}) custom-call(f32[4]{0:T(128)S(1)} %copy-done.13, s32[1,128]{1,0:T(1,128)S(1)} %bitcast.13, bf16[128,512]{1,0:T(8,128)(2,1)S(1)} %copy-done.12, bf16[128,512]{1,0:T(8,128)(2,1)S(1)} %copy-done.3, ...), custom_call_target="tpu_custom_call" | custom-call | flops 503316480 | bytes 1716752 | tf_op jit(solution)/shard_map/solve/pallas_call | solution.py:37
  41.2 2.4 %collective-permute-start.16 = (bf16[128,512]{1,0:T(8,128)(2,1)S(1)}, bf16[128,512]{1,0:T(8,128)(2,1)}, u32[]{:S(2)}, u32[]{:S(2)}) collective-permute-start(bf16[128,512]{1,0:T(8,128)(2,1)S(1)} %get-tuple-element.20.mixed_ref), channel_id=1, source_target_pairs={{0,16},{4,20},{8,24},{12,28},{16,0},{20,4},{24,8},{28,12},{1,17},{... | collective-permute-start | bytes 393224 | tf_op jit(solution)/shard_map/ppermute | solution.py:252
  43.7 0.7 constant_dynamic-slice_fusion.3
  44.4 1.4 %collective-permute-start.14 = (bf16[128,512]{1,0:T(8,128)(2,1)}, bf16[128,512]{1,0:T(8,128)(2,1)}, u32[]{:S(2)}, u32[]{:S(2)}) collective-permute-start(bf16[128,512]{1,0:T(8,128)(2,1)} %get-tuple-element.34), channel_id=1, source_target_pairs={{0,24},{4,28},{8,16},{12,20},{16,8},{20,12},{24,0},{28,4},{1,25},{... | collective-permute-start | bytes 393224 | tf_op jit(solution)/shard_map/ppermute | solution.py:252
  45.8 2.0 %collective-permute-start.13 = (bf16[128,512]{1,0:T(8,128)(2,1)}, bf16[128,512]{1,0:T(8,128)(2,1)}, u32[]{:S(2)}, u32[]{:S(2)}) collective-permute-start(bf16[128,512]{1,0:T(8,128)(2,1)} %get-tuple-element.35), channel_id=1, source_target_pairs={{0,16},{4,20},{8,24},{12,28},{16,0},{20,4},{24,8},{28,12},{1,17},{... | collective-permute-start | bytes 393224 | tf_op jit(solution)/shard_map/ppermute | solution.py:252
  47.8 1.0 %collective-permute-start.12 = (bf16[128,512]{1,0:T(8,128)(2,1)S(1)}, bf16[128,512]{1,0:T(8,128)(2,1)}, u32[]{:S(2)}, u32[]{:S(2)}) collective-permute-start(bf16[128,512]{1,0:T(8,128)(2,1)S(1)} %get-tuple-element.36), channel_id=1, source_target_pairs={{0,8},{4,12},{8,0},{12,4},{16,24},{20,28},{24,16},{28,20},{1,9},{5... | collective-permute-start | bytes 393224 | tf_op jit(solution)/shard_map/ppermute | solution.py:252
  48.8 1.0 %collective-permute-start.15 = (bf16[128,512]{1,0:T(8,128)(2,1)S(1)}, bf16[128,512]{1,0:T(8,128)(2,1)}, u32[]{:S(2)}, u32[]{:S(2)}) collective-permute-start(bf16[128,512]{1,0:T(8,128)(2,1)S(1)} %get-tuple-element.20.mixed_ref), channel_id=1, source_target_pairs={{0,8},{4,12},{8,0},{12,4},{16,24},{20,28},{24,16},{28,20},{1,9},{5... | collective-permute-start | bytes 393224 | tf_op jit(solution)/shard_map/ppermute | solution.py:252
  49.8 7.1 %collective-permute-done.16 = bf16[128,512]{1,0:T(8,128)(2,1)} collective-permute-done((bf16[128,512]{1,0:T(8,128)(2,1)S(1)}, bf16[128,512]{1,0:T(8,128)(2,1)}, u32[]{:S(2)}, u32[]{:S(2)}) %collective-permute-start.16) | collective-permute-done | bytes 131104 | tf_op jit(solution)/shard_map/ppermute | solution.py:252
  57.0 1.0 %project.1 = (f32[128,512]{1,0:T(8,128)S(1)}, bf16[128,512]{1,0:T(8,128)(2,1)S(1)}, bf16[128,512]{1,0:T(8,128)(2,1)S(1)}, bf16[128,512]{1,0:T(8,128)(2,1)S(1)}) custom-call(s32[2]{0:T(128)S(1)} %pad_add_fusion.place_ref, bf16[128,512]{1,0:T(8,128)(2,1)S(1)} %get-tuple-element.20.mixed_ref, bf16[512,2048]{1,0:T(8,128)(2,1)S(1)} %copy-done.1), custom_call_target="tpu_custom_call" | custom-call | flops 268435456 | bytes 2883592 | tf_op jit(solution)/shard_map/project/pallas_call | solution.py:37
  58.0 2.9 %collective-permute-start.10 = (bf16[1040,128]{1,0:T(8,128)(2,1)S(1)}, bf16[1040,128]{1,0:T(8,128)(2,1)S(1)}, u32[]{:S(2)}, u32[]{:S(2)}) collective-permute-start(bf16[1040,128]{1,0:T(8,128)(2,1)S(1)} %get-tuple-element.26), channel_id=1, source_target_pairs={{0,24},{4,28},{8,0},{12,4},{16,8},{20,12},{24,16},{28,20},{1,25},{... | collective-permute-start | bytes 798728 | tf_op jit(solution)/shard_map/ppermute | solution.py:247
  60.9 1.5 %collective-permute-done.13 = bf16[128,512]{1,0:T(8,128)(2,1)} collective-permute-done((bf16[128,512]{1,0:T(8,128)(2,1)}, bf16[128,512]{1,0:T(8,128)(2,1)}, u32[]{:S(2)}, u32[]{:S(2)}) %collective-permute-start.13) | collective-permute-done | bytes 131104 | tf_op jit(solution)/shard_map/ppermute | solution.py:252
  62.4 0.7 collective-permute-start.9
  63.1 1.1 %local_grads.1 = (f32[128,512]{1,0:T(8,128)S(1)}, f32[128,512]{1,0:T(8,128)S(1)}) custom-call(s32[1,128]{1,0:T(1,128)S(1)} %bitcast.14, bf16[128,512]{1,0:T(8,128)(2,1)S(1)} %copy-done.3, bf16[128,512]{1,0:T(8,128)(2,1)S(1)} %copy-done.5, bf16[128,512]{1,0:T(8,128)(2,1)S(1)} %get-tuple-element.19.cot_ref, bf16[128,512]{1,0:T(8,128)(2,1)S(1)} %get-tuple-element.27.sol_ref, ...), custom_call_target="tpu_custom_call" | custom-call | flops 117440512 | bytes 1180160 | tf_op jit(solution)/shard_map/local_grads/pallas_call | solution.py:37
  64.2 0.9 collective-permute-start.8
  65.0 0.8 collective-permute-start.7
  65.8 0.3 collective-permute-start.6
  66.1 1.7 %fusion.2 = f32[512,512]{1,0:T(8,128)S(1)} fusion(bf16[128,512]{1,0:T(8,128)(2,1)} %collective-permute-done.14, bf16[128,512]{1,0:T(8,128)(2,1)} %collective-permute-done.13, bf16[128,512]{1,0:T(8,128)(2,1)} %collective-permute-done.12, bf16[128,512]{1,0:T(8,128)(2,1)S(1)} %get-tuple-element.33, bf16[128,512]{1,0:T(8,128)(2,1)} %collective-permute-done.17, ...), kind=kOutput, calls=%fused_computation.4 | convolution fusion | flops 272629760 | bytes 2097152 | tf_op jit(solution)/shard_map/dot_general | solution.py:344
  67.8 3.0 %collective-permute-done.10 = bf16[1040,128]{1,0:T(8,128)(2,1)S(1)} collective-permute-done((bf16[1040,128]{1,0:T(8,128)(2,1)S(1)}, bf16[1040,128]{1,0:T(8,128)(2,1)S(1)}, u32[]{:S(2)}, u32[]{:S(2)}) %collective-permute-start.10) | collective-permute-done | bytes 266272 | tf_op jit(solution)/shard_map/ppermute | solution.py:247
  70.8 1.6 %collective-permute-done.9 = bf16[1040,128]{1,0:T(8,128)(2,1)S(1)} collective-permute-done((bf16[1040,128]{1,0:T(8,128)(2,1)S(1)}, bf16[1040,128]{1,0:T(8,128)(2,1)S(1)}, u32[]{:S(2)}, u32[]{:S(2)}) %collective-permute-start.9) | collective-permute-done | bytes 266272 | tf_op jit(solution)/shard_map/ppermute | solution.py:247
  72.4 0.3 fusion.1.near_ref
  72.7 9.1 %collective-permute-start.11 = (bf16[1040,128]{1,0:T(8,128)(2,1)S(1)}, bf16[1040,128]{1,0:T(8,128)(2,1)S(1)}, u32[]{:S(2)}, u32[]{:S(2)}) collective-permute-start(bf16[1040,128]{1,0:T(8,128)(2,1)S(1)} %fusion.1.near_ref), channel_id=1, source_target_pairs={{0,24},{4,28},{8,0},{12,4},{16,8},{20,12},{24,16},{28,20},{1,25},{... | collective-permute-start | bytes 798728 | tf_op jit(solution)/shard_map/ppermute | solution.py:247
  81.8 0.7 add_convert_fusion
  82.5 0.9 bitcast_add_fusion
  83.4 4.7 %collective-permute-done.11.far_ref = bf16[1040,128]{1,0:T(8,128)(2,1)S(1)} collective-permute-done((bf16[1040,128]{1,0:T(8,128)(2,1)S(1)}, bf16[1040,128]{1,0:T(8,128)(2,1)S(1)}, u32[]{:S(2)}, u32[]{:S(2)}) %collective-permute-start.11) | collective-permute-done | bytes 266272 | tf_op jit(solution)/shard_map/ppermute | solution.py:247
  88.1 1.0 %final_grads.1 = (bf16[128,512]{1,0:T(8,128)(2,1)}, bf16[128,512]{1,0:T(8,128)(2,1)}) custom-call(s32[1,128]{1,0:T(1,128)S(1)} %bitcast.15, bf16[128,512]{1,0:T(8,128)(2,1)S(1)} %copy-done.3, bf16[128,512]{1,0:T(8,128)(2,1)S(1)} %copy-done.5, bf16[1040,128]{1,0:T(8,128)(2,1)S(1)} %fusion.1.near_ref, bf16[1040,128]{1,0:T(8,128)(2,1)S(1)} %collective-permute-done.11.far_ref, ...), custom_call_target="tpu_custom_call" | custom-call | flops 50331648 | bytes 1581568 | tf_op jit(solution)/shard_map/final_grads/pallas_call | solution.py:37
  (43 shorter events, 0.1 us)
Async XLA Ops:
  0.6 34.6 %copy-start.9 = (s32[128]{0:T(128)S(1)}, s32[128]{0:T(128)}, u32[]{:S(2)}) copy-start(s32[128]{0:T(128)} %param.13) | copy-start | bytes 1540
  0.6 34.5 %copy-start.13 = (f32[4]{0:T(128)S(1)}, f32[4]{0:T(128)}, u32[]{:S(2)}) copy-start(f32[4]{0:T(128)} %ridge_ref.1) | copy-start | bytes 52
  0.7 0.9 %copy-start.2 = (bf16[128,512]{1,0:T(8,128)(2,1)S(1)}, bf16[128,512]{1,0:T(8,128)(2,1)}, u32[]{:S(2)}) copy-start(bf16[128,512]{1,0:T(8,128)(2,1)} %key_ref.7) | copy-start | bytes 393220
  1.6 0.9 %copy-start.4 = (bf16[128,512]{1,0:T(8,128)(2,1)S(1)}, bf16[128,512]{1,0:T(8,128)(2,1)}, u32[]{:S(2)}) copy-start(bf16[128,512]{1,0:T(8,128)(2,1)} %value_ref.7) | copy-start | bytes 393220
  2.5 0.7 copy-start.8
  3.1 32.1 %copy-start.3 = (bf16[128,512]{1,0:T(8,128)(2,1)S(1)}, bf16[128,512]{1,0:T(8,128)(2,1)}, u32[]{:S(2)}) copy-start(bf16[128,512]{1,0:T(8,128)(2,1)} %key_ref.7) | copy-start | bytes 393220
  3.1 32.1 %copy-start.5 = (bf16[128,512]{1,0:T(8,128)(2,1)S(1)}, bf16[128,512]{1,0:T(8,128)(2,1)}, u32[]{:S(2)}) copy-start(bf16[128,512]{1,0:T(8,128)(2,1)} %value_ref.7) | copy-start | bytes 393220
  3.1 32.1 %copy-start.12 = (bf16[128,512]{1,0:T(8,128)(2,1)S(1)}, bf16[128,512]{1,0:T(8,128)(2,1)}, u32[]{:S(2)}) copy-start(bf16[128,512]{1,0:T(8,128)(2,1)} %query_ref.1) | copy-start | bytes 393220
  3.5 11.5 %collective-permute-start.4 = (bf16[1040,128]{1,0:T(8,128)(2,1)S(1)}, bf16[1040,128]{1,0:T(8,128)(2,1)S(1)}, u32[]{:S(2)}, u32[]{:S(2)}) collective-permute-start(bf16[1040,128]{1,0:T(8,128)(2,1)S(1)} %tail_states.1), channel_id=1, source_target_pairs={{0,8},{4,12},{8,16},{12,20},{16,24},{20,28},{24,0},{28,4},{1,9},{5... | collective-permute-start | bytes 798728 | tf_op jit(solution)/shard_map/ppermute | solution.py:247
  6.6 15.1 %collective-permute-start.3 = (bf16[1040,128]{1,0:T(8,128)(2,1)S(1)}, bf16[1040,128]{1,0:T(8,128)(2,1)S(1)}, u32[]{:S(2)}, u32[]{:S(2)}) collective-permute-start(bf16[1040,128]{1,0:T(8,128)(2,1)S(1)} %tail_states.1), channel_id=1, source_target_pairs={{0,4},{4,8},{8,12},{12,16},{16,20},{20,24},{24,28},{28,0},{1,5},{5... | collective-permute-start | bytes 798728 | tf_op jit(solution)/shard_map/ppermute | solution.py:247
  8.1 13.6 %copy-start.14 = (pred[1040]{0:T(1024)(128)(4,1)}, pred[1040]{0:T(1024)(128)(4,1)S(1)}, u32[]{:S(2)}) copy-start(pred[1040]{0:T(1024)(128)(4,1)S(1)} %iota_compare_fusion) | copy-start | bytes 3124
  22.0 12.5 %collective-permute-start.5 = (bf16[1040,128]{1,0:T(8,128)(2,1)S(1)}, bf16[1040,128]{1,0:T(8,128)(2,1)S(1)}, u32[]{:S(2)}, u32[]{:S(2)}) collective-permute-start(bf16[1040,128]{1,0:T(8,128)(2,1)S(1)} %fusion.near_ref), channel_id=1, source_target_pairs={{0,8},{4,12},{8,16},{12,20},{16,24},{20,28},{24,0},{28,4},{1,9},{5... | collective-permute-start | bytes 798728 | tf_op jit(solution)/shard_map/ppermute | solution.py:247
  22.0 2.0 %collective-permute-start = (bf16[128,512]{1,0:T(8,128)(2,1)}, bf16[128,512]{1,0:T(8,128)(2,1)S(1)}, u32[]{:S(2)}, u32[]{:S(2)}) collective-permute-start(bf16[128,512]{1,0:T(8,128)(2,1)} %refs_0_.1), channel_id=1, source_target_pairs={{0,1},{1,0},{2,3},{3,2},{4,5},{5,4},{6,7},{7,6},{8,9},{9,8},{10,11... | collective-permute-start | bytes 393224 | tf_op jit(solution)/shard_map/ppermute | solution.py:252
  22.1 6.6 %collective-permute-start.1 = (bf16[128,512]{1,0:T(8,128)(2,1)}, bf16[128,512]{1,0:T(8,128)(2,1)S(1)}, u32[]{:S(2)}, u32[]{:S(2)}) collective-permute-start(bf16[128,512]{1,0:T(8,128)(2,1)} %refs_0_.1), channel_id=1, source_target_pairs={{0,2},{1,3},{2,0},{3,1},{4,6},{5,7},{6,4},{7,5},{8,10},{9,11},{10,... | collective-permute-start | bytes 393224 | tf_op jit(solution)/shard_map/ppermute | solution.py:252
  23.7 6.9 %collective-permute-start.2 = (bf16[128,512]{1,0:T(8,128)(2,1)}, bf16[128,512]{1,0:T(8,128)(2,1)S(1)}, u32[]{:S(2)}, u32[]{:S(2)}) collective-permute-start(bf16[128,512]{1,0:T(8,128)(2,1)} %refs_0_.1), channel_id=1, source_target_pairs={{0,3},{1,2},{2,1},{3,0},{4,7},{5,6},{6,5},{7,4},{8,11},{9,10},{10,... | collective-permute-start | bytes 393224 | tf_op jit(solution)/shard_map/ppermute | solution.py:252
  30.6 1.6 %copy-start = (bf16[512,2048]{1,0:T(8,128)(2,1)S(1)}, bf16[512,2048]{1,0:T(8,128)(2,1)}, u32[]{:S(2)}) copy-start(bf16[512,2048]{1,0:T(8,128)(2,1)} %weight_ref.1) | copy-start | bytes 6291460
  32.2 0.9 %copy-start.6 = (bf16[128,512]{1,0:T(8,128)(2,1)S(1)}, bf16[128,512]{1,0:T(8,128)(2,1)}, u32[]{:S(2)}) copy-start(bf16[128,512]{1,0:T(8,128)(2,1)} %refs_0_.1) | copy-start | bytes 393220
  34.5 22.5 %copy-start.1 = (bf16[512,2048]{1,0:T(8,128)(2,1)S(1)}, bf16[512,2048]{1,0:T(8,128)(2,1)}, u32[]{:S(2)}) copy-start(bf16[512,2048]{1,0:T(8,128)(2,1)} %weight_ref.1) | copy-start | bytes 6291460
  34.5 0.7 copy-start.10
  35.2 1.0 %copy-start.11 = (bf16[1040,128]{1,0:T(8,128)(2,1)S(1)}, bf16[1040,128]{1,0:T(8,128)(2,1)}, u32[]{:S(2)}) copy-start(bf16[1040,128]{1,0:T(8,128)(2,1)} %copy-done.10) | copy-start | bytes 798724
  41.2 21.8 %copy-start.7 = (bf16[128,512]{1,0:T(8,128)(2,1)S(1)}, bf16[128,512]{1,0:T(8,128)(2,1)}, u32[]{:S(2)}) copy-start(bf16[128,512]{1,0:T(8,128)(2,1)} %get-tuple-element.15.dual_ref) | copy-start | bytes 393220
  41.2 15.7 %collective-permute-start.16 = (bf16[128,512]{1,0:T(8,128)(2,1)S(1)}, bf16[128,512]{1,0:T(8,128)(2,1)}, u32[]{:S(2)}, u32[]{:S(2)}) collective-permute-start(bf16[128,512]{1,0:T(8,128)(2,1)S(1)} %get-tuple-element.20.mixed_ref), channel_id=1, source_target_pairs={{0,16},{4,20},{8,24},{12,28},{16,0},{20,4},{24,8},{28,12},{1,17},{... | collective-permute-start | bytes 393224 | tf_op jit(solution)/shard_map/ppermute | solution.py:252
  44.4 13.6 %collective-permute-start.14 = (bf16[128,512]{1,0:T(8,128)(2,1)}, bf16[128,512]{1,0:T(8,128)(2,1)}, u32[]{:S(2)}, u32[]{:S(2)}) collective-permute-start(bf16[128,512]{1,0:T(8,128)(2,1)} %get-tuple-element.34), channel_id=1, source_target_pairs={{0,24},{4,28},{8,16},{12,20},{16,8},{20,12},{24,0},{28,4},{1,25},{... | collective-permute-start | bytes 393224 | tf_op jit(solution)/shard_map/ppermute | solution.py:252
  45.8 16.6 %collective-permute-start.13 = (bf16[128,512]{1,0:T(8,128)(2,1)}, bf16[128,512]{1,0:T(8,128)(2,1)}, u32[]{:S(2)}, u32[]{:S(2)}) collective-permute-start(bf16[128,512]{1,0:T(8,128)(2,1)} %get-tuple-element.35), channel_id=1, source_target_pairs={{0,16},{4,20},{8,24},{12,28},{16,0},{20,4},{24,8},{28,12},{1,17},{... | collective-permute-start | bytes 393224 | tf_op jit(solution)/shard_map/ppermute | solution.py:252
  47.8 16.3 %collective-permute-start.12 = (bf16[128,512]{1,0:T(8,128)(2,1)S(1)}, bf16[128,512]{1,0:T(8,128)(2,1)}, u32[]{:S(2)}, u32[]{:S(2)}) collective-permute-start(bf16[128,512]{1,0:T(8,128)(2,1)S(1)} %get-tuple-element.36), channel_id=1, source_target_pairs={{0,8},{4,12},{8,0},{12,4},{16,24},{20,28},{24,16},{28,20},{1,9},{5... | collective-permute-start | bytes 393224 | tf_op jit(solution)/shard_map/ppermute | solution.py:252
  48.8 16.2 %collective-permute-start.15 = (bf16[128,512]{1,0:T(8,128)(2,1)S(1)}, bf16[128,512]{1,0:T(8,128)(2,1)}, u32[]{:S(2)}, u32[]{:S(2)}) collective-permute-start(bf16[128,512]{1,0:T(8,128)(2,1)S(1)} %get-tuple-element.20.mixed_ref), channel_id=1, source_target_pairs={{0,8},{4,12},{8,0},{12,4},{16,24},{20,28},{24,16},{28,20},{1,9},{5... | collective-permute-start | bytes 393224 | tf_op jit(solution)/shard_map/ppermute | solution.py:252
  57.0 8.8 %collective-permute-start.17 = (bf16[128,512]{1,0:T(8,128)(2,1)}, bf16[128,512]{1,0:T(8,128)(2,1)}, u32[]{:S(2)}, u32[]{:S(2)}) collective-permute-start(bf16[128,512]{1,0:T(8,128)(2,1)} %collective-permute-done.16), channel_id=1, source_target_pairs={{0,8},{4,12},{8,0},{12,4},{16,24},{20,28},{24,16},{28,20},{1,9},{5... | collective-permute-start | bytes 393224 | tf_op jit(solution)/shard_map/ppermute | solution.py:252
  58.0 12.8 %collective-permute-start.10 = (bf16[1040,128]{1,0:T(8,128)(2,1)S(1)}, bf16[1040,128]{1,0:T(8,128)(2,1)S(1)}, u32[]{:S(2)}, u32[]{:S(2)}) collective-permute-start(bf16[1040,128]{1,0:T(8,128)(2,1)S(1)} %get-tuple-element.26), channel_id=1, source_target_pairs={{0,24},{4,28},{8,0},{12,4},{16,8},{20,12},{24,16},{28,20},{1,25},{... | collective-permute-start | bytes 798728 | tf_op jit(solution)/shard_map/ppermute | solution.py:247
  62.4 10.0 %collective-permute-start.9 = (bf16[1040,128]{1,0:T(8,128)(2,1)S(1)}, bf16[1040,128]{1,0:T(8,128)(2,1)S(1)}, u32[]{:S(2)}, u32[]{:S(2)}) collective-permute-start(bf16[1040,128]{1,0:T(8,128)(2,1)S(1)} %get-tuple-element.26), channel_id=1, source_target_pairs={{0,28},{4,0},{8,4},{12,8},{16,12},{20,16},{24,20},{28,24},{1,29},{... | collective-permute-start | bytes 798728 | tf_op jit(solution)/shard_map/ppermute | solution.py:247
  64.2 17.6 %collective-permute-start.8 = (bf16[128,512]{1,0:T(8,128)(2,1)S(1)}, bf16[128,512]{1,0:T(8,128)(2,1)S(1)}, u32[]{:S(2)}, u32[]{:S(2)}) collective-permute-start(bf16[128,512]{1,0:T(8,128)(2,1)S(1)} %get-tuple-element.24), channel_id=1, source_target_pairs={{0,3},{1,2},{2,1},{3,0},{4,7},{5,6},{6,5},{7,4},{8,11},{9,10},{10,... | collective-permute-start | bytes 393224 | tf_op jit(solution)/shard_map/ppermute | solution.py:252
  65.0 16.7 %collective-permute-start.7 = (bf16[128,512]{1,0:T(8,128)(2,1)S(1)}, bf16[128,512]{1,0:T(8,128)(2,1)S(1)}, u32[]{:S(2)}, u32[]{:S(2)}) collective-permute-start(bf16[128,512]{1,0:T(8,128)(2,1)S(1)} %get-tuple-element.23), channel_id=1, source_target_pairs={{0,2},{1,3},{2,0},{3,1},{4,6},{5,7},{6,4},{7,5},{8,10},{9,11},{10,... | collective-permute-start | bytes 393224 | tf_op jit(solution)/shard_map/ppermute | solution.py:252
  65.8 16.0 %collective-permute-start.6 = (bf16[128,512]{1,0:T(8,128)(2,1)S(1)}, bf16[128,512]{1,0:T(8,128)(2,1)S(1)}, u32[]{:S(2)}, u32[]{:S(2)}) collective-permute-start(bf16[128,512]{1,0:T(8,128)(2,1)S(1)} %get-tuple-element.22), channel_id=1, source_target_pairs={{0,1},{1,0},{2,3},{3,2},{4,5},{5,4},{6,7},{7,6},{8,9},{9,8},{10,11... | collective-permute-start | bytes 393224 | tf_op jit(solution)/shard_map/ppermute | solution.py:252
  66.1 6.3 %copy-start.15 = (pred[1040]{0:T(1024)(128)(4,1)S(1)}, pred[1040]{0:T(1024)(128)(4,1)}, u32[]{:S(2)}) copy-start(pred[1040]{0:T(1024)(128)(4,1)} %copy-done.14) | copy-start | bytes 3124
  70.8 11.7 %collective-permute-start.18 = (bf16[256,512]{1,0:T(8,128)(2,1)S(1)}, bf16[256,512]{1,0:T(8,128)(2,1)S(1)}, u32[]{:S(2)}, u32[]{:S(2)}) collective-permute-start(bf16[256,512]{1,0:T(8,128)(2,1)S(1)} %fusion.17), channel_id=1, source_target_pairs={{0,4},{4,0},{8,12},{12,8},{16,20},{20,16},{24,28},{28,24},{1,5},{5... | collective-permute-start | bytes 786440 | tf_op jit(solution)/shard_map/ppermute | solution.py:252
  72.7 15.4 %collective-permute-start.11 = (bf16[1040,128]{1,0:T(8,128)(2,1)S(1)}, bf16[1040,128]{1,0:T(8,128)(2,1)S(1)}, u32[]{:S(2)}, u32[]{:S(2)}) collective-permute-start(bf16[1040,128]{1,0:T(8,128)(2,1)S(1)} %fusion.1.near_ref), channel_id=1, source_target_pairs={{0,24},{4,28},{8,0},{12,4},{16,8},{20,12},{24,16},{28,20},{1,25},{... | collective-permute-start | bytes 798728 | tf_op jit(solution)/shard_map/ppermute | solution.py:247

commit v2 on v1

--- a/solution.py
+++ b/solution.py
@@ -13,6 +13,7 @@
 F32 = jnp.float32
 BF16 = jnp.bfloat16
 VMEM_LIMIT = 48 * 1024 * 1024
+FLOPS_PER_US = 1e9
 
 
 def mm(a, b):
@@ -27,7 +28,7 @@
     return lax.dot_general(a, b, (((0,), (0,)), ((), ())), preferred_element_type=F32)
 
 
-def kernel_call(body, out_shape, operands, flops, name, smem=()):
+def kernel_call(body, out_shape, operands, microseconds, name, smem=()):
     in_specs = [
         pl.BlockSpec(memory_space=pltpu.SMEM if i in smem else pltpu.VMEM)
         for i in range(len(operands))
@@ -40,7 +41,7 @@
         in_specs=in_specs,
         out_specs=[pl.BlockSpec(memory_space=pltpu.VMEM)] * len(out_shape),
         compiler_params=pltpu.CompilerParams(vmem_limit_bytes=VMEM_LIMIT),
-        cost_estimate=pl.CostEstimate(flops=flops, bytes_accessed=nbytes, transcendentals=0),
+        cost_estimate=pl.CostEstimate(flops=int(microseconds * FLOPS_PER_US), bytes_accessed=nbytes, transcendentals=0),
         name=name,
     )(*operands)
 
@@ -54,6 +55,54 @@
     row = lax.broadcasted_iota(jnp.int32, across.shape, 0)
     col = lax.broadcasted_iota(jnp.int32, across.shape, 1)
     return (across == down) & (col <= row)
+
+
+def triangle(width):
+    row = lax.broadcasted_iota(jnp.int32, (width, width), 0)
+    col = lax.broadcasted_iota(jnp.int32, (width, width), 1)
+    return col < row, col == row
+
+
+def pack_symmetric(out_ref, base, extra, matrices):
+    width = matrices[0].shape[0]
+    below, diagonal = triangle(width)
+    rows = []
+    for pair in range(len(matrices) // 2):
+        one, two = matrices[2 * pair], matrices[2 * pair + 1]
+        square = jnp.where(below | diagonal, one, two)
+        out_ref[base + pair * width : base + (pair + 1) * width, :] = square.astype(BF16)
+        rows.append(jnp.sum(jnp.where(diagonal, two, 0.0), axis=0, keepdims=True))
+    rows.append(jnp.broadcast_to(extra, (LABEL_ROWS - len(rows), width)))
+    out_ref[base + len(matrices) // 2 * width :, :] = jnp.concatenate(rows, axis=0).astype(BF16)
+
+
+def unpack_symmetric(square, row):
+    below, diagonal = triangle(square.shape[0])
+    flipped = square.T
+    one = jnp.where(below | diagonal, square, flipped)
+    two = jnp.where(diagonal, row, jnp.where(below, flipped, square))
+    return one, two
+
+
+def received_states(near_ref, far_ref, heads, width):
+    base = heads * width
+    tail = base + heads // 2 * width
+    near_rest = near_ref[tail : tail + LABEL_ROWS, :].astype(F32)
+    far_rest = far_ref[tail : tail + LABEL_ROWS, :].astype(F32)
+    label = near_rest[LABEL_ROWS - 1 :, :]
+    joined = (label == far_rest[LABEL_ROWS - 1 :, :]).astype(F32)
+    rest = near_rest + joined * far_rest
+
+    def square(index):
+        rows = slice(index * width, (index + 1) * width)
+        return near_ref[rows, :].astype(F32) + joined * far_ref[rows, :].astype(F32)
+
+    full = [square(h).astype(BF16) for h in range(heads)]
+    symmetric = []
+    for pair in range(heads // 2):
+        for matrix in unpack_symmetric(square(heads + pair), rest[pair : pair + 1, :]):
+            symmetric.append(matrix.astype(BF16))
+    return label, full, symmetric
 
 
 def tail_body(heads, width, doc_ref, key_ref, value_ref, out_ref):
@@ -61,17 +110,14 @@
     across, down = label_grids(doc_ref, piece)
     last = jnp.max(across, axis=1, keepdims=True)
     tail = (down == last).astype(F32).astype(BF16)
-    states = heads * width
+    grams = []
     for h in range(heads):
         cols = slice(h * width, (h + 1) * width)
         key_h = key_ref[:, cols]
         masked = key_h * tail[:, :width]
-        out_ref[h * width : (h + 1) * width, :] = mm_tn(key_h, masked).astype(BF16)
-        out_ref[states + h * width : states + (h + 1) * width, :] = mm_tn(
-            value_ref[:, cols], masked
-        ).astype(BF16)
-    label = (last[:LABEL_ROWS] + 1).astype(F32)
-    out_ref[2 * states :, :] = jnp.broadcast_to(label, (LABEL_ROWS, width)).astype(BF16)
+        grams.append(mm_tn(key_h, masked))
+        out_ref[h * width : (h + 1) * width, :] = mm_tn(value_ref[:, cols], masked).astype(BF16)
+    pack_symmetric(out_ref, heads * width, (last[:1] + 1).astype(F32), grams)
 
 
 def cot_body(count, shard, place_ref, *refs):
@@ -118,38 +164,27 @@
     out_ref,
 ):
     piece = key_ref.shape[0]
-    states = heads * width
     across, down = label_grids(doc_ref, piece)
     same = document_mask(across, down).astype(F32)
     same_two = jnp.concatenate([same, same], axis=0)
     first = jnp.min(across, axis=1, keepdims=True)
     head_rows = (down == first)[:, :width].astype(F32)
-    near_label = near_ref[2 * states : 2 * states + LABEL_ROWS, :].astype(F32)[0:1, :]
-    far_label = far_ref[2 * states : 2 * states + LABEL_ROWS, :].astype(F32)[0:1, :]
-    joined = jnp.broadcast_to((near_label == far_label).astype(F32), (width, width))
-    carried = ((down + 1).astype(F32)[:, :width] == near_label).astype(F32)
+    label, value_states, gram_states = received_states(near_ref, far_ref, heads, width)
+    carried = ((down + 1).astype(F32)[:, :width] == label).astype(F32)
     carried_two = jnp.concatenate([carried, carried], axis=0)
-
-    def state(index):
-        rows = slice(index * width, (index + 1) * width)
-        return (near_ref[rows, :].astype(F32) + joined * far_ref[rows, :].astype(F32)).astype(BF16)
-
-    keys, rhs_keys, values, grams, solutions, residuals, directions, squares = ([] for _ in range(8))
-    value_states = []
+    keys, rhs_keys, values, solutions, residuals, directions, squares = ([] for _ in range(7))
     for h in range(heads):
         cols = slice(h * width, (h + 1) * width)
         key_h = key_ref[:, cols]
         value_h = value_ref[:, cols]
-        value_state = state(heads + h)
         cot_h = cot_ref[:, cols]
-        both = mm(cot_h, jnp.concatenate([value_h.T, value_state], axis=1))
+        both = mm(cot_h, jnp.concatenate([value_h.T, value_states[h]], axis=1))
         scores = (both[:, :piece] * same).astype(BF16)
         target = carried * both[:, piece:] + mm(scores, key_h)
         start = jnp.concatenate([query_ref[:, cols].astype(F32), target], axis=0)
         keys.append(key_h)
         values.append(value_h)
-        value_states.append(value_state)
-        rhs_keys.append(jnp.concatenate([key_h.T, state(h)], axis=1))
+        rhs_keys.append(jnp.concatenate([key_h.T, gram_states[h]], axis=1))
         solutions.append(jnp.zeros_like(start))
         residuals.append(start)
         directions.append(start)
@@ -167,6 +202,7 @@
                 new_sq = jnp.sum(residuals[h] * residuals[h], axis=1, keepdims=True)
                 directions[h] = residuals[h] + new_sq / (squares[h] + EPSILON) * p
                 squares[h] = new_sq
+    crosses = []
     for h in range(heads):
         cols = slice(h * width, (h + 1) * width)
         sol = solutions[h][:piece]
@@ -181,9 +217,8 @@
         masked = (head_rows * sol).astype(BF16)
         out_ref[h * width : (h + 1) * width, :] = mm_tn(cot_ref[:, cols], masked).astype(BF16)
         cross = mm_tn(dual_b, masked)
-        out_ref[states + h * width : states + (h + 1) * width, :] = (cross + cross.T).astype(BF16)
-    label = (first[:LABEL_ROWS] + 1).astype(F32)
-    out_ref[2 * states :, :] = jnp.broadcast_to(label, (LABEL_ROWS, width)).astype(BF16)
+        crosses.append(cross + cross.T)
+    pack_symmetric(out_ref, heads * width, (first[:1] + 1).astype(F32), crosses)
 
 
 def local_grads_body(
@@ -221,21 +256,13 @@
     grad_v_ref,
 ):
     piece = key_ref.shape[0]
-    states = heads * width
     _, down = label_grids(doc_ref, piece)
-    near_label = near_ref[2 * states : 2 * states + LABEL_ROWS, :].astype(F32)[0:1, :]
-    far_label = far_ref[2 * states : 2 * states + LABEL_ROWS, :].astype(F32)[0:1, :]
-    joined = jnp.broadcast_to((near_label == far_label).astype(F32), (width, width))
-    later = ((down + 1).astype(F32)[:, :width] == near_label).astype(F32)
-
-    def state(index):
-        rows = slice(index * width, (index + 1) * width)
-        return (near_ref[rows, :].astype(F32) + joined * far_ref[rows, :].astype(F32)).astype(BF16)
-
+    label, grad_states, gram_grads = received_states(near_ref, far_ref, heads, width)
+    later = ((down + 1).astype(F32)[:, :width] == label).astype(F32)
     for h in range(heads):
         cols = slice(h * width, (h + 1) * width)
         key_h, value_h = key_ref[:, cols], value_ref[:, cols]
-        grad_state, gram_grad = state(h), state(heads + h)
+        grad_state, gram_grad = grad_states[h], gram_grads[h]
         grad_v = local_v_ref[:, cols] + later * mm_nt(key_h, grad_state)
         grad_k = local_k_ref[:, cols] + later * (mm(value_h, grad_state) - mm(key_h, gram_grad))
         grad_v_ref[:, cols] = grad_v.astype(BF16)
@@ -252,28 +279,30 @@
     return lax.ppermute(value, axis, [(i, i ^ mask) for i in range(devices)])
 
 
-def joined_states(near, far, states):
+def joined_states(near, far):
     rows = lax.broadcasted_iota(jnp.int32, near.shape, 0)
-    matches = (near[states:, :] == far[states:, :])[0:1, :]
+    numbers = near.shape[0] - LABEL_ROWS // 2
+    matches = (near[-1:, :] == far[-1:, :]) & (rows < numbers)
     total = near.astype(F32) + far.astype(F32)
-    return jnp.where((rows < states) & matches, total, near.astype(F32)).astype(BF16)
-
-
-def scan_states(element, states, sign):
+    return jnp.where(matches, total, near.astype(F32)).astype(BF16)
+
+
+def scan_states(element, sign, beside):
     window = lax.axis_size("seq") // 2
     near, far, reach = rotated(element, sign), rotated(element, 2 * sign), 2
+    near, far, beside = lax.optimization_barrier((near, far, beside))
     while reach < window:
-        near = joined_states(near, far, states)
+        near = joined_states(near, far)
         far = rotated(near, sign * reach)
         reach *= 2
-    return near, far
+    return near, far, beside
 
 
 def per_device(query_rows, key_rows, value_rows, ridge_reg, out_weight, out_grad, doc_ids):
     heads = ridge_reg.shape[0]
     piece, features = key_rows.shape
     width = features // heads
-    states = 2 * heads * width
+    states = heads * width + heads // 2 * width
     seq_size, head_size = lax.axis_size("seq"), lax.axis_size("head")
     seq_at, head_at = lax.axis_index("seq"), lax.axis_index("head")
     place = jnp.stack([seq_at, head_at]).astype(jnp.int32)
@@ -288,17 +317,16 @@
         functools.partial(tail_body, heads, width),
         [payload],
         (doc_row, key_rows, value_rows),
-        4 * piece * features * width,
+        0.5,
         "tail_states",
     )
-    near, far = scan_states(element, states, 1)
-
     cots = [out_grad] + [swapped(out_grad, "head", b) for b in range(1, head_size)]
+    near, far, cots = scan_states(element, 1, cots)
     out_cot, cot_full = kernel_call(
         functools.partial(cot_body, head_size, shard),
         [rows_bf16, jax.ShapeDtypeStruct((piece, model), BF16)],
         (place, *cots, out_weight),
-        2 * piece * features * model,
+        1.5,
         "cotangent",
         smem=(0,),
     )
@@ -307,18 +335,16 @@
         functools.partial(solve_body, heads, width),
         [rows_bf16, rows_bf16, rows_bf16, payload],
         (ridge_reg, doc_row, query_rows, key_rows, value_rows, out_cot, near, far),
-        60 * piece * features * width,
+        5.0,
         "solve",
         smem=(0,),
     )
-    later_near, later_far = scan_states(back, states, -1)
-
     own, *sends = kernel_call(
         functools.partial(project_body, head_size, shard),
         [jax.ShapeDtypeStruct((piece, shard), F32)]
         + [jax.ShapeDtypeStruct((piece, shard), BF16)] * (head_size - 1),
         (place, mixed, out_weight),
-        2 * piece * features * model,
+        1.0,
         "project",
         smem=(0,),
     )
@@ -330,17 +356,21 @@
     pair_rows = 2 * (model // seq_size)
     pairs = seq_size // 2
     pair_at = seq_at // 2
-    cot_blocks, mixed_blocks = [], []
+    cot_blocks = []
     for c in range(pairs):
         start = jnp.bitwise_xor(pair_at, c) * pair_rows
         block = lax.dynamic_slice_in_dim(cot_full, start, pair_rows, 1)
         cot_blocks.append(block if c == 0 else swapped(block, "seq", 2 * c))
-        if c == 0:
-            mixed_blocks.append(mixed)
-        else:
-            low = c & -c
-            rest = mixed_blocks[c ^ low]
-            mixed_blocks.append(swapped(rest, "seq", 2 * low))
+    gathered, cot_blocks = lax.optimization_barrier((mixed, cot_blocks))
+    mixed_blocks = [gathered] + [None] * (pairs - 1)
+    for c in range(1, pairs):
+        if c & (c - 1) == 0:
+            mixed_blocks[c] = swapped(gathered, "seq", 2 * c)
+    later_near, later_far, mixed_blocks = scan_states(back, -1, mixed_blocks)
+    for c in range(1, pairs):
+        low = c & -c
+        if c != low:
+            mixed_blocks[c] = swapped(mixed_blocks[c ^ low], "seq", 2 * low)
     pair_grad = lax.dot_general(
         jnp.concatenate(cot_blocks, axis=0),
         jnp.concatenate(mixed_blocks, axis=0),
@@ -356,14 +386,14 @@
         functools.partial(local_grads_body, heads, width),
         [rows_f32, rows_f32],
         (doc_row, key_rows, value_rows, out_cot, sol, dual),
-        14 * piece * features * width,
+        1.1,
         "local_grads",
     )
     grad_keys, grad_values = kernel_call(
         functools.partial(final_grads_body, heads, width),
         [rows_bf16, rows_bf16],
         (doc_row, key_rows, value_rows, later_near, later_far, local_k, local_v),
-        6 * piece * features * width,
+        1.0,
         "final_grads",
     )
     return (layer_out, dual, grad_keys, grad_values, grad_weight)

time: 89.3 us -> 69.4 us (0.78)
  waiting for transfers between devices: 38 us -> 16.5 us
  local copies, waits for them, and re-layouts: 7.42 us -> 3.45 us
  starting transfers between devices: 29.1 us -> 33 us
  other arithmetic: 2.2 us -> 3.67 us
    ppermute x6, waiting for transfers between devices: 22.8 us -> 4.01 us  [rotated(): lax.ppermute(value, 'seq', [(i, (i + by) % devices) for i in range(device...]
    ppermute x13, starting transfers between devices: 11.7 us -> 21.9 us  [swapped(): return lax.ppermute(value, axis, [(i, i ^ mask) for i in range(devices)])]
    ppermute x6, starting transfers between devices: 17.3 us -> 11.1 us  [rotated(): lax.ppermute(value, 'seq', [(i, (i + by) % devices) for i in range(device...]
    unnamed x32 -> x28, local copies, waits for them, and re-layouts: 6.64 us -> 2.67 us
    ppermute x13, waiting for transfers between devices: 15.2 us -> 12.5 us  [swapped(): return lax.ppermute(value, axis, [(i, i ^ mask) for i in range(devices)])]
  transfers between devices with their start and end apart: 19 -> 19, of which waited for: 9 -> 8; matrix products, arithmetic and copies ran while one was open for 5% -> 7% of each run, Pallas kernels for 4% -> 14%
where the time goes in v2:
time: 69.4 us; the launch traced here: 69.2 us
  starting transfers between devices  33 us (48%)
  waiting for transfers between devices  16.5 us (24%)
  Pallas kernels  10.1 us (15%)
  other arithmetic  3.67 us (5%)
  local copies, waits for them, and re-layouts  3.45 us (5%)
  matrix products  1.5 us (2%)
  between operations  0.86 us (1%)
    ppermute x13, starting transfers between devices, swapped(): return lax.ppermute(value, axis, [(i, i ^ mask) for i in range(devices)])  21.9 us
    ppermute x13, waiting for transfers between devices, swapped(): return lax.ppermute(value, axis, [(i, i ^ mask) for i in range(devices)])  12.5 us
    ppermute x6, starting transfers between devices, rotated(): lax.ppermute(value, 'seq', [(i, (i + by) % devices) for i in range(device...  11.1 us
    pallas_call x6, Pallas kernels, kernel_call(): pl.pallas_call(body, out_shape=out_shape, in_specs=in_specs, out_specs=[p...  10.1 us
    ppermute x6, waiting for transfers between devices, rotated(): lax.ppermute(value, 'seq', [(i, (i + by) % devices) for i in range(device...  4.01 us
    unnamed x28, local copies, waits for them, and re-layouts  2.67 us
    dot_general x1, matrix products, per_device(): lax.dot_general(jnp.concatenate(cot_blocks, axis=0), jnp.concatenate(mixe...  1.5 us
  transfers between devices with their start and end apart: 19, of which 8 were waited for; matrix products, arithmetic and copies ran while one was open for 7% of the time, Pallas kernels for 14%

profile of v2, /device:TPU:0, one launch (start us, length us, event | category | flops | bytes accessed | tf_op | source)
XLA Modules:
  0.0 69.2 jit_solution(14908043634952904324)
XLA Ops:
  0.6 0.0 copy-start.1
  0.7 0.0 copy-start.3
  0.7 1.0 %copy-done.3 = bf16[128,512]{1,0:T(8,128)(2,1)S(1)} copy-done((bf16[128,512]{1,0:T(8,128)(2,1)S(1)}, bf16[128,512]{1,0:T(8,128)(2,1)}, u32[]{:S(2)}) %copy-start.3) | copy-done | bytes 131096
  1.7 0.9 %copy-done.5 = bf16[128,512]{1,0:T(8,128)(2,1)S(1)} copy-done((bf16[128,512]{1,0:T(8,128)(2,1)S(1)}, bf16[128,512]{1,0:T(8,128)(2,1)}, u32[]{:S(2)}) %copy-start.5) | copy-done | bytes 131096
  2.6 0.7 copy-done.8
  3.3 0.4 tail_states.1
  3.7 3.0 %collective-permute-start = (bf16[784,128]{1,0:T(8,128)(2,1)S(1)}, bf16[784,128]{1,0:T(8,128)(2,1)S(1)}, u32[]{:S(2)}, u32[]{:S(2)}) collective-permute-start(bf16[784,128]{1,0:T(8,128)(2,1)S(1)} %tail_states.1), channel_id=1, source_target_pairs={{0,4},{4,8},{8,12},{12,16},{16,20},{20,24},{24,28},{28,0},{1,5},{5... | collective-permute-start | bytes 602120 | tf_op jit(solution)/shard_map/ppermute | solution.py:274
  6.7 1.6 %collective-permute-start.1 = (bf16[784,128]{1,0:T(8,128)(2,1)S(1)}, bf16[784,128]{1,0:T(8,128)(2,1)S(1)}, u32[]{:S(2)}, u32[]{:S(2)}) collective-permute-start(bf16[784,128]{1,0:T(8,128)(2,1)S(1)} %tail_states.1), channel_id=1, source_target_pairs={{0,8},{4,12},{8,16},{12,20},{16,24},{20,28},{24,0},{28,4},{1,9},{5... | collective-permute-start | bytes 602120 | tf_op jit(solution)/shard_map/ppermute | solution.py:274
  8.3 1.5 %collective-permute-start.3 = (bf16[128,512]{1,0:T(8,128)(2,1)}, bf16[128,512]{1,0:T(8,128)(2,1)S(1)}, u32[]{:S(2)}, u32[]{:S(2)}) collective-permute-start(bf16[128,512]{1,0:T(8,128)(2,1)} %refs_0_), channel_id=1, source_target_pairs={{0,2},{1,3},{2,0},{3,1},{4,6},{5,7},{6,4},{7,5},{8,10},{9,11},{10,... | collective-permute-start | bytes 393224 | tf_op jit(solution)/shard_map/ppermute | solution.py:279
  9.8 0.4 collective-permute-start.4
  10.1 0.1 pad_add_fusion.place_ref
  10.2 4.6 %collective-permute-done.3.refs_2_ = bf16[128,512]{1,0:T(8,128)(2,1)S(1)} collective-permute-done((bf16[128,512]{1,0:T(8,128)(2,1)}, bf16[128,512]{1,0:T(8,128)(2,1)S(1)}, u32[]{:S(2)}, u32[]{:S(2)}) %collective-permute-start.3) | collective-permute-done | bytes 131104 | tf_op jit(solution)/shard_map/ppermute | solution.py:279
  14.8 2.0 %collective-permute-done.4.refs_3_ = bf16[128,512]{1,0:T(8,128)(2,1)S(1)} collective-permute-done((bf16[128,512]{1,0:T(8,128)(2,1)}, bf16[128,512]{1,0:T(8,128)(2,1)S(1)}, u32[]{:S(2)}, u32[]{:S(2)}) %collective-permute-start.4) | collective-permute-done | bytes 131104 | tf_op jit(solution)/shard_map/ppermute | solution.py:279
  16.8 0.2 fusion.15.near_ref
  17.0 0.0 copy-start.2
  17.1 0.0 copy-start.4
  17.1 0.0 copy-start.6
  17.1 0.0 copy-start.7
  17.1 1.6 %collective-permute-start.5 = (bf16[784,128]{1,0:T(8,128)(2,1)S(1)}, bf16[784,128]{1,0:T(8,128)(2,1)S(1)}, u32[]{:S(2)}, u32[]{:S(2)}) collective-permute-start(bf16[784,128]{1,0:T(8,128)(2,1)S(1)} %fusion.15.near_ref), channel_id=1, source_target_pairs={{0,8},{4,12},{8,16},{12,20},{16,24},{20,28},{24,0},{28,4},{1,9},{5... | collective-permute-start | bytes 602120 | tf_op jit(solution)/shard_map/ppermute | solution.py:274
  18.7 1.4 %cotangent.1 = (bf16[128,512]{1,0:T(8,128)(2,1)S(1)}, bf16[128,2048]{1,0:T(8,128)(2,1)S(1)}) custom-call(s32[2]{0:T(128)S(1)} %pad_add_fusion.place_ref, bf16[128,512]{1,0:T(8,128)(2,1)S(1)} %copy-done.1, bf16[128,512]{1,0:T(8,128)(2,1)S(1)} %collective-permute-done.2.refs_1_, bf16[128,512]{1,0:T(8,128)(2,1)S(1)} %collective-permute-done.3.refs_2_, ...), custom_call_target="tpu_custom_call" | custom-call | flops 1500000000 | bytes 3276808 | tf_op jit(solution)/shard_map/cotangent/pallas_call | solution.py:38
  20.1 0.7 %constant_dynamic-slice_fusion = (bf16[128,512]{1,0:T(8,128)(2,1)S(1)}, bf16[128,512]{1,0:T(8,128)(2,1)S(1)}, bf16[128,512]{1,0:T(8,128)(2,1)}, bf16[128,512]{1,0:T(8,128)(2,1)}) fusion(bf16[128,2048]{1,0:T(8,128)(2,1)S(1)} %get-tuple-element.49, s32[]{:T(128)S(6)} %select_n.44, s32[]{:T(128)S(6)} %select_n.43, s32[]{:T(128)S(6)} %select_n.42, s32[]{:T(128)S(6)} %select_n.41), kind=kLoop, calls=%fused_computation.26 | loop fusion | bytes 1048592 | tf_op jit(solution)/shard_map/dynamic_slice | solution.py:362
  20.9 1.6 %collective-permute-start.11 = (bf16[128,512]{1,0:T(8,128)(2,1)}, bf16[128,512]{1,0:T(8,128)(2,1)}, u32[]{:S(2)}, u32[]{:S(2)}) collective-permute-start(bf16[128,512]{1,0:T(8,128)(2,1)} %get-tuple-element.67), channel_id=1, source_target_pairs={{0,8},{4,12},{8,0},{12,4},{16,24},{20,28},{24,16},{28,20},{1,9},{5... | collective-permute-start | bytes 393224 | tf_op jit(solution)/shard_map/ppermute | solution.py:279
  22.4 1.2 %collective-permute-start.12 = (bf16[128,512]{1,0:T(8,128)(2,1)S(1)}, bf16[128,512]{1,0:T(8,128)(2,1)}, u32[]{:S(2)}, u32[]{:S(2)}) collective-permute-start(bf16[128,512]{1,0:T(8,128)(2,1)S(1)} %get-tuple-element.66), channel_id=1, source_target_pairs={{0,16},{4,20},{8,24},{12,28},{16,0},{20,4},{24,8},{28,12},{1,17},{... | collective-permute-start | bytes 393224 | tf_op jit(solution)/shard_map/ppermute | solution.py:279
  23.7 1.6 %collective-permute-start.13 = (bf16[128,512]{1,0:T(8,128)(2,1)S(1)}, bf16[128,512]{1,0:T(8,128)(2,1)}, u32[]{:S(2)}, u32[]{:S(2)}) collective-permute-start(bf16[128,512]{1,0:T(8,128)(2,1)S(1)} %get-tuple-element.65), channel_id=1, source_target_pairs={{0,24},{4,28},{8,16},{12,20},{16,8},{20,12},{24,0},{28,4},{1,25},{... | collective-permute-start | bytes 393224 | tf_op jit(solution)/shard_map/ppermute | solution.py:279
  25.2 1.6 %collective-permute-done.5.far_ref = bf16[784,128]{1,0:T(8,128)(2,1)S(1)} collective-permute-done((bf16[784,128]{1,0:T(8,128)(2,1)S(1)}, bf16[784,128]{1,0:T(8,128)(2,1)S(1)}, u32[]{:S(2)}, u32[]{:S(2)}) %collective-permute-start.5) | collective-permute-done | bytes 200736 | tf_op jit(solution)/shard_map/ppermute | solution.py:274
  26.9 5.3 %solve.1 = (bf16[128,512]{1,0:T(8,128)(2,1)S(1)}, bf16[128,512]{1,0:T(8,128)(2,1)}, bf16[128,512]{1,0:T(8,128)(2,1)S(1)}, bf16[784,128]{1,0:T(8,128)(2,1)S(1)}) custom-call(f32[4]{0:T(128)S(1)} %copy-done.7, s32[1,128]{1,0:T(1,128)S(1)} %bitcast.13, bf16[128,512]{1,0:T(8,128)(2,1)S(1)} %copy-done.2, bf16[128,512]{1,0:T(8,128)(2,1)S(1)} %copy-done.4, ...), custom_call_target="tpu_custom_call" | custom-call | flops 5000000000 | bytes 1520144 | tf_op jit(solution)/shard_map/solve/pallas_call | solution.py:38
  32.1 2.9 %collective-permute-start.9 = (bf16[784,128]{1,0:T(8,128)(2,1)S(1)}, bf16[784,128]{1,0:T(8,128)(2,1)S(1)}, u32[]{:S(2)}, u32[]{:S(2)}) collective-permute-start(bf16[784,128]{1,0:T(8,128)(2,1)S(1)} %get-tuple-element.48), channel_id=1, source_target_pairs={{0,28},{4,0},{8,4},{12,8},{16,12},{20,16},{24,20},{28,24},{1,29},{... | collective-permute-start | bytes 602120 | tf_op jit(solution)/shard_map/ppermute | solution.py:274
  35.0 0.4 collective-permute-done.12
  35.5 9.3 %collective-permute-start.14 = (bf16[128,512]{1,0:T(8,128)(2,1)S(1)}, bf16[128,512]{1,0:T(8,128)(2,1)S(1)}, u32[]{:S(2)}, u32[]{:S(2)}) collective-permute-start(bf16[128,512]{1,0:T(8,128)(2,1)S(1)} %get-tuple-element.62.mixed_ref), channel_id=1, source_target_pairs={{0,8},{4,12},{8,0},{12,4},{16,24},{20,28},{24,16},{28,20},{1,9},{5... | collective-permute-start | bytes 393224 | tf_op jit(solution)/shard_map/ppermute | solution.py:279
  44.8 2.0 %collective-permute-start.15 = (bf16[128,512]{1,0:T(8,128)(2,1)S(1)}, bf16[128,512]{1,0:T(8,128)(2,1)S(1)}, u32[]{:S(2)}, u32[]{:S(2)}) collective-permute-start(bf16[128,512]{1,0:T(8,128)(2,1)S(1)} %get-tuple-element.62.mixed_ref), channel_id=1, source_target_pairs={{0,16},{4,20},{8,24},{12,28},{16,0},{20,4},{24,8},{28,12},{1,17},{... | collective-permute-start | bytes 393224 | tf_op jit(solution)/shard_map/ppermute | solution.py:279
  46.8 1.0 %project.1 = (f32[128,512]{1,0:T(8,128)S(1)}, bf16[128,512]{1,0:T(8,128)(2,1)S(1)}, bf16[128,512]{1,0:T(8,128)(2,1)S(1)}, bf16[128,512]{1,0:T(8,128)(2,1)S(1)}) custom-call(s32[2]{0:T(128)S(1)} %pad_add_fusion.place_ref, bf16[128,512]{1,0:T(8,128)(2,1)S(1)} %get-tuple-element.62.mixed_ref, bf16[512,2048]{1,0:T(8,128)(2,1)S(1)} %copy-done), custom_call_target="tpu_custom_call" | custom-call | flops 1000000000 | bytes 2883592 | tf_op jit(solution)/shard_map/project/pallas_call | solution.py:38
  47.9 0.0 copy-start.13
  47.9 0.3 collective-permute-start.8
  48.1 1.1 %local_grads.1 = (f32[128,512]{1,0:T(8,128)S(1)}, f32[128,512]{1,0:T(8,128)S(1)}) custom-call(s32[1,128]{1,0:T(1,128)S(1)} %bitcast.14, bf16[128,512]{1,0:T(8,128)(2,1)S(1)} %copy-done.4, bf16[128,512]{1,0:T(8,128)(2,1)S(1)} %copy-done.6, bf16[128,512]{1,0:T(8,128)(2,1)S(1)} %get-tuple-element.39.cot_ref, bf16[128,512]{1,0:T(8,128)(2,1)S(1)} %get-tuple-element.53.sol_ref, ...), custom_call_target="tpu_custom_call" | custom-call | flops 1100000000 | bytes 1180160 | tf_op jit(solution)/shard_map/local_grads/pallas_call | solution.py:38
  49.2 1.4 %collective-permute-start.7 = (bf16[128,512]{1,0:T(8,128)(2,1)S(1)}, bf16[128,512]{1,0:T(8,128)(2,1)S(1)}, u32[]{:S(2)}, u32[]{:S(2)}) collective-permute-start(bf16[128,512]{1,0:T(8,128)(2,1)S(1)} %get-tuple-element.45), channel_id=1, source_target_pairs={{0,2},{1,3},{2,0},{3,1},{4,6},{5,7},{6,4},{7,5},{8,10},{9,11},{10,... | collective-permute-start | bytes 393224 | tf_op jit(solution)/shard_map/ppermute | solution.py:279
  50.7 1.3 %collective-permute-done.15 = bf16[128,512]{1,0:T(8,128)(2,1)S(1)} collective-permute-done((bf16[128,512]{1,0:T(8,128)(2,1)S(1)}, bf16[128,512]{1,0:T(8,128)(2,1)S(1)}, u32[]{:S(2)}, u32[]{:S(2)}) %collective-permute-start.15) | collective-permute-done | bytes 131104 | tf_op jit(solution)/shard_map/ppermute | solution.py:279
  51.9 2.6 %collective-permute-start.17 = (bf16[128,512]{1,0:T(8,128)(2,1)S(1)}, bf16[128,512]{1,0:T(8,128)(2,1)S(1)}, u32[]{:S(2)}, u32[]{:S(2)}) collective-permute-start(bf16[128,512]{1,0:T(8,128)(2,1)S(1)} %collective-permute-done.15), channel_id=1, source_target_pairs={{0,8},{4,12},{8,0},{12,4},{16,24},{20,28},{24,16},{28,20},{1,9},{5... | collective-permute-start | bytes 393224 | tf_op jit(solution)/shard_map/ppermute | solution.py:279
  54.5 0.7 compare_bitcast_fusion
  55.2 1.1 %fusion.16.near_ref = bf16[784,128]{1,0:T(8,128)(2,1)S(1)} fusion(bf16[784,128]{1,0:T(8,128)(2,1)} %collective-permute-done.10, bf16[784,128]{1,0:T(8,128)(2,1)S(1)} %collective-permute-done.9, pred[128]{0:T(512)(128)(4,1)S(1)} %compare_bitcast_fusion, pred[784]{0:T(1024)(128)(4,1)S(1)} %copy-done.13), kind=kLoop, calls=%fused_computation.20 | loop fusion | flops 602112 | bytes 603024 | tf_op jit(solution)/shard_map/convert_element_type | solution.py:287
  56.3 2.0 %collective-permute-start.16 = (bf16[784,128]{1,0:T(8,128)(2,1)S(1)}, bf16[784,128]{1,0:T(8,128)(2,1)S(1)}, u32[]{:S(2)}, u32[]{:S(2)}) collective-permute-start(bf16[784,128]{1,0:T(8,128)(2,1)S(1)} %fusion.16.near_ref), channel_id=1, source_target_pairs={{0,24},{4,28},{8,0},{12,4},{16,8},{20,12},{24,16},{28,20},{1,25},{... | collective-permute-start | bytes 602120 | tf_op jit(solution)/shard_map/ppermute | solution.py:274
  58.3 0.3 collective-permute-done.17
  58.6 1.5 %fusion = f32[512,512]{1,0:T(8,128)S(1)} fusion(bf16[128,512]{1,0:T(8,128)(2,1)} %collective-permute-done.13, bf16[128,512]{1,0:T(8,128)(2,1)} %collective-permute-done.12, bf16[128,512]{1,0:T(8,128)(2,1)} %collective-permute-done.11, bf16[128,512]{1,0:T(8,128)(2,1)S(1)} %copy-done.11, bf16[128,512]{1,0:T(8,128)(2,1)S(1)} %collective-permute-done.17, ...), kind=kOutput, calls=%fused_computation.2 | convolution fusion | flops 272629760 | bytes 2097152 | tf_op jit(solution)/shard_map/dot_general | solution.py:374
  60.2 0.1 collective-permute-start.18
  60.3 0.7 %add_convert_fusion = bf16[128,512]{1,0:T(8,128)(2,1)} fusion(bf16[128,512]{1,0:T(8,128)(2,1)S(1)} %collective-permute-done.8, bf16[128,512]{1,0:T(8,128)(2,1)S(1)} %collective-permute-done.7, f32[128,512]{1,0:T(8,128)S(1)} %get-tuple-element.43, bf16[128,512]{1,0:T(8,128)(2,1)S(1)} %collective-permute-done.6), kind=kLoop, calls=%fused_computation.22 | loop fusion | flops 458752 | bytes 786432 | tf_op jit(solution)/shard_map/convert_element_type | solution.py:354
  61.0 2.4 %collective-permute-done.16.far_ref = bf16[784,128]{1,0:T(8,128)(2,1)S(1)} collective-permute-done((bf16[784,128]{1,0:T(8,128)(2,1)S(1)}, bf16[784,128]{1,0:T(8,128)(2,1)S(1)}, u32[]{:S(2)}, u32[]{:S(2)}) %collective-permute-start.16) | collective-permute-done | bytes 200736 | tf_op jit(solution)/shard_map/ppermute | solution.py:274
  63.4 1.0 %final_grads.1 = (bf16[128,512]{1,0:T(8,128)(2,1)}, bf16[128,512]{1,0:T(8,128)(2,1)}) custom-call(s32[1,128]{1,0:T(1,128)S(1)} %bitcast.15, bf16[128,512]{1,0:T(8,128)(2,1)S(1)} %copy-done.4, bf16[128,512]{1,0:T(8,128)(2,1)S(1)} %copy-done.6, bf16[784,128]{1,0:T(8,128)(2,1)S(1)} %fusion.16.near_ref, bf16[784,128]{1,0:T(8,128)(2,1)S(1)} %collective-permute-done.16.far_ref, ...), custom_call_target="tpu_custom_call" | custom-call | flops 1000000000 | bytes 1450496 | tf_op jit(solution)/shard_map/final_grads/pallas_call | solution.py:38
  64.5 3.9 %collective-permute-done.18 = bf16[256,512]{1,0:T(8,128)(2,1)S(1)} collective-permute-done((bf16[256,512]{1,0:T(8,128)(2,1)S(1)}, bf16[256,512]{1,0:T(8,128)(2,1)S(1)}, u32[]{:S(2)}, u32[]{:S(2)}) %collective-permute-start.18) | collective-permute-done | bytes 262176 | tf_op jit(solution)/shard_map/ppermute | solution.py:279
  68.3 0.9 %bitcast_add_fusion = f32[256,512]{1,0:T(8,128)} fusion(bf16[256,512]{1,0:T(8,128)(2,1)S(1)} %collective-permute-done.18, f32[2,256,512]{2,1,0:T(8,128)S(1)} %bitcast.17, s32[]{:T(128)S(6)} %select_n.47), kind=kLoop, calls=%fused_computation.17 | loop fusion | flops 262144 | bytes 1310724 | tf_op jit(solution)/shard_map/add | solution.py:383
  (35 shorter events, 0.1 us)
Async XLA Ops:
  0.6 18.1 %copy-start.1 = (bf16[128,512]{1,0:T(8,128)(2,1)S(1)}, bf16[128,512]{1,0:T(8,128)(2,1)}, u32[]{:S(2)}) copy-start(bf16[128,512]{1,0:T(8,128)(2,1)} %refs_0_) | copy-start | bytes 393220
  0.6 18.1 %copy-start = (bf16[512,2048]{1,0:T(8,128)(2,1)S(1)}, bf16[512,2048]{1,0:T(8,128)(2,1)}, u32[]{:S(2)}) copy-start(bf16[512,2048]{1,0:T(8,128)(2,1)} %weight_ref.1) | copy-start | bytes 6291460
  0.7 1.1 %copy-start.3 = (bf16[128,512]{1,0:T(8,128)(2,1)S(1)}, bf16[128,512]{1,0:T(8,128)(2,1)}, u32[]{:S(2)}) copy-start(bf16[128,512]{1,0:T(8,128)(2,1)} %key_ref.7) | copy-start | bytes 393220
  1.7 0.9 %copy-start.5 = (bf16[128,512]{1,0:T(8,128)(2,1)S(1)}, bf16[128,512]{1,0:T(8,128)(2,1)}, u32[]{:S(2)}) copy-start(bf16[128,512]{1,0:T(8,128)(2,1)} %value_ref.7) | copy-start | bytes 393220
  2.6 0.7 copy-start.8
  3.7 13.1 %collective-permute-start = (bf16[784,128]{1,0:T(8,128)(2,1)S(1)}, bf16[784,128]{1,0:T(8,128)(2,1)S(1)}, u32[]{:S(2)}, u32[]{:S(2)}) collective-permute-start(bf16[784,128]{1,0:T(8,128)(2,1)S(1)} %tail_states.1), channel_id=1, source_target_pairs={{0,4},{4,8},{8,12},{12,16},{16,20},{20,24},{24,28},{28,0},{1,5},{5... | collective-permute-start | bytes 602120 | tf_op jit(solution)/shard_map/ppermute | solution.py:274
  6.7 10.1 %collective-permute-start.1 = (bf16[784,128]{1,0:T(8,128)(2,1)S(1)}, bf16[784,128]{1,0:T(8,128)(2,1)S(1)}, u32[]{:S(2)}, u32[]{:S(2)}) collective-permute-start(bf16[784,128]{1,0:T(8,128)(2,1)S(1)} %tail_states.1), channel_id=1, source_target_pairs={{0,8},{4,12},{8,16},{12,20},{16,24},{20,28},{24,0},{28,4},{1,9},{5... | collective-permute-start | bytes 602120 | tf_op jit(solution)/shard_map/ppermute | solution.py:274
  8.3 1.9 %collective-permute-start.2 = (bf16[128,512]{1,0:T(8,128)(2,1)}, bf16[128,512]{1,0:T(8,128)(2,1)S(1)}, u32[]{:S(2)}, u32[]{:S(2)}) collective-permute-start(bf16[128,512]{1,0:T(8,128)(2,1)} %refs_0_), channel_id=1, source_target_pairs={{0,1},{1,0},{2,3},{3,2},{4,5},{5,4},{6,7},{7,6},{8,9},{9,8},{10,11... | collective-permute-start | bytes 393224 | tf_op jit(solution)/shard_map/ppermute | solution.py:279
  8.3 6.5 %collective-permute-start.3 = (bf16[128,512]{1,0:T(8,128)(2,1)}, bf16[128,512]{1,0:T(8,128)(2,1)S(1)}, u32[]{:S(2)}, u32[]{:S(2)}) collective-permute-start(bf16[128,512]{1,0:T(8,128)(2,1)} %refs_0_), channel_id=1, source_target_pairs={{0,2},{1,3},{2,0},{3,1},{4,6},{5,7},{6,4},{7,5},{8,10},{9,11},{10,... | collective-permute-start | bytes 393224 | tf_op jit(solution)/shard_map/ppermute | solution.py:279
  9.8 7.0 %collective-permute-start.4 = (bf16[128,512]{1,0:T(8,128)(2,1)}, bf16[128,512]{1,0:T(8,128)(2,1)S(1)}, u32[]{:S(2)}, u32[]{:S(2)}) collective-permute-start(bf16[128,512]{1,0:T(8,128)(2,1)} %refs_0_), channel_id=1, source_target_pairs={{0,3},{1,2},{2,1},{3,0},{4,7},{5,6},{6,5},{7,4},{8,11},{9,10},{10,... | collective-permute-start | bytes 393224 | tf_op jit(solution)/shard_map/ppermute | solution.py:279
  10.2 6.6 %copy-start.12 = (pred[784]{0:T(1024)(128)(4,1)}, pred[784]{0:T(1024)(128)(4,1)S(1)}, u32[]{:S(2)}) copy-start(pred[784]{0:T(1024)(128)(4,1)S(1)} %iota_compare_fusion) | copy-start | bytes 2356
  17.0 9.8 %copy-start.2 = (bf16[128,512]{1,0:T(8,128)(2,1)S(1)}, bf16[128,512]{1,0:T(8,128)(2,1)}, u32[]{:S(2)}) copy-start(bf16[128,512]{1,0:T(8,128)(2,1)} %query_ref.1) | copy-start | bytes 393220
  17.1 9.8 %copy-start.4 = (bf16[128,512]{1,0:T(8,128)(2,1)S(1)}, bf16[128,512]{1,0:T(8,128)(2,1)}, u32[]{:S(2)}) copy-start(bf16[128,512]{1,0:T(8,128)(2,1)} %key_ref.7) | copy-start | bytes 393220
  17.1 9.8 %copy-start.6 = (bf16[128,512]{1,0:T(8,128)(2,1)S(1)}, bf16[128,512]{1,0:T(8,128)(2,1)}, u32[]{:S(2)}) copy-start(bf16[128,512]{1,0:T(8,128)(2,1)} %value_ref.7) | copy-start | bytes 393220
  17.1 9.8 %copy-start.7 = (f32[4]{0:T(128)S(1)}, f32[4]{0:T(128)}, u32[]{:S(2)}) copy-start(f32[4]{0:T(128)} %ridge_ref.1) | copy-start | bytes 52
  17.1 9.8 %copy-start.9 = (s32[128]{0:T(128)S(1)}, s32[128]{0:T(128)}, u32[]{:S(2)}) copy-start(s32[128]{0:T(128)} %param.13) | copy-start | bytes 1540
  17.1 9.7 %collective-permute-start.5 = (bf16[784,128]{1,0:T(8,128)(2,1)S(1)}, bf16[784,128]{1,0:T(8,128)(2,1)S(1)}, u32[]{:S(2)}, u32[]{:S(2)}) collective-permute-start(bf16[784,128]{1,0:T(8,128)(2,1)S(1)} %fusion.15.near_ref), channel_id=1, source_target_pairs={{0,8},{4,12},{8,16},{12,20},{16,24},{20,28},{24,0},{28,4},{1,9},{5... | collective-permute-start | bytes 602120 | tf_op jit(solution)/shard_map/ppermute | solution.py:274
  20.9 14.2 %collective-permute-start.11 = (bf16[128,512]{1,0:T(8,128)(2,1)}, bf16[128,512]{1,0:T(8,128)(2,1)}, u32[]{:S(2)}, u32[]{:S(2)}) collective-permute-start(bf16[128,512]{1,0:T(8,128)(2,1)} %get-tuple-element.67), channel_id=1, source_target_pairs={{0,8},{4,12},{8,0},{12,4},{16,24},{20,28},{24,16},{28,20},{1,9},{5... | collective-permute-start | bytes 393224 | tf_op jit(solution)/shard_map/ppermute | solution.py:279
  22.4 13.0 %collective-permute-start.12 = (bf16[128,512]{1,0:T(8,128)(2,1)S(1)}, bf16[128,512]{1,0:T(8,128)(2,1)}, u32[]{:S(2)}, u32[]{:S(2)}) collective-permute-start(bf16[128,512]{1,0:T(8,128)(2,1)S(1)} %get-tuple-element.66), channel_id=1, source_target_pairs={{0,16},{4,20},{8,24},{12,28},{16,0},{20,4},{24,8},{28,12},{1,17},{... | collective-permute-start | bytes 393224 | tf_op jit(solution)/shard_map/ppermute | solution.py:279
  23.7 11.8 %collective-permute-start.13 = (bf16[128,512]{1,0:T(8,128)(2,1)S(1)}, bf16[128,512]{1,0:T(8,128)(2,1)}, u32[]{:S(2)}, u32[]{:S(2)}) collective-permute-start(bf16[128,512]{1,0:T(8,128)(2,1)S(1)} %get-tuple-element.65), channel_id=1, source_target_pairs={{0,24},{4,28},{8,16},{12,20},{16,8},{20,12},{24,0},{28,4},{1,25},{... | collective-permute-start | bytes 393224 | tf_op jit(solution)/shard_map/ppermute | solution.py:279
  32.1 16.0 %copy-start.10 = (bf16[128,512]{1,0:T(8,128)(2,1)S(1)}, bf16[128,512]{1,0:T(8,128)(2,1)}, u32[]{:S(2)}) copy-start(bf16[128,512]{1,0:T(8,128)(2,1)} %get-tuple-element.31.dual_ref) | copy-start | bytes 393220
  32.1 19.8 %collective-permute-start.9 = (bf16[784,128]{1,0:T(8,128)(2,1)S(1)}, bf16[784,128]{1,0:T(8,128)(2,1)S(1)}, u32[]{:S(2)}, u32[]{:S(2)}) collective-permute-start(bf16[784,128]{1,0:T(8,128)(2,1)S(1)} %get-tuple-element.48), channel_id=1, source_target_pairs={{0,28},{4,0},{8,4},{12,8},{16,12},{20,16},{24,20},{28,24},{1,29},{... | collective-permute-start | bytes 602120 | tf_op jit(solution)/shard_map/ppermute | solution.py:274
  35.0 16.9 %collective-permute-start.10 = (bf16[784,128]{1,0:T(8,128)(2,1)S(1)}, bf16[784,128]{1,0:T(8,128)(2,1)}, u32[]{:S(2)}, u32[]{:S(2)}) collective-permute-start(bf16[784,128]{1,0:T(8,128)(2,1)S(1)} %get-tuple-element.48), channel_id=1, source_target_pairs={{0,24},{4,28},{8,0},{12,4},{16,8},{20,12},{24,16},{28,20},{1,25},{... | collective-permute-start | bytes 602120 | tf_op jit(solution)/shard_map/ppermute | solution.py:274
  35.5 13.8 %collective-permute-start.14 = (bf16[128,512]{1,0:T(8,128)(2,1)S(1)}, bf16[128,512]{1,0:T(8,128)(2,1)S(1)}, u32[]{:S(2)}, u32[]{:S(2)}) collective-permute-start(bf16[128,512]{1,0:T(8,128)(2,1)S(1)} %get-tuple-element.62.mixed_ref), channel_id=1, source_target_pairs={{0,8},{4,12},{8,0},{12,4},{16,24},{20,28},{24,16},{28,20},{1,9},{5... | collective-permute-start | bytes 393224 | tf_op jit(solution)/shard_map/ppermute | solution.py:279
  44.8 7.1 %collective-permute-start.15 = (bf16[128,512]{1,0:T(8,128)(2,1)S(1)}, bf16[128,512]{1,0:T(8,128)(2,1)S(1)}, u32[]{:S(2)}, u32[]{:S(2)}) collective-permute-start(bf16[128,512]{1,0:T(8,128)(2,1)S(1)} %get-tuple-element.62.mixed_ref), channel_id=1, source_target_pairs={{0,16},{4,20},{8,24},{12,28},{16,0},{20,4},{24,8},{28,12},{1,17},{... | collective-permute-start | bytes 393224 | tf_op jit(solution)/shard_map/ppermute | solution.py:279
  47.9 7.3 %copy-start.13 = (pred[784]{0:T(1024)(128)(4,1)S(1)}, pred[784]{0:T(1024)(128)(4,1)}, u32[]{:S(2)}) copy-start(pred[784]{0:T(1024)(128)(4,1)} %copy-done.12) | copy-start | bytes 2356
  47.9 12.4 %collective-permute-start.8 = (bf16[128,512]{1,0:T(8,128)(2,1)S(1)}, bf16[128,512]{1,0:T(8,128)(2,1)S(1)}, u32[]{:S(2)}, u32[]{:S(2)}) collective-permute-start(bf16[128,512]{1,0:T(8,128)(2,1)S(1)} %get-tuple-element.46), channel_id=1, source_target_pairs={{0,3},{1,2},{2,1},{3,0},{4,7},{5,6},{6,5},{7,4},{8,11},{9,10},{10,... | collective-permute-start | bytes 393224 | tf_op jit(solution)/shard_map/ppermute | solution.py:279
  48.1 10.5 %copy-start.11 = (bf16[128,512]{1,0:T(8,128)(2,1)S(1)}, bf16[128,512]{1,0:T(8,128)(2,1)}, u32[]{:S(2)}) copy-start(bf16[128,512]{1,0:T(8,128)(2,1)} %get-tuple-element.58) | copy-start | bytes 393220
  49.2 11.0 %collective-permute-start.7 = (bf16[128,512]{1,0:T(8,128)(2,1)S(1)}, bf16[128,512]{1,0:T(8,128)(2,1)S(1)}, u32[]{:S(2)}, u32[]{:S(2)}) collective-permute-start(bf16[128,512]{1,0:T(8,128)(2,1)S(1)} %get-tuple-element.45), channel_id=1, source_target_pairs={{0,2},{1,3},{2,0},{3,1},{4,6},{5,7},{6,4},{7,5},{8,10},{9,11},{10,... | collective-permute-start | bytes 393224 | tf_op jit(solution)/shard_map/ppermute | solution.py:279
  51.9 8.3 %collective-permute-start.6 = (bf16[128,512]{1,0:T(8,128)(2,1)S(1)}, bf16[128,512]{1,0:T(8,128)(2,1)S(1)}, u32[]{:S(2)}, u32[]{:S(2)}) collective-permute-start(bf16[128,512]{1,0:T(8,128)(2,1)S(1)} %get-tuple-element.44), channel_id=1, source_target_pairs={{0,1},{1,0},{2,3},{3,2},{4,5},{5,4},{6,7},{7,6},{8,9},{9,8},{10,11... | collective-permute-start | bytes 393224 | tf_op jit(solution)/shard_map/ppermute | solution.py:279
  51.9 6.7 %collective-permute-start.17 = (bf16[128,512]{1,0:T(8,128)(2,1)S(1)}, bf16[128,512]{1,0:T(8,128)(2,1)S(1)}, u32[]{:S(2)}, u32[]{:S(2)}) collective-permute-start(bf16[128,512]{1,0:T(8,128)(2,1)S(1)} %collective-permute-done.15), channel_id=1, source_target_pairs={{0,8},{4,12},{8,0},{12,4},{16,24},{20,28},{24,16},{28,20},{1,9},{5... | collective-permute-start | bytes 393224 | tf_op jit(solution)/shard_map/ppermute | solution.py:279
  56.3 7.1 %collective-permute-start.16 = (bf16[784,128]{1,0:T(8,128)(2,1)S(1)}, bf16[784,128]{1,0:T(8,128)(2,1)S(1)}, u32[]{:S(2)}, u32[]{:S(2)}) collective-permute-start(bf16[784,128]{1,0:T(8,128)(2,1)S(1)} %fusion.16.near_ref), channel_id=1, source_target_pairs={{0,24},{4,28},{8,0},{12,4},{16,8},{20,12},{24,16},{28,20},{1,25},{... | collective-permute-start | bytes 602120 | tf_op jit(solution)/shard_map/ppermute | solution.py:274
  60.2 8.1 %collective-permute-start.18 = (bf16[256,512]{1,0:T(8,128)(2,1)S(1)}, bf16[256,512]{1,0:T(8,128)(2,1)S(1)}, u32[]{:S(2)}, u32[]{:S(2)}) collective-permute-start(bf16[256,512]{1,0:T(8,128)(2,1)S(1)} %fusion.17), channel_id=1, source_target_pairs={{0,4},{4,0},{8,12},{12,8},{16,20},{20,16},{24,28},{28,24},{1,5},{5... | collective-permute-start | bytes 786440 | tf_op jit(solution)/shard_map/ppermute | solution.py:279

commit v3 on v2

v3 whole, which is shorter than its diff:
```python
import functools

import jax
import jax.numpy as jnp
from jax import lax
from jax.experimental import pallas as pl
from jax.experimental.pallas import tpu as pltpu
from jax.sharding import PartitionSpec as P

CG_STEPS = 4
EPSILON = 1e-06
LABEL_ROWS = 16
F32 = jnp.float32
BF16 = jnp.bfloat16
VMEM_LIMIT = 48 * 1024 * 1024
FLOPS_PER_US = 1e9
COT_US = 1.5
FINAL_US = 1.0
PAIR_JOIN_US = 5.0
MINE_US = 6.0


def mm(a, b):
    return lax.dot_general(a, b, (((1,), (0,)), ((), ())), preferred_element_type=F32)


def mm_nt(a, b):
    return lax.dot_general(a, b, (((1,), (1,)), ((), ())), preferred_element_type=F32)


def mm_tn(a, b):
    return lax.dot_general(a, b, (((0,), (0,)), ((), ())), preferred_element_type=F32)


def kernel_call(body, out_shape, operands, microseconds, name, smem=(), scratch=()):
    nbytes = sum(o.size * o.dtype.itemsize for o in operands)
    nbytes += sum(o.size * o.dtype.itemsize for o in out_shape)
    return pl.pallas_call(
        body,
        out_shape=out_shape,
        in_specs=[
            pl.BlockSpec(memory_space=pltpu.SMEM if i in smem else pltpu.VMEM)
            for i in range(len(operands))
        ],
        out_specs=[pl.BlockSpec(memory_space=pltpu.VMEM)] * len(out_shape),
        scratch_shapes=scratch,
        compiler_params=pltpu.CompilerParams(vmem_limit_bytes=VMEM_LIMIT),
        cost_estimate=pl.CostEstimate(
            flops=int(microseconds * FLOPS_PER_US), bytes_accessed=nbytes, transcendentals=0
        ),
        name=name,
    )(*operands)


def label_grids(rows_ref):
    piece = rows_ref.shape[0] - LABEL_ROWS
    labels = rows_ref[piece : piece + LABEL_ROWS, :piece].astype(F32)[0:1, :]
    across = jnp.broadcast_to(labels, (piece, piece))
    return piece, across, across.T


def document_mask(across, down):
    row = lax.broadcasted_iota(jnp.int32, across.shape, 0)
    col = lax.broadcasted_iota(jnp.int32, across.shape, 1)
    return (across == down) & (col <= row)


def triangle(width):
    row = lax.broadcasted_iota(jnp.int32, (width, width), 0)
    col = lax.broadcasted_iota(jnp.int32, (width, width), 1)
    return col < row, col == row


def unit_rows(width):
    return 3 * width + LABEL_ROWS


def pack_states(out_ref, label, full, symmetric):
    width = full[0].shape[0]
    below, diagonal = triangle(width)
    for unit in range(len(full) // 2):
        base = unit * unit_rows(width)
        for i in range(2):
            rows = slice(base + i * width, base + (i + 1) * width)
            out_ref[rows, :] = full[2 * unit + i].astype(BF16)
        one, two = symmetric[2 * unit], symmetric[2 * unit + 1]
        square = jnp.where(below | diagonal, one, two)
        out_ref[base + 2 * width : base + 3 * width, :] = square.astype(BF16)
        second = jnp.sum(jnp.where(diagonal, two, 0.0), axis=0, keepdims=True)
        rest = jnp.broadcast_to(label, (LABEL_ROWS - 1, width))
        out_ref[base + 3 * width : base + unit_rows(width), :] = jnp.concatenate(
            [second, rest], axis=0
        ).astype(BF16)


def join_units(near, far, width):
    total = near.astype(F32)
    tail = slice(near.shape[0] - LABEL_ROWS, near.shape[0])
    near_label, far_label = near[tail].astype(F32), far[tail].astype(F32)
    joined = (near_label[LABEL_ROWS - 1 :] == far_label[LABEL_ROWS - 1 :]).astype(F32)
    total = total + joined * far.astype(F32)
    row = lax.rem(lax.broadcasted_iota(jnp.int32, near.shape, 0), unit_rows(width))
    return jnp.where(row <= 3 * width, total, near.astype(F32))


def unpack_symmetric(square, row):
    below, diagonal = triangle(square.shape[0])
    flipped = square.T
    one = jnp.where(below | diagonal, square, flipped)
    two = jnp.where(diagonal, row, jnp.where(below, flipped, square))
    return one, two


def unpack_states(units, heads, width):
    size = unit_rows(width)
    label = units[size - 1 : size, :]
    full, symmetric = [], []
    for unit in range(heads // 2):
        part = units[unit * size : (unit + 1) * size, :]
        full += [part[:width].astype(BF16), part[width : 2 * width].astype(BF16)]
        square = part[2 * width : 3 * width]
        symmetric += [
            m.astype(BF16) for m in unpack_symmetric(square, part[3 * width : 3 * width + 1])
        ]
    return label, full, symmetric


def head_rows_of(rows_ref, heads, width, part, h):
    start = (part * heads + h) * width
    return rows_ref[: rows_ref.shape[0] - LABEL_ROWS, start : start + width]


def tail_body(heads, width, rows_ref, out_ref):
    piece, across, down = label_grids(rows_ref)
    last = jnp.max(across, axis=1, keepdims=True)
    tail = (down == last).astype(F32).astype(BF16)
    sums, grams = [], []
    for h in range(heads):
        key_h = head_rows_of(rows_ref, heads, width, 0, h)
        value_h = head_rows_of(rows_ref, heads, width, 1, h)
        masked = key_h * tail[:, :width]
        grams.append(mm_tn(key_h, masked))
        sums.append(mm_tn(value_h, masked))
    pack_states(out_ref, last[:1] + 1, sums, grams)


def cot_body(count, shard, place_ref, *refs):
    cots, weight_ref, cot_ref = refs[:count], refs[count], refs[count + 1]
    me = place_ref[1]
    total = None
    for b in range(count):
        owner = jnp.bitwise_xor(me, b)
        cols = pl.ds(pl.multiple_of(owner * shard, shard), shard)
        part = mm_nt(cots[b][...], weight_ref[:, cols])
        total = part if total is None else total + part
    cot_ref[...] = total.astype(BF16)


def project_body(count, shard, place_ref, mixed_ref, weight_ref, turned_ref, keep_ref, send_ref):
    piece = mixed_ref.shape[0]
    me = place_ref[1]
    mixed = mixed_ref[...]
    for c in range(count):
        owner = jnp.bitwise_xor(me, c)
        cols = pl.ds(pl.multiple_of(owner * shard, shard), shard)
        part = mm(mixed, weight_ref[:, cols])
        rows = slice(c // 2 * piece, (c // 2 + 1) * piece)
        if c % 2:
            send_ref[rows, :] = part.astype(BF16)
        else:
            keep_ref[rows, :] = part
    send_ref[count // 2 * piece :, :] = turned_ref[...]


def halve_body(blocks, piece, keep_ref, got_ref, turned_ref, rest_ref, send_ref):
    for c in range(blocks):
        rows = slice(c * piece, (c + 1) * piece)
        target = slice(c // 2 * piece, (c // 2 + 1) * piece)
        total = keep_ref[rows, :] + got_ref[rows, :].astype(F32)
        if c % 2:
            send_ref[target, :] = total.astype(BF16)
        else:
            rest_ref[target, :] = total
    sent, gathered = blocks // 2 * piece, turned_ref.shape[0]
    send_ref[sent : sent + gathered, :] = turned_ref[...]
    send_ref[sent + gathered :, :] = got_ref[blocks * piece :, :]


def join_body(width, near_ref, far_ref, *refs):
    out_ref = refs[-1]
    out_ref[...] = join_units(near_ref[...], far_ref[...], width).astype(BF16)


def pair_join_body(width, place_ref, here_ref, there_ref, out_ref, both_ref):
    half = out_ref.shape[0]
    odd = lax.rem(place_ref[0], 2)
    mine = pl.ds(pl.multiple_of(odd * half, LABEL_ROWS), half)
    both_ref[pl.ds(pl.multiple_of(odd * half, LABEL_ROWS), half), :] = here_ref[mine, :]
    both_ref[pl.ds(pl.multiple_of((1 - odd) * half, LABEL_ROWS), half), :] = there_ref[mine, :]
    total = join_units(both_ref[:half, :], both_ref[half:, :], width)
    out_ref[...] = total.astype(BF16)


def pair_grad_body(piece, parts, arrays, by_place, place_ref, *refs):
    count = len(parts)
    cots, mixes = refs[:arrays], refs[arrays : arrays + count]
    kept_ref, given_ref, cot_ref, mix_ref, total_ref = refs[arrays + count :]
    for i, (array, row) in enumerate(parts):
        cot_at = jnp.bitwise_xor(place_ref[1], i) if by_place else i
        mix_at = jnp.bitwise_xor(lax.div(place_ref[0], 2), i) if by_place else i
        cot = cots[array][row : row + piece, :]
        cot_ref[pl.ds(pl.multiple_of(cot_at * piece, piece), piece), :] = cot
        mix_ref[pl.ds(pl.multiple_of(mix_at * piece, piece), piece), :] = mixes[i][...]
    total_ref[...] = mm_tn(cot_ref[...], mix_ref[...])
    half = kept_ref.shape[0]
    odd = lax.rem(place_ref[0], 2)
    kept_ref[...] = total_ref[pl.ds(pl.multiple_of(odd * half, half), half), :]
    given_ref[...] = total_ref[pl.ds(pl.multiple_of((1 - odd) * half, half), half), :].astype(BF16)


def solve_body(
    heads,
    width,
    ridge_ref,
    rows_ref,
    cot_ref,
    near_ref,
    far_ref,
    sol_ref,
    dual_ref,
    mixed_ref,
    out_ref,
):
    piece, across, down = label_grids(rows_ref)
    same = document_mask(across, down).astype(F32)
    same_two = jnp.concatenate([same, same], axis=0)
    first = jnp.min(across, axis=1, keepdims=True)
    head_rows = (down == first)[:, :width].astype(F32)
    units = join_units(near_ref[...], far_ref[...], width)
    label, value_states, gram_states = unpack_states(units, heads, width)
    carried = ((down + 1)[:, :width] == label).astype(F32)
    carried_two = jnp.concatenate([carried, carried], axis=0)
    keys, rhs_keys, values, solutions, residuals, directions, squares = ([] for _ in range(7))
    for h in range(heads):
        cols = slice(h * width, (h + 1) * width)
        key_h = head_rows_of(rows_ref, heads, width, 0, h)
        value_h = head_rows_of(rows_ref, heads, width, 1, h)
        query_h = head_rows_of(rows_ref, heads, width, 2, h)
        cot_h = cot_ref[:, cols]
        both = mm(cot_h, jnp.concatenate([value_h.T, value_states[h]], axis=1))
        scores = (both[:, :piece] * same).astype(BF16)
        target = carried * both[:, piece:] + mm(scores, key_h)
        start = jnp.concatenate([query_h.astype(F32), target], axis=0)
        keys.append(key_h)
        values.append(value_h)
        rhs_keys.append(jnp.concatenate([key_h.T, gram_states[h]], axis=1))
        solutions.append(jnp.zeros_like(start))
        residuals.append(start)
        directions.append(start)
        squares.append(jnp.sum(start * start, axis=1, keepdims=True))
    for step in range(CG_STEPS):
        for h in range(heads):
            p = directions[h]
            both = mm(p.astype(BF16), rhs_keys[h])
            scores = (both[:, :piece] * same_two).astype(BF16)
            applied = carried_two * both[:, piece:] + mm(scores, keys[h]) + ridge_ref[h] * p
            size = squares[h] / (jnp.sum(p * applied, axis=1, keepdims=True) + EPSILON)
            solutions[h] = solutions[h] + size * p
            if step + 1 < CG_STEPS:
                residuals[h] = residuals[h] - size * applied
                new_sq = jnp.sum(residuals[h] * residuals[h], axis=1, keepdims=True)
                directions[h] = residuals[h] + new_sq / (squares[h] + EPSILON) * p
                squares[h] = new_sq
    sums, crosses = [], []
    for h in range(heads):
        cols = slice(h * width, (h + 1) * width)
        sol = solutions[h][:piece]
        sol_b = sol.astype(BF16)
        dual_b = solutions[h][piece:].astype(BF16)
        both = mm(sol_b, jnp.concatenate([rhs_keys[h][:, :piece], value_states[h].T], axis=1))
        scores = (both[:, :piece] * same).astype(BF16)
        output = carried * both[:, piece:] + mm(scores, values[h])
        mixed_ref[:, cols] = output.astype(BF16)
        sol_ref[:, cols] = sol_b
        dual_ref[:, cols] = dual_b
        masked = (head_rows * sol).astype(BF16)
        sums.append(mm_tn(cot_ref[:, cols], masked))
        cross = mm_tn(dual_b, masked)
        crosses.append(cross + cross.T)
    pack_states(out_ref, first[:1] + 1, sums, crosses)


def local_grads_body(
    heads, width, rows_ref, cot_ref, sol_ref, dual_ref, grad_k_ref, grad_v_ref
):
    piece, across, down = label_grids(rows_ref)
    same = document_mask(across, down).astype(F32)
    same_two = jnp.concatenate([same, same], axis=0)
    for h in range(heads):
        cols = slice(h * width, (h + 1) * width)
        key_h = head_rows_of(rows_ref, heads, width, 0, h)
        value_h = head_rows_of(rows_ref, heads, width, 1, h)
        cot_h = cot_ref[:, cols]
        sol, dual = sol_ref[:, cols], dual_ref[:, cols]
        score_two = (mm_nt(cot_h, value_h) * same).astype(BF16)
        pair = (mm_nt(jnp.concatenate([sol, dual], axis=0), key_h) * same_two).astype(BF16)
        score_one, score_three = pair[:piece], pair[piece:]
        grad_v_ref[:, cols] = mm_tn(score_one, cot_h)
        grad_k_ref[:, cols] = mm_tn(
            jnp.concatenate([score_two, -score_three, -score_one], axis=0),
            jnp.concatenate([sol, sol, dual], axis=0),
        )


def final_grads_body(
    heads,
    width,
    place_ref,
    rows_ref,
    there_ref,
    mine_ref,
    theirs_ref,
    local_k_ref,
    local_v_ref,
    grad_k_ref,
    grad_v_ref,
    later_ref,
):
    piece, _, down = label_grids(rows_ref)
    half = mine_ref.shape[0]
    odd = lax.rem(place_ref[0], 2)
    later_ref[pl.ds(pl.multiple_of(odd * half, LABEL_ROWS), half), :] = mine_ref[...]
    later_ref[pl.ds(pl.multiple_of((1 - odd) * half, LABEL_ROWS), half), :] = theirs_ref[...]
    units = jnp.where(
        odd == 1,
        later_ref[...].astype(F32),
        join_units(there_ref[...], later_ref[...], width),
    )
    label, grad_states, gram_grads = unpack_states(units, heads, width)
    later = ((down + 1)[:, :width] == label).astype(F32)
    for h in range(heads):
        cols = slice(h * width, (h + 1) * width)
        key_h = head_rows_of(rows_ref, heads, width, 0, h)
        value_h = head_rows_of(rows_ref, heads, width, 1, h)
        grad_state, gram_grad = grad_states[h], gram_grads[h]
        grad_v = local_v_ref[:, cols] + later * mm_nt(key_h, grad_state)
        grad_k = local_k_ref[:, cols] + later * (mm(value_h, grad_state) - mm(key_h, gram_grad))
        grad_v_ref[:, cols] = grad_v.astype(BF16)
        grad_k_ref[:, cols] = grad_k.astype(BF16)


def rotated(value, by):
    devices = lax.axis_size("seq")
    return lax.ppermute(value, "seq", [(i, (i + by) % devices) for i in range(devices)])


def swapped(value, axis, mask):
    devices = lax.axis_size(axis)
    return lax.ppermute(value, axis, [(i, i ^ mask) for i in range(devices)])


def joined_inputs(key_rows, value_rows, query_rows, doc_row):
    piece, features = key_rows.shape
    parts = (key_rows, value_rows, query_rows)
    width = len(parts) * features
    total = jnp.pad(
        doc_row.astype(BF16), ((piece, LABEL_ROWS - 1), (0, width - doc_row.shape[1]))
    )
    for i, part in enumerate(parts):
        total += jnp.pad(part, ((0, LABEL_ROWS), (i * features, width - (i + 1) * features)))
    return total


def join_states(near, far, width, *after):
    (joined,) = kernel_call(
        functools.partial(join_body, width),
        [jax.ShapeDtypeStruct(far.shape, BF16)],
        (near, far, *after),
        MINE_US if after else 0.5,
        "join_states",
    )
    return joined


def per_device(query_rows, key_rows, value_rows, ridge_reg, out_weight, out_grad, doc_ids):
    heads = ridge_reg.shape[0]
    piece, features = key_rows.shape
    width = features // heads
    seq_size, head_size = lax.axis_size("seq"), lax.axis_size("head")
    seq_at, head_at = lax.axis_index("seq"), lax.axis_index("head")
    place = jnp.stack([seq_at, head_at]).astype(jnp.int32)
    model = out_weight.shape[1]
    shard = model // head_size
    doc_row = doc_ids.reshape(1, piece)
    payload = jax.ShapeDtypeStruct((heads // 2 * unit_rows(width), width), BF16)
    half_payload = jax.ShapeDtypeStruct((payload.shape[0] // 2, width), BF16)
    rows_bf16 = jax.ShapeDtypeStruct((piece, features), BF16)
    rows_f32 = jax.ShapeDtypeStruct((piece, features), F32)
    window = seq_size // 2
    pairs = seq_size // 2
    pair_rows = model // pairs
    pair_at = seq_at // 2
    square = pairs == head_size

    rows_in = joined_inputs(key_rows, value_rows, query_rows, doc_row)
    (element,) = kernel_call(
        functools.partial(tail_body, heads, width),
        [payload],
        (rows_in,),
        0.5,
        "tail_states",
    )
    near, far, reach = rotated(element, 1), rotated(element, 2), 2
    cots = [out_grad] + [swapped(out_grad, "head", b) for b in range(1, head_size)]
    near, far, cots = lax.optimization_barrier((near, far, cots))
    while reach < window:
        near = join_states(near, far, width)
        far = rotated(near, reach)
        reach *= 2
    near, cot_here = lax.optimization_barrier((near, out_grad))
    if square:
        turned = lax.ppermute(
            cot_here,
            ("seq", "head"),
            [
                ((2 * z + y) * head_size + h, (2 * h + y) * head_size + z)
                for z in range(pairs)
                for y in range(2)
                for h in range(head_size)
            ],
        )
    else:
        turned = cot_here

    (out_cot,) = kernel_call(
        functools.partial(cot_body, head_size, shard),
        [rows_bf16],
        (place, *cots, out_weight),
        1.5,
        "cotangent",
        smem=(0,),
    )
    sol, dual, mixed, back = kernel_call(
        functools.partial(solve_body, heads, width),
        [rows_bf16, rows_bf16, rows_bf16, payload],
        (ridge_reg, rows_in, out_cot, near, far),
        5.0,
        "solve",
        smem=(0,),
    )
    mixes = [mixed] + [None] * (pairs - 1)
    for step in range(1, pairs):
        if not square:
            mixes[step] = rotated(mixed, -2 * step)
        elif step & (step - 1) == 0:
            mixes[step] = swapped(mixed, "seq", 2 * step)
    there = swapped(back, "seq", 1)
    (pair_half,) = kernel_call(
        functools.partial(pair_join_body, width),
        [half_payload],
        (place, back, there),
        PAIR_JOIN_US,
        "pair_join",
        smem=(0,),
        scratch=[pltpu.VMEM(payload.shape, BF16)],
    )
    ready, turned = lax.optimization_barrier((mixed, turned))
    blocks = head_size // 2
    keep, send = kernel_call(
        functools.partial(project_body, head_size, shard),
        [
            jax.ShapeDtypeStruct((blocks * piece, shard), F32),
            jax.ShapeDtypeStruct((blocks * piece + piece, shard), BF16),
        ],
        (place, ready, out_weight, turned),
        1.0,
        "project",
        smem=(0,),
    )
    gathered, parts = [turned], [(0, 0)]
    mask, so_far = 1, turned
    got = swapped(send, "head", mask)
    held = {i: mixes[i] for i in range(1, pairs) if mixes[i] is not None and i % 2 == 0}
    held, got, after = lax.optimization_barrier((held, got, pair_half))
    near, far, reach = rotated(pair_half, -2), rotated(pair_half, -4), 4
    while reach < window:
        near = join_states(near, far, width)
        far = rotated(near, -reach)
        reach *= 2
    mine = join_states(near, far, width, after)
    theirs = swapped(mine, "seq", 1)
    for step in range(1, pairs):
        low = step & -step
        if mixes[step] is None:
            held[step] = mixes[step] = swapped(held[step ^ low], "seq", 2 * low)

    while blocks > 1:
        for c in range(mask):
            parts.append((len(gathered), (blocks + c) * piece))
        gathered.append(got)
        blocks //= 2
        mask *= 2
        keep, send = kernel_call(
            functools.partial(halve_body, 2 * blocks, piece),
            [
                jax.ShapeDtypeStruct((blocks * piece, shard), F32),
                jax.ShapeDtypeStruct((blocks * piece + mask * piece, shard), BF16),
            ],
            (keep, got, so_far),
            0.5,
            "halve",
        )
        so_far = send[blocks * piece :]
        got = swapped(send, "head", mask)
    for c in range(mask):
        parts.append((len(gathered), (blocks + c) * piece))
    gathered.append(got)
    layer_out = (keep + got[:piece].astype(F32)).astype(BF16)
    if not square:
        cot_full = lax.all_gather(out_grad, "head", axis=1, tiled=True)
        gathered = []
        for step in range(pairs):
            start = lax.rem(pair_at + pairs - step, pairs) * pair_rows
            block = lax.dynamic_slice_in_dim(cot_full, start, pair_rows, 1)
            gathered.append(rotated(block, -2 * step) if step else block)
        parts = [(step, 0) for step in range(pairs)]

    kept, given = kernel_call(
        functools.partial(pair_grad_body, piece, tuple(parts), len(gathered), square),
        [
            jax.ShapeDtypeStruct((pair_rows // 2, features), F32),
            jax.ShapeDtypeStruct((pair_rows // 2, features), BF16),
        ],
        (place, *gathered, *mixes),
        1.5,
        "pair_grad",
        smem=(0,),
        scratch=[
            pltpu.VMEM((pairs * piece, pair_rows), BF16),
            pltpu.VMEM((pairs * piece, features), BF16),
            pltpu.VMEM((pair_rows, features), F32),
        ],
    )
    grad_weight = kept + swapped(given, "seq", 1).astype(F32)

    local_k, local_v = kernel_call(
        functools.partial(local_grads_body, heads, width),
        [rows_f32, rows_f32],
        (rows_in, out_cot, sol, dual),
        1.1,
        "local_grads",
    )
    grad_keys, grad_values = kernel_call(
        functools.partial(final_grads_body, heads, width),
        [rows_bf16, rows_bf16],
        (place, rows_in, there, mine, theirs, local_k, local_v),
        FINAL_US,
        "final_grads",
        smem=(0,),
        scratch=[pltpu.VMEM(payload.shape, BF16)],
    )
    return (layer_out, dual, grad_keys, grad_values, grad_weight)


def solution(mesh):
    rows = P("seq", "head")
    in_specs = (rows, rows, rows, P("head"), P("head", None), rows, P("seq"))
    return jax.shard_map(
        per_device, mesh=mesh, in_specs=in_specs, out_specs=(rows,) * 5, check_vma=False
    )
```

time: 69.4 us -> 62 us (0.89)
  starting transfers between devices: 33 us -> 20.3 us
  waiting for transfers between devices: 16.5 us -> 24.2 us
  local copies, waits for them, and re-layouts: 3.45 us -> 0.02 us
  Pallas kernels: 10.1 us -> 13.1 us
  matrix products: 1.5 us -> 0 us
    ppermute x13 -> x11, starting transfers between devices: 21.9 us -> 11.4 us  [swapped(): return lax.ppermute(value, axis, [(i, i ^ mask) for i in range(devices)])]
    ppermute x13 -> x11, waiting for transfers between devices: 12.5 us -> 17 us  [swapped(): return lax.ppermute(value, axis, [(i, i ^ mask) for i in range(devices)])]
    ppermute x6 -> x5, waiting for transfers between devices: 4.01 us -> 7.22 us  [rotated(): lax.ppermute(value, 'seq', [(i, (i + by) % devices) for i in range(device...]
    ppermute x6 -> x5, starting transfers between devices: 11.1 us -> 8.07 us  [rotated(): lax.ppermute(value, 'seq', [(i, (i + by) % devices) for i in range(device...]
    pallas_call x6 -> x11, Pallas kernels: 10.1 us -> 13.1 us  [kernel_call(): pl.pallas_call(body, out_shape=out_shape, in_specs=[pl.BlockSpec(memory_s...]
    unnamed x28 -> x8, local copies, waits for them, and re-layouts: 2.67 us -> 0.02 us
    dot_general x1 -> x0, matrix products: 1.5 us -> none  [per_device(): lax.dot_general(jnp.concatenate(cot_blocks, axis=0), jnp.concatenate(mixe...]
    add x0 -> x1, other arithmetic: none -> 1.21 us  [joined_inputs(): total += jnp.pad(part, ((0, LABEL_ROWS), (i * features, width - (i + 1) *...]
  transfers between devices with their start and end apart: 19 -> 17, of which waited for: 8 -> 8; matrix products, arithmetic and copies ran while one was open for 7% -> 1% of each run, Pallas kernels for 14% -> 20%
where the time goes in v3:
time: 62 us; the launch traced here: 61.9 us
  waiting for transfers between devices  24.2 us (39%)
  starting transfers between devices  20.3 us (33%)
  Pallas kernels  13.1 us (21%)
  other arithmetic  3.53 us (6%)
  between operations  0.78 us (1%)
    ppermute x11, waiting for transfers between devices, swapped(): return lax.ppermute(value, axis, [(i, i ^ mask) for i in range(devices)])  17 us
    pallas_call x11, Pallas kernels, kernel_call(): pl.pallas_call(body, out_shape=out_shape, in_specs=[pl.BlockSpec(memory_s...  13.1 us
    ppermute x11, starting transfers between devices, swapped(): return lax.ppermute(value, axis, [(i, i ^ mask) for i in range(devices)])  11.4 us
    ppermute x5, starting transfers between devices, rotated(): lax.ppermute(value, 'seq', [(i, (i + by) % devices) for i in range(device...  8.07 us
    ppermute x5, waiting for transfers between devices, rotated(): lax.ppermute(value, 'seq', [(i, (i + by) % devices) for i in range(device...  7.22 us
  transfers between devices with their start and end apart: 17, of which 8 were waited for; matrix products, arithmetic and copies ran while one was open for 1% of the time, Pallas kernels for 20%

profile of v3, /device:TPU:0, one launch (start us, length us, event | category | flops | bytes accessed | tf_op | source)
XLA Modules:
  0.0 61.9 jit_solution(1923670173454216117)
XLA Ops:
  0.6 0.7 %convert_bitcast_fusion = bf16[1,128]{1,0:T(2,128)(2,1)S(1)} fusion(s32[128]{0:T(128)} %param.13), kind=kLoop, calls=%fused_computation.4 | loop fusion | flops 128 | bytes 768 | tf_op jit(solution)/shard_map/convert_element_type | solution.py:367
  1.3 1.2 %pad_add_fusion.rows_ref = bf16[144,1536]{1,0:T(8,128)(2,1)S(1)} fusion(bf16[128,512]{1,0:T(8,128)(2,1)} %param.7, bf16[128,512]{1,0:T(8,128)(2,1)} %param.9, bf16[128,512]{1,0:T(8,128)(2,1)} %param.8, bf16[1,128]{1,0:T(2,128)(2,1)S(1)} %convert_bitcast_fusion), kind=kLoop, calls=%fused_computation.1 | loop fusion | flops 1769472 | bytes 835840 | tf_op jit(solution)/shard_map/add | solution.py:370
  2.5 0.3 tail_states.1
  2.9 3.0 %collective-permute-start = (bf16[800,128]{1,0:T(8,128)(2,1)S(1)}, bf16[800,128]{1,0:T(8,128)(2,1)S(1)}, u32[]{:S(2)}, u32[]{:S(2)}) collective-permute-start(bf16[800,128]{1,0:T(8,128)(2,1)S(1)} %tail_states.1), channel_id=1, source_target_pairs={{0,4},{4,8},{8,12},{12,16},{16,20},{20,24},{24,28},{28,0},{1,5},{5... | collective-permute-start | bytes 614408 | tf_op jit(solution)/shard_map/ppermute | solution.py:354
  5.9 1.6 %collective-permute-start.1 = (bf16[800,128]{1,0:T(8,128)(2,1)S(1)}, bf16[800,128]{1,0:T(8,128)(2,1)S(1)}, u32[]{:S(2)}, u32[]{:S(2)}) collective-permute-start(bf16[800,128]{1,0:T(8,128)(2,1)S(1)} %tail_states.1), channel_id=1, source_target_pairs={{0,8},{4,12},{8,16},{12,20},{16,24},{20,28},{24,0},{28,4},{1,9},{5... | collective-permute-start | bytes 614408 | tf_op jit(solution)/shard_map/ppermute | solution.py:354
  7.5 0.0 collective-permute-start.2
  7.5 1.5 %collective-permute-start.3 = (bf16[128,512]{1,0:T(8,128)(2,1)S(1)}, bf16[128,512]{1,0:T(8,128)(2,1)S(1)}, u32[]{:S(2)}, u32[]{:S(2)}) collective-permute-start(bf16[128,512]{1,0:T(8,128)(2,1)S(1)} %copy-done.1), channel_id=1, source_target_pairs={{0,2},{1,3},{2,0},{3,1},{4,6},{5,7},{6,4},{7,5},{8,10},{9,11},{10,... | collective-permute-start | bytes 393224 | tf_op jit(solution)/shard_map/ppermute | solution.py:359
  9.0 0.4 collective-permute-start.4
  9.4 0.0 collective-permute-done.2.refs_1_
  9.4 4.4 %collective-permute-done.3.refs_2_ = bf16[128,512]{1,0:T(8,128)(2,1)S(1)} collective-permute-done((bf16[128,512]{1,0:T(8,128)(2,1)S(1)}, bf16[128,512]{1,0:T(8,128)(2,1)S(1)}, u32[]{:S(2)}, u32[]{:S(2)}) %collective-permute-start.3) | collective-permute-done | bytes 131104 | tf_op jit(solution)/shard_map/ppermute | solution.py:359
  13.8 2.1 %collective-permute-done.4.refs_3_ = bf16[128,512]{1,0:T(8,128)(2,1)} collective-permute-done((bf16[128,512]{1,0:T(8,128)(2,1)S(1)}, bf16[128,512]{1,0:T(8,128)(2,1)}, u32[]{:S(2)}, u32[]{:S(2)}) %collective-permute-start.4) | collective-permute-done | bytes 131104 | tf_op jit(solution)/shard_map/ppermute | solution.py:359
  15.9 0.0 collective-permute-done.near_ref
  15.9 0.0 collective-permute-done.1.far_ref
  15.9 0.2 join_states.2.near_ref
  16.1 1.6 %collective-permute-start.5 = (bf16[800,128]{1,0:T(8,128)(2,1)S(1)}, bf16[800,128]{1,0:T(8,128)(2,1)S(1)}, u32[]{:S(2)}, u32[]{:S(2)}) collective-permute-start(bf16[800,128]{1,0:T(8,128)(2,1)S(1)} %join_states.2.near_ref), channel_id=1, source_target_pairs={{0,8},{4,12},{8,16},{12,20},{16,24},{20,28},{24,0},{28,4},{1,9},{5... | collective-permute-start | bytes 614408 | tf_op jit(solution)/shard_map/ppermute | solution.py:354
  17.7 0.1 pad_add_fusion.1.place_ref
  17.8 0.8 %collective-permute-start.6 = (bf16[128,512]{1,0:T(8,128)(2,1)S(1)}, bf16[128,512]{1,0:T(8,128)(2,1)S(1)}, u32[]{:S(2)}, u32[]{:S(2)}) collective-permute-start(bf16[128,512]{1,0:T(8,128)(2,1)S(1)} %copy-done.1), channel_id=1, source_target_pairs={{0,0},{1,8},{2,16},{3,24},{4,4},{5,12},{6,20},{7,28},{8,1},{9,9},{... | collective-permute-start | bytes 393224 | tf_op jit(solution)/shard_map/ppermute | solution.py:422
  18.6 1.7 %cotangent.1.cot_ref = bf16[128,512]{1,0:T(8,128)(2,1)S(1)} custom-call(s32[2]{0:T(128)S(1)} %pad_add_fusion.1.place_ref, bf16[128,512]{1,0:T(8,128)(2,1)S(1)} %copy-done.1, bf16[128,512]{1,0:T(8,128)(2,1)S(1)} %collective-permute-done.2.refs_1_, bf16[128,512]{1,0:T(8,128)(2,1)S(1)} %collective-permute-done.3.refs_2_, ...), custom_call_target="tpu_custom_call" | custom-call | flops 1500000000 | bytes 2752520 | tf_op jit(solution)/shard_map/cotangent/pallas_call | solution.py:38
  20.4 4.9 %collective-permute-done.5.far_ref = bf16[800,128]{1,0:T(8,128)(2,1)S(1)} collective-permute-done((bf16[800,128]{1,0:T(8,128)(2,1)S(1)}, bf16[800,128]{1,0:T(8,128)(2,1)S(1)}, u32[]{:S(2)}, u32[]{:S(2)}) %collective-permute-start.5) | collective-permute-done | bytes 204832 | tf_op jit(solution)/shard_map/ppermute | solution.py:354
  25.3 5.1 %solve.1 = (bf16[128,512]{1,0:T(8,128)(2,1)S(1)}, bf16[128,512]{1,0:T(8,128)(2,1)}, bf16[128,512]{1,0:T(8,128)(2,1)S(1)}, bf16[800,128]{1,0:T(8,128)(2,1)S(1)}) custom-call(f32[4]{0:T(128)S(1)} %copy-done.2, bf16[144,1536]{1,0:T(8,128)(2,1)S(1)} %pad_add_fusion.rows_ref, bf16[128,512]{1,0:T(8,128)(2,1)S(1)} %cotangent.1.cot_ref, ...), custom_call_target="tpu_custom_call" | custom-call | flops 5000000000 | bytes 1581072 | tf_op jit(solution)/shard_map/solve/pallas_call | solution.py:38
  30.4 3.5 %collective-permute-start.9 = (bf16[800,128]{1,0:T(8,128)(2,1)S(1)}, bf16[800,128]{1,0:T(8,128)(2,1)S(1)}, u32[]{:S(2)}, u32[]{:S(2)}) collective-permute-start(bf16[800,128]{1,0:T(8,128)(2,1)S(1)} %get-tuple-element.45.here_ref), channel_id=1, source_target_pairs={{0,4},{4,0},{8,12},{12,8},{16,20},{20,16},{24,28},{28,24},{1,5},{5... | collective-permute-start | bytes 614408 | tf_op jit(solution)/shard_map/ppermute | solution.py:359
  33.9 0.0 collective-permute-start.7
  33.9 0.1 collective-permute-start.14
  33.9 0.0 collective-permute-done.6.turned_ref.refs_0_
  33.9 1.0 %project.1 = (f32[256,512]{1,0:T(8,128)S(1)}, bf16[384,512]{1,0:T(8,128)(2,1)S(1)}) custom-call(s32[2]{0:T(128)S(1)} %pad_add_fusion.1.place_ref, bf16[128,512]{1,0:T(8,128)(2,1)S(1)} %get-tuple-element.41.mixed_ref.refs_3_, bf16[512,2048]{1,0:T(8,128)(2,1)S(1)} %copy-done, bf16[128,512]{1,0:T(8,128)(2,1)S(1)} %collective-permute-done.6.turned_ref.refs_0_), custom_call_target="tpu_custom_call" | custom-call | flops 1000000000 | bytes 3276808 | tf_op jit(solution)/shard_map/project/pallas_call | solution.py:38
  35.0 0.0 copy-start.3
  35.0 0.1 collective-permute-start.8
  35.0 2.6 %collective-permute-done.9.there_ref = bf16[800,128]{1,0:T(8,128)(2,1)S(1)} collective-permute-done((bf16[800,128]{1,0:T(8,128)(2,1)S(1)}, bf16[800,128]{1,0:T(8,128)(2,1)S(1)}, u32[]{:S(2)}, u32[]{:S(2)}) %collective-permute-start.9) | collective-permute-done | bytes 204832 | tf_op jit(solution)/shard_map/ppermute | solution.py:359
  37.6 0.7 %pair_join.1.refs_0_ = bf16[400,128]{1,0:T(8,128)(2,1)S(1)} custom-call(s32[2]{0:T(128)S(1)} %pad_add_fusion.1.place_ref, bf16[800,128]{1,0:T(8,128)(2,1)S(1)} %get-tuple-element.45.here_ref, bf16[800,128]{1,0:T(8,128)(2,1)S(1)} %collective-permute-done.9.there_ref), custom_call_target="tpu_custom_call" | custom-call | flops 5000000000 | bytes 512008 | tf_op jit(solution)/shard_map/pair_join/pallas_call | solution.py:38
  38.3 1.8 %collective-permute-start.11 = (bf16[400,128]{1,0:T(8,128)(2,1)S(1)}, bf16[400,128]{1,0:T(8,128)(2,1)S(1)}, u32[]{:S(2)}, u32[]{:S(2)}) collective-permute-start(bf16[400,128]{1,0:T(8,128)(2,1)S(1)} %pair_join.1.refs_0_), channel_id=1, source_target_pairs={{0,24},{4,28},{8,0},{12,4},{16,8},{20,12},{24,16},{28,20},{1,25},{... | collective-permute-start | bytes 307208 | tf_op jit(solution)/shard_map/ppermute | solution.py:354
  40.1 1.1 %local_grads.1 = (f32[128,512]{1,0:T(8,128)S(1)}, f32[128,512]{1,0:T(8,128)S(1)}) custom-call(bf16[144,1536]{1,0:T(8,128)(2,1)S(1)} %pad_add_fusion.rows_ref, bf16[128,512]{1,0:T(8,128)(2,1)S(1)} %cotangent.1.cot_ref, bf16[128,512]{1,0:T(8,128)(2,1)S(1)} %get-tuple-element.51.sol_ref, bf16[128,512]{1,0:T(8,128)(2,1)S(1)} %copy-done.3), custom_call_target="tpu_custom_call" | custom-call | flops 1100000000 | bytes 1359872 | tf_op jit(solution)/shard_map/local_grads/pallas_call | solution.py:38
  41.2 0.0 collective-permute-done.7.refs_5_
  41.2 0.1 halve.1
  41.3 2.6 %collective-permute-start.10 = (bf16[384,512]{1,0:T(8,128)(2,1)S(1)}, bf16[384,512]{1,0:T(8,128)(2,1)S(1)}, u32[]{:S(2)}, u32[]{:S(2)}) collective-permute-start(bf16[384,512]{1,0:T(8,128)(2,1)S(1)} %get-tuple-element.48), channel_id=1, source_target_pairs={{0,2},{1,3},{2,0},{3,1},{4,6},{5,7},{6,4},{7,5},{8,10},{9,11},{10,... | collective-permute-start | bytes 1179656 | tf_op jit(solution)/shard_map/ppermute | solution.py:359
  43.9 1.9 %collective-permute-start.15 = (bf16[128,512]{1,0:T(8,128)(2,1)S(1)}, bf16[128,512]{1,0:T(8,128)(2,1)S(1)}, u32[]{:S(2)}, u32[]{:S(2)}) collective-permute-start(bf16[128,512]{1,0:T(8,128)(2,1)S(1)} %collective-permute-done.7.refs_5_), channel_id=1, source_target_pairs={{0,8},{4,12},{8,0},{12,4},{16,24},{20,28},{24,16},{28,20},{1,9},{5... | collective-permute-start | bytes 393224 | tf_op jit(solution)/shard_map/ppermute | solution.py:359
  45.8 0.0 collective-permute-done.11.near_ref
  45.8 2.3 %collective-permute-done.12.far_ref = bf16[400,128]{1,0:T(8,128)(2,1)S(1)} collective-permute-done((bf16[400,128]{1,0:T(8,128)(2,1)S(1)}, bf16[400,128]{1,0:T(8,128)(2,1)S(1)}, u32[]{:S(2)}, u32[]{:S(2)}) %collective-permute-start.12) | collective-permute-done | bytes 102432 | tf_op jit(solution)/shard_map/ppermute | solution.py:354
  48.1 0.1 join_states.3.mine_ref
  48.2 0.1 collective-permute-start.13
  48.3 1.5 %collective-permute-done.15.refs_6_ = bf16[128,512]{1,0:T(8,128)(2,1)S(1)} collective-permute-done((bf16[128,512]{1,0:T(8,128)(2,1)S(1)}, bf16[128,512]{1,0:T(8,128)(2,1)S(1)}, u32[]{:S(2)}, u32[]{:S(2)}) %collective-permute-start.15) | collective-permute-done | bytes 131104 | tf_op jit(solution)/shard_map/ppermute | solution.py:359
  49.8 2.8 %collective-permute-done.10.refs_2_ = bf16[384,512]{1,0:T(8,128)(2,1)S(1)} collective-permute-done((bf16[384,512]{1,0:T(8,128)(2,1)S(1)}, bf16[384,512]{1,0:T(8,128)(2,1)S(1)}, u32[]{:S(2)}, u32[]{:S(2)}) %collective-permute-start.10) | collective-permute-done | bytes 393248 | tf_op jit(solution)/shard_map/ppermute | solution.py:359
  52.6 1.2 %pair_grad.1 = (f32[256,512]{1,0:T(8,128)S(1)}, bf16[256,512]{1,0:T(8,128)(2,1)S(1)}) custom-call(s32[2]{0:T(128)S(1)} %pad_add_fusion.1.place_ref, bf16[128,512]{1,0:T(8,128)(2,1)S(1)} %collective-permute-done.6.turned_ref.refs_0_, bf16[384,512]{1,0:T(8,128)(2,1)S(1)} %collective-permute-done.8.got_ref.refs_1_, ...), custom_call_target="tpu_custom_call" | custom-call | flops 1500000000 | bytes 2228232 | tf_op jit(solution)/shard_map/pair_grad/pallas_call | solution.py:38
  53.8 1.4 %collective-permute-start.16 = (bf16[256,512]{1,0:T(8,128)(2,1)S(1)}, bf16[256,512]{1,0:T(8,128)(2,1)S(1)}, u32[]{:S(2)}, u32[]{:S(2)}) collective-permute-start(bf16[256,512]{1,0:T(8,128)(2,1)S(1)} %get-tuple-element.58), channel_id=1, source_target_pairs={{0,4},{4,0},{8,12},{12,8},{16,20},{20,16},{24,28},{28,24},{1,5},{5... | collective-permute-start | bytes 786440 | tf_op jit(solution)/shard_map/ppermute | solution.py:359
  55.1 0.0 collective-permute-done.13.theirs_ref
  55.1 1.6 %final_grads.1 = (bf16[128,512]{1,0:T(8,128)(2,1)}, bf16[128,512]{1,0:T(8,128)(2,1)}) custom-call(s32[2]{0:T(128)S(1)} %pad_add_fusion.1.place_ref, bf16[144,1536]{1,0:T(8,128)(2,1)S(1)} %pad_add_fusion.rows_ref, bf16[800,128]{1,0:T(8,128)(2,1)S(1)} %collective-permute-done.9.there_ref, bf16[400,128]{1,0:T(8,128)(2,1)S(1)} %join_states.3.mine_ref, ...), custom_call_target="tpu_custom_call" | custom-call | flops 1000000000 | bytes 1638408 | tf_op jit(solution)/shard_map/final_grads/pallas_call | solution.py:38
  56.8 0.7 %add_convert_fusion = bf16[128,512]{1,0:T(8,128)(2,1)} fusion(f32[128,512]{1,0:T(8,128)S(1)} %get-tuple-element.47, bf16[384,512]{1,0:T(8,128)(2,1)S(1)} %collective-permute-done.10.refs_2_), kind=kLoop, calls=%fused_computation.2 | loop fusion | flops 196608 | bytes 524288 | tf_op jit(solution)/shard_map/convert_element_type | solution.py:518
  57.4 3.5 %collective-permute-done.16 = bf16[256,512]{1,0:T(8,128)(2,1)S(1)} collective-permute-done((bf16[256,512]{1,0:T(8,128)(2,1)S(1)}, bf16[256,512]{1,0:T(8,128)(2,1)S(1)}, u32[]{:S(2)}, u32[]{:S(2)}) %collective-permute-start.16) | collective-permute-done | bytes 262176 | tf_op jit(solution)/shard_map/ppermute | solution.py:359
  61.0 0.9 %convert_add_fusion = f32[256,512]{1,0:T(8,128)} fusion(f32[256,512]{1,0:T(8,128)S(1)} %get-tuple-element.57, bf16[256,512]{1,0:T(8,128)(2,1)S(1)} %collective-permute-done.16), kind=kLoop, calls=%fused_computation | loop fusion | flops 262144 | bytes 1310720 | tf_op jit(solution)/shard_map/add | solution.py:544
  (10 shorter events, 0.0 us)
Async XLA Ops:
  0.6 6.9 %copy-start.1 = (bf16[128,512]{1,0:T(8,128)(2,1)S(1)}, bf16[128,512]{1,0:T(8,128)(2,1)}, u32[]{:S(2)}) copy-start(bf16[128,512]{1,0:T(8,128)(2,1)} %refs_0_) | copy-start | bytes 393220
  1.3 17.3 %copy-start = (bf16[512,2048]{1,0:T(8,128)(2,1)S(1)}, bf16[512,2048]{1,0:T(8,128)(2,1)}, u32[]{:S(2)}) copy-start(bf16[512,2048]{1,0:T(8,128)(2,1)} %weight_ref.1) | copy-start | bytes 6291460
  2.9 13.0 %collective-permute-start = (bf16[800,128]{1,0:T(8,128)(2,1)S(1)}, bf16[800,128]{1,0:T(8,128)(2,1)S(1)}, u32[]{:S(2)}, u32[]{:S(2)}) collective-permute-start(bf16[800,128]{1,0:T(8,128)(2,1)S(1)} %tail_states.1), channel_id=1, source_target_pairs={{0,4},{4,8},{8,12},{12,16},{16,20},{20,24},{24,28},{28,0},{1,5},{5... | collective-permute-start | bytes 614408 | tf_op jit(solution)/shard_map/ppermute | solution.py:354
  5.9 10.0 %collective-permute-start.1 = (bf16[800,128]{1,0:T(8,128)(2,1)S(1)}, bf16[800,128]{1,0:T(8,128)(2,1)S(1)}, u32[]{:S(2)}, u32[]{:S(2)}) collective-permute-start(bf16[800,128]{1,0:T(8,128)(2,1)S(1)} %tail_states.1), channel_id=1, source_target_pairs={{0,8},{4,12},{8,16},{12,20},{16,24},{20,28},{24,0},{28,4},{1,9},{5... | collective-permute-start | bytes 614408 | tf_op jit(solution)/shard_map/ppermute | solution.py:354
  7.5 1.9 %collective-permute-start.2 = (bf16[128,512]{1,0:T(8,128)(2,1)S(1)}, bf16[128,512]{1,0:T(8,128)(2,1)S(1)}, u32[]{:S(2)}, u32[]{:S(2)}) collective-permute-start(bf16[128,512]{1,0:T(8,128)(2,1)S(1)} %copy-done.1), channel_id=1, source_target_pairs={{0,1},{1,0},{2,3},{3,2},{4,5},{5,4},{6,7},{7,6},{8,9},{9,8},{10,11... | collective-permute-start | bytes 393224 | tf_op jit(solution)/shard_map/ppermute | solution.py:359
  7.5 6.3 %collective-permute-start.3 = (bf16[128,512]{1,0:T(8,128)(2,1)S(1)}, bf16[128,512]{1,0:T(8,128)(2,1)S(1)}, u32[]{:S(2)}, u32[]{:S(2)}) collective-permute-start(bf16[128,512]{1,0:T(8,128)(2,1)S(1)} %copy-done.1), channel_id=1, source_target_pairs={{0,2},{1,3},{2,0},{3,1},{4,6},{5,7},{6,4},{7,5},{8,10},{9,11},{10,... | collective-permute-start | bytes 393224 | tf_op jit(solution)/shard_map/ppermute | solution.py:359
  9.0 6.9 %collective-permute-start.4 = (bf16[128,512]{1,0:T(8,128)(2,1)S(1)}, bf16[128,512]{1,0:T(8,128)(2,1)}, u32[]{:S(2)}, u32[]{:S(2)}) collective-permute-start(bf16[128,512]{1,0:T(8,128)(2,1)S(1)} %copy-done.1), channel_id=1, source_target_pairs={{0,3},{1,2},{2,1},{3,0},{4,7},{5,6},{6,5},{7,4},{8,11},{9,10},{10,... | collective-permute-start | bytes 393224 | tf_op jit(solution)/shard_map/ppermute | solution.py:359
  16.1 9.2 %collective-permute-start.5 = (bf16[800,128]{1,0:T(8,128)(2,1)S(1)}, bf16[800,128]{1,0:T(8,128)(2,1)S(1)}, u32[]{:S(2)}, u32[]{:S(2)}) collective-permute-start(bf16[800,128]{1,0:T(8,128)(2,1)S(1)} %join_states.2.near_ref), channel_id=1, source_target_pairs={{0,8},{4,12},{8,16},{12,20},{16,24},{20,28},{24,0},{28,4},{1,9},{5... | collective-permute-start | bytes 614408 | tf_op jit(solution)/shard_map/ppermute | solution.py:354
  17.8 7.5 %copy-start.2 = (f32[4]{0:T(128)S(1)}, f32[4]{0:T(128)}, u32[]{:S(2)}) copy-start(f32[4]{0:T(128)} %ridge_ref.1) | copy-start | bytes 52
  17.8 16.1 %collective-permute-start.6 = (bf16[128,512]{1,0:T(8,128)(2,1)S(1)}, bf16[128,512]{1,0:T(8,128)(2,1)S(1)}, u32[]{:S(2)}, u32[]{:S(2)}) collective-permute-start(bf16[128,512]{1,0:T(8,128)(2,1)S(1)} %copy-done.1), channel_id=1, source_target_pairs={{0,0},{1,8},{2,16},{3,24},{4,4},{5,12},{6,20},{7,28},{8,1},{9,9},{... | collective-permute-start | bytes 393224 | tf_op jit(solution)/shard_map/ppermute | solution.py:422
  30.4 7.2 %collective-permute-start.9 = (bf16[800,128]{1,0:T(8,128)(2,1)S(1)}, bf16[800,128]{1,0:T(8,128)(2,1)S(1)}, u32[]{:S(2)}, u32[]{:S(2)}) collective-permute-start(bf16[800,128]{1,0:T(8,128)(2,1)S(1)} %get-tuple-element.45.here_ref), channel_id=1, source_target_pairs={{0,4},{4,0},{8,12},{12,8},{16,20},{20,16},{24,28},{28,24},{1,5},{5... | collective-permute-start | bytes 614408 | tf_op jit(solution)/shard_map/ppermute | solution.py:359
  33.9 7.3 %collective-permute-start.7 = (bf16[128,512]{1,0:T(8,128)(2,1)S(1)}, bf16[128,512]{1,0:T(8,128)(2,1)S(1)}, u32[]{:S(2)}, u32[]{:S(2)}) collective-permute-start(bf16[128,512]{1,0:T(8,128)(2,1)S(1)} %get-tuple-element.41.mixed_ref.refs_3_), channel_id=1, source_target_pairs={{0,16},{4,20},{8,24},{12,28},{16,0},{20,4},{24,8},{28,12},{1,17},{... | collective-permute-start | bytes 393224 | tf_op jit(solution)/shard_map/ppermute | solution.py:359
  33.9 14.4 %collective-permute-start.14 = (bf16[128,512]{1,0:T(8,128)(2,1)S(1)}, bf16[128,512]{1,0:T(8,128)(2,1)S(1)}, u32[]{:S(2)}, u32[]{:S(2)}) collective-permute-start(bf16[128,512]{1,0:T(8,128)(2,1)S(1)} %get-tuple-element.41.mixed_ref.refs_3_), channel_id=1, source_target_pairs={{0,8},{4,12},{8,0},{12,4},{16,24},{20,28},{24,16},{28,20},{1,9},{5... | collective-permute-start | bytes 393224 | tf_op jit(solution)/shard_map/ppermute | solution.py:359
  35.0 5.2 %copy-start.3 = (bf16[128,512]{1,0:T(8,128)(2,1)S(1)}, bf16[128,512]{1,0:T(8,128)(2,1)}, u32[]{:S(2)}) copy-start(bf16[128,512]{1,0:T(8,128)(2,1)} %get-tuple-element.28.dual_ref) | copy-start | bytes 393220
  35.0 6.2 %collective-permute-start.8 = (bf16[384,512]{1,0:T(8,128)(2,1)S(1)}, bf16[384,512]{1,0:T(8,128)(2,1)S(1)}, u32[]{:S(2)}, u32[]{:S(2)}) collective-permute-start(bf16[384,512]{1,0:T(8,128)(2,1)S(1)} %get-tuple-element.44), channel_id=1, source_target_pairs={{0,1},{1,0},{2,3},{3,2},{4,5},{5,4},{6,7},{7,6},{8,9},{9,8},{10,11... | collective-permute-start | bytes 1179656 | tf_op jit(solution)/shard_map/ppermute | solution.py:359
  38.3 7.6 %collective-permute-start.11 = (bf16[400,128]{1,0:T(8,128)(2,1)S(1)}, bf16[400,128]{1,0:T(8,128)(2,1)S(1)}, u32[]{:S(2)}, u32[]{:S(2)}) collective-permute-start(bf16[400,128]{1,0:T(8,128)(2,1)S(1)} %pair_join.1.refs_0_), channel_id=1, source_target_pairs={{0,24},{4,28},{8,0},{12,4},{16,8},{20,12},{24,16},{28,20},{1,25},{... | collective-permute-start | bytes 307208 | tf_op jit(solution)/shard_map/ppermute | solution.py:354
  40.1 8.0 %collective-permute-start.12 = (bf16[400,128]{1,0:T(8,128)(2,1)S(1)}, bf16[400,128]{1,0:T(8,128)(2,1)S(1)}, u32[]{:S(2)}, u32[]{:S(2)}) collective-permute-start(bf16[400,128]{1,0:T(8,128)(2,1)S(1)} %pair_join.1.refs_0_), channel_id=1, source_target_pairs={{0,16},{4,20},{8,24},{12,28},{16,0},{20,4},{24,8},{28,12},{1,17},{... | collective-permute-start | bytes 307208 | tf_op jit(solution)/shard_map/ppermute | solution.py:354
  41.3 11.3 %collective-permute-start.10 = (bf16[384,512]{1,0:T(8,128)(2,1)S(1)}, bf16[384,512]{1,0:T(8,128)(2,1)S(1)}, u32[]{:S(2)}, u32[]{:S(2)}) collective-permute-start(bf16[384,512]{1,0:T(8,128)(2,1)S(1)} %get-tuple-element.48), channel_id=1, source_target_pairs={{0,2},{1,3},{2,0},{3,1},{4,6},{5,7},{6,4},{7,5},{8,10},{9,11},{10,... | collective-permute-start | bytes 1179656 | tf_op jit(solution)/shard_map/ppermute | solution.py:359
  43.9 6.0 %collective-permute-start.15 = (bf16[128,512]{1,0:T(8,128)(2,1)S(1)}, bf16[128,512]{1,0:T(8,128)(2,1)S(1)}, u32[]{:S(2)}, u32[]{:S(2)}) collective-permute-start(bf16[128,512]{1,0:T(8,128)(2,1)S(1)} %collective-permute-done.7.refs_5_), channel_id=1, source_target_pairs={{0,8},{4,12},{8,0},{12,4},{16,24},{20,28},{24,16},{28,20},{1,9},{5... | collective-permute-start | bytes 393224 | tf_op jit(solution)/shard_map/ppermute | solution.py:359
  48.2 6.9 %collective-permute-start.13 = (bf16[400,128]{1,0:T(8,128)(2,1)S(1)}, bf16[400,128]{1,0:T(8,128)(2,1)S(1)}, u32[]{:S(2)}, u32[]{:S(2)}) collective-permute-start(bf16[400,128]{1,0:T(8,128)(2,1)S(1)} %join_states.3.mine_ref), channel_id=1, source_target_pairs={{0,4},{4,0},{8,12},{12,8},{16,20},{20,16},{24,28},{28,24},{1,5},{5... | collective-permute-start | bytes 307208 | tf_op jit(solution)/shard_map/ppermute | solution.py:359
  53.8 7.2 %collective-permute-start.16 = (bf16[256,512]{1,0:T(8,128)(2,1)S(1)}, bf16[256,512]{1,0:T(8,128)(2,1)S(1)}, u32[]{:S(2)}, u32[]{:S(2)}) collective-permute-start(bf16[256,512]{1,0:T(8,128)(2,1)S(1)} %get-tuple-element.58), channel_id=1, source_target_pairs={{0,4},{4,0},{8,12},{12,8},{16,20},{20,16},{24,28},{28,24},{1,5},{5... | collective-permute-start | bytes 786440 | tf_op jit(solution)/shard_map/ppermute | solution.py:359

commit v4 on v3

--- a/solution.py
+++ b/solution.py
@@ -18,6 +18,8 @@
 FINAL_US = 1.0
 PAIR_JOIN_US = 5.0
 MINE_US = 6.0
+PAIR_US = 1.5
+HALVE_US = 0.5
 
 
 def mm(a, b):
@@ -94,13 +96,16 @@
 
 
 def join_units(near, far, width):
-    total = near.astype(F32)
-    tail = slice(near.shape[0] - LABEL_ROWS, near.shape[0])
-    near_label, far_label = near[tail].astype(F32), far[tail].astype(F32)
-    joined = (near_label[LABEL_ROWS - 1 :] == far_label[LABEL_ROWS - 1 :]).astype(F32)
-    total = total + joined * far.astype(F32)
-    row = lax.rem(lax.broadcasted_iota(jnp.int32, near.shape, 0), unit_rows(width))
-    return jnp.where(row <= 3 * width, total, near.astype(F32))
+    near, far = near.astype(F32), far.astype(F32)
+    size = unit_rows(width)
+    joined = (near[size - 1 : size, :] == far[size - 1 : size, :]).astype(F32)
+    number = lax.broadcasted_iota(jnp.int32, (LABEL_ROWS, width), 0) == 0
+    parts = []
+    for base in range(0, near.shape[0], size):
+        body, rest = slice(base, base + 3 * width), slice(base + 3 * width, base + size)
+        parts.append(near[body] + joined * far[body])
+        parts.append(jnp.where(number, near[rest] + joined * far[rest], near[rest]))
+    return jnp.concatenate(parts, axis=0)
 
 
 def unpack_symmetric(square, row):
@@ -156,7 +161,8 @@
     cot_ref[...] = total.astype(BF16)
 
 
-def project_body(count, shard, place_ref, mixed_ref, weight_ref, turned_ref, keep_ref, send_ref):
+def project_body(count, shard, place_ref, mixed_ref, weight_ref, *refs):
+    extras, keep_ref, send_ref = refs[:-2], refs[-2], refs[-1]
     piece = mixed_ref.shape[0]
     me = place_ref[1]
     mixed = mixed_ref[...]
@@ -169,10 +175,12 @@
             send_ref[rows, :] = part.astype(BF16)
         else:
             keep_ref[rows, :] = part
-    send_ref[count // 2 * piece :, :] = turned_ref[...]
-
-
-def halve_body(blocks, piece, keep_ref, got_ref, turned_ref, rest_ref, send_ref):
+    for i, extra in enumerate(extras):
+        row = (count // 2 + i) * piece
+        send_ref[row : row + piece, :] = extra[...]
+
+
+def halve_body(blocks, piece, keep_ref, got_ref, rest_ref, send_ref):
     for c in range(blocks):
         rows = slice(c * piece, (c + 1) * piece)
         target = slice(c // 2 * piece, (c // 2 + 1) * piece)
@@ -181,9 +189,6 @@
             send_ref[target, :] = total.astype(BF16)
         else:
             rest_ref[target, :] = total
-    sent, gathered = blocks // 2 * piece, turned_ref.shape[0]
-    send_ref[sent : sent + gathered, :] = turned_ref[...]
-    send_ref[sent + gathered :, :] = got_ref[blocks * piece :, :]
 
 
 def join_body(width, near_ref, far_ref, *refs):
@@ -191,14 +196,13 @@
     out_ref[...] = join_units(near_ref[...], far_ref[...], width).astype(BF16)
 
 
-def pair_join_body(width, place_ref, here_ref, there_ref, out_ref, both_ref):
+def pair_join_body(width, place_ref, here_ref, there_ref, out_ref):
     half = out_ref.shape[0]
     odd = lax.rem(place_ref[0], 2)
     mine = pl.ds(pl.multiple_of(odd * half, LABEL_ROWS), half)
-    both_ref[pl.ds(pl.multiple_of(odd * half, LABEL_ROWS), half), :] = here_ref[mine, :]
-    both_ref[pl.ds(pl.multiple_of((1 - odd) * half, LABEL_ROWS), half), :] = there_ref[mine, :]
-    total = join_units(both_ref[:half, :], both_ref[half:, :], width)
-    out_ref[...] = total.astype(BF16)
+    here, there = here_ref[mine, :].astype(F32), there_ref[mine, :].astype(F32)
+    first, second = jnp.where(odd == 1, there, here), jnp.where(odd == 1, here, there)
+    out_ref[...] = join_units(first, second, width).astype(BF16)
 
 
 def pair_grad_body(piece, parts, arrays, by_place, place_ref, *refs):
@@ -235,59 +239,61 @@
     same = document_mask(across, down).astype(F32)
     same_two = jnp.concatenate([same, same], axis=0)
     first = jnp.min(across, axis=1, keepdims=True)
-    head_rows = (down == first)[:, :width].astype(F32)
+    head_rows = (down == first)[:, :width].astype(F32).astype(BF16)
     units = join_units(near_ref[...], far_ref[...], width)
     label, value_states, gram_states = unpack_states(units, heads, width)
     carried = ((down + 1)[:, :width] == label).astype(F32)
     carried_two = jnp.concatenate([carried, carried], axis=0)
-    keys, rhs_keys, values, solutions, residuals, directions, squares = ([] for _ in range(7))
-    for h in range(heads):
+    every = range(heads)
+    keys = [head_rows_of(rows_ref, heads, width, 0, h) for h in every]
+    values = [head_rows_of(rows_ref, heads, width, 1, h) for h in every]
+    queries = [head_rows_of(rows_ref, heads, width, 2, h).astype(F32) for h in every]
+    cots = [cot_ref[:, h * width : (h + 1) * width] for h in every]
+    boths = [
+        mm(cots[h], jnp.concatenate([values[h].T, value_states[h]], axis=1)) for h in every
+    ]
+    scores = [(both[:, :piece] * same).astype(BF16) for both in boths]
+    targets = [carried * boths[h][:, piece:] + mm(scores[h], keys[h]) for h in every]
+    rhs_keys = [jnp.concatenate([keys[h].T, gram_states[h]], axis=1) for h in every]
+    directions = [jnp.concatenate([queries[h], targets[h]], axis=0) for h in every]
+    residuals = directions
+    solutions = [jnp.zeros_like(start) for start in directions]
+    squares = [jnp.sum(start * start, axis=1, keepdims=True) for start in directions]
+    for step in range(CG_STEPS):
+        ps = directions
+        boths = [mm(ps[h].astype(BF16), rhs_keys[h]) for h in range(heads)]
+        scores = [(both[:, :piece] * same_two).astype(BF16) for both in boths]
+        locals_ = [mm(scores[h], keys[h]) for h in range(heads)]
+        applied = [
+            carried_two * boths[h][:, piece:] + locals_[h] + ridge_ref[h] * ps[h]
+            for h in range(heads)
+        ]
+        sizes = [squares[h] / (jnp.sum(ps[h] * applied[h], axis=1, keepdims=True) + EPSILON) for h in range(heads)]
+        solutions = [solutions[h] + sizes[h] * ps[h] for h in range(heads)]
+        if step + 1 < CG_STEPS:
+            residuals = [residuals[h] - sizes[h] * applied[h] for h in range(heads)]
+            news = [jnp.sum(residuals[h] * residuals[h], axis=1, keepdims=True) for h in range(heads)]
+            directions = [
+                residuals[h] + news[h] / (squares[h] + EPSILON) * ps[h] for h in range(heads)
+            ]
+            squares = news
+    sols = [solutions[h][:piece].astype(BF16) for h in every]
+    duals = [solutions[h][piece:].astype(BF16) for h in every]
+    masked = [sol * head_rows for sol in sols]
+    sums = [mm_tn(cots[h], masked[h]) for h in every]
+    crosses = [mm_tn(duals[h], masked[h]) for h in every]
+    boths = [
+        mm(sols[h], jnp.concatenate([rhs_keys[h][:, :piece], value_states[h].T], axis=1))
+        for h in every
+    ]
+    scores = [(both[:, :piece] * same).astype(BF16) for both in boths]
+    outputs = [carried * boths[h][:, piece:] + mm(scores[h], values[h]) for h in every]
+    for h in every:
         cols = slice(h * width, (h + 1) * width)
-        key_h = head_rows_of(rows_ref, heads, width, 0, h)
-        value_h = head_rows_of(rows_ref, heads, width, 1, h)
-        query_h = head_rows_of(rows_ref, heads, width, 2, h)
-        cot_h = cot_ref[:, cols]
-        both = mm(cot_h, jnp.concatenate([value_h.T, value_states[h]], axis=1))
-        scores = (both[:, :piece] * same).astype(BF16)
-        target = carried * both[:, piece:] + mm(scores, key_h)
-        start = jnp.concatenate([query_h.astype(F32), target], axis=0)
-        keys.append(key_h)
-        values.append(value_h)
-        rhs_keys.append(jnp.concatenate([key_h.T, gram_states[h]], axis=1))
-        solutions.append(jnp.zeros_like(start))
-        residuals.append(start)
-        directions.append(start)
-        squares.append(jnp.sum(start * start, axis=1, keepdims=True))
-    for step in range(CG_STEPS):
-        for h in range(heads):
-            p = directions[h]
-            both = mm(p.astype(BF16), rhs_keys[h])
-            scores = (both[:, :piece] * same_two).astype(BF16)
-            applied = carried_two * both[:, piece:] + mm(scores, keys[h]) + ridge_ref[h] * p
-            size = squares[h] / (jnp.sum(p * applied, axis=1, keepdims=True) + EPSILON)
-            solutions[h] = solutions[h] + size * p
-            if step + 1 < CG_STEPS:
-                residuals[h] = residuals[h] - size * applied
-                new_sq = jnp.sum(residuals[h] * residuals[h], axis=1, keepdims=True)
-                directions[h] = residuals[h] + new_sq / (squares[h] + EPSILON) * p
-                squares[h] = new_sq
-    sums, crosses = [], []
-    for h in range(heads):
-        cols = slice(h * width, (h + 1) * width)
-        sol = solutions[h][:piece]
-        sol_b = sol.astype(BF16)
-        dual_b = solutions[h][piece:].astype(BF16)
-        both = mm(sol_b, jnp.concatenate([rhs_keys[h][:, :piece], value_states[h].T], axis=1))
-        scores = (both[:, :piece] * same).astype(BF16)
-        output = carried * both[:, piece:] + mm(scores, values[h])
-        mixed_ref[:, cols] = output.astype(BF16)
-        sol_ref[:, cols] = sol_b
-        dual_ref[:, cols] = dual_b
-        masked = (head_rows * sol).astype(BF16)
-        sums.append(mm_tn(cot_ref[:, cols], masked))
-        cross = mm_tn(dual_b, masked)
-        crosses.append(cross + cross.T)
-    pack_states(out_ref, first[:1] + 1, sums, crosses)
+        mixed_ref[:, cols] = outputs[h].astype(BF16)
+        sol_ref[:, cols] = sols[h]
+        dual_ref[:, cols] = duals[h]
+    pack_states(out_ref, first[:1] + 1, sums, [cross + cross.T for cross in crosses])
 
 
 def local_grads_body(
@@ -338,15 +344,15 @@
     )
     label, grad_states, gram_grads = unpack_states(units, heads, width)
     later = ((down + 1)[:, :width] == label).astype(F32)
-    for h in range(heads):
+    every = range(heads)
+    keys = [head_rows_of(rows_ref, heads, width, 0, h) for h in every]
+    values = [head_rows_of(rows_ref, heads, width, 1, h) for h in every]
+    from_values = [mm_nt(keys[h], grad_states[h]) for h in every]
+    from_keys = [mm(values[h], grad_states[h]) - mm(keys[h], gram_grads[h]) for h in every]
+    for h in every:
         cols = slice(h * width, (h + 1) * width)
-        key_h = head_rows_of(rows_ref, heads, width, 0, h)
-        value_h = head_rows_of(rows_ref, heads, width, 1, h)
-        grad_state, gram_grad = grad_states[h], gram_grads[h]
-        grad_v = local_v_ref[:, cols] + later * mm_nt(key_h, grad_state)
-        grad_k = local_k_ref[:, cols] + later * (mm(value_h, grad_state) - mm(key_h, gram_grad))
-        grad_v_ref[:, cols] = grad_v.astype(BF16)
-        grad_k_ref[:, cols] = grad_k.astype(BF16)
+        grad_v_ref[:, cols] = (local_v_ref[:, cols] + later * from_values[h]).astype(BF16)
+        grad_k_ref[:, cols] = (local_k_ref[:, cols] + later * from_keys[h]).astype(BF16)
 
 
 def rotated(value, by):
@@ -462,24 +468,27 @@
         PAIR_JOIN_US,
         "pair_join",
         smem=(0,),
-        scratch=[pltpu.VMEM(payload.shape, BF16)],
     )
     ready, turned = lax.optimization_barrier((mixed, turned))
+    even_blocks, mask = {0: turned}, 2
+    while square and mask < head_size:
+        for i in list(even_blocks):
+            even_blocks[i | mask] = swapped(even_blocks[i], "head", mask)
+        mask *= 2
+    even_blocks = [even_blocks[i] for i in sorted(even_blocks)]
     blocks = head_size // 2
     keep, send = kernel_call(
         functools.partial(project_body, head_size, shard),
         [
             jax.ShapeDtypeStruct((blocks * piece, shard), F32),
-            jax.ShapeDtypeStruct((blocks * piece + piece, shard), BF16),
+            jax.ShapeDtypeStruct(((blocks + len(even_blocks)) * piece, shard), BF16),
         ],
-        (place, ready, out_weight, turned),
+        (place, ready, out_weight, *even_blocks),
         1.0,
         "project",
         smem=(0,),
     )
-    gathered, parts = [turned], [(0, 0)]
-    mask, so_far = 1, turned
-    got = swapped(send, "head", mask)
+    got, mask = swapped(send, "head", 1), 2
     held = {i: mixes[i] for i in range(1, pairs) if mixes[i] is not None and i % 2 == 0}
     held, got, after = lax.optimization_barrier((held, got, pair_half))
     near, far, reach = rotated(pair_half, -2), rotated(pair_half, -4), 4
@@ -494,27 +503,24 @@
         if mixes[step] is None:
             held[step] = mixes[step] = swapped(held[step ^ low], "seq", 2 * low)
 
+    gathered = [*even_blocks, got]
+    parts = []
+    for i in range(len(even_blocks)):
+        parts += [(i, 0), (len(even_blocks), (blocks + i) * piece)]
     while blocks > 1:
-        for c in range(mask):
-            parts.append((len(gathered), (blocks + c) * piece))
-        gathered.append(got)
         blocks //= 2
-        mask *= 2
         keep, send = kernel_call(
             functools.partial(halve_body, 2 * blocks, piece),
             [
                 jax.ShapeDtypeStruct((blocks * piece, shard), F32),
-                jax.ShapeDtypeStruct((blocks * piece + mask * piece, shard), BF16),
+                jax.ShapeDtypeStruct((blocks * piece, shard), BF16),
             ],
-            (keep, got, so_far),
+            (keep, got),
             0.5,
             "halve",
         )
-        so_far = send[blocks * piece :]
         got = swapped(send, "head", mask)
-    for c in range(mask):
-        parts.append((len(gathered), (blocks + c) * piece))
-    gathered.append(got)
+        mask *= 2
     layer_out = (keep + got[:piece].astype(F32)).astype(BF16)
     if not square:
         cot_full = lax.all_gather(out_grad, "head", axis=1, tiled=True)
@@ -532,7 +538,7 @@
             jax.ShapeDtypeStruct((pair_rows // 2, features), BF16),
         ],
         (place, *gathered, *mixes),
-        1.5,
+        PAIR_US,
         "pair_grad",
         smem=(0,),
         scratch=[

time: 62 us -> 59.6 us (0.961)
  waiting for transfers between devices: 24.2 us -> 21.2 us
  starting transfers between devices: 20.3 us -> 22.5 us
  Pallas kernels: 13.1 us -> 11.4 us
    ppermute x11 -> x12, waiting for transfers between devices: 17 us -> 12.9 us  [swapped(): return lax.ppermute(value, axis, [(i, i ^ mask) for i in range(devices)])]
    pallas_call x11, Pallas kernels: 13.1 us -> 11.4 us  [kernel_call(): pl.pallas_call(body, out_shape=out_shape, in_specs=[pl.BlockSpec(memory_s...]
    ppermute x11 -> x12, starting transfers between devices: 11.4 us -> 12.9 us  [swapped(): return lax.ppermute(value, axis, [(i, i ^ mask) for i in range(devices)])]
    ppermute x5, waiting for transfers between devices: 7.22 us -> 8.26 us  [rotated(): lax.ppermute(value, 'seq', [(i, (i + by) % devices) for i in range(device...]
    ppermute x5, starting transfers between devices: 8.07 us -> 8.79 us  [rotated(): lax.ppermute(value, 'seq', [(i, (i + by) % devices) for i in range(device...]
  transfers between devices with their start and end apart: 17 -> 18, of which waited for: 8 -> 8; matrix products, arithmetic and copies ran while one was open for 1% -> 1% of each run, Pallas kernels for 20% -> 19%
where the time goes in v4:
time: 59.6 us; the launch traced here: 59.5 us
  starting transfers between devices  22.5 us (38%)
  waiting for transfers between devices  21.2 us (36%)
  Pallas kernels  11.4 us (19%)
  other arithmetic  3.54 us (6%)
  between operations  0.76 us (1%)
    ppermute x12, starting transfers between devices, swapped(): return lax.ppermute(value, axis, [(i, i ^ mask) for i in range(devices)])  12.9 us
    ppermute x12, waiting for transfers between devices, swapped(): return lax.ppermute(value, axis, [(i, i ^ mask) for i in range(devices)])  12.9 us
    pallas_call x11, Pallas kernels, kernel_call(): pl.pallas_call(body, out_shape=out_shape, in_specs=[pl.BlockSpec(memory_s...  11.4 us
    ppermute x5, starting transfers between devices, rotated(): lax.ppermute(value, 'seq', [(i, (i + by) % devices) for i in range(device...  8.79 us
    ppermute x5, waiting for transfers between devices, rotated(): lax.ppermute(value, 'seq', [(i, (i + by) % devices) for i in range(device...  8.26 us
    add x1, other arithmetic, joined_inputs(): total += jnp.pad(part, ((0, LABEL_ROWS), (i * features, width - (i + 1) *...  1.21 us
  transfers between devices with their start and end apart: 18, of which 8 were waited for; matrix products, arithmetic and copies ran while one was open for 1% of the time, Pallas kernels for 19%

profile of v4, /device:TPU:0, one launch (start us, length us, event | category | flops | bytes accessed | tf_op | source)
XLA Modules:
  0.0 59.5 jit_solution(14492627995404126741)
XLA Ops:
  0.6 0.7 %convert_bitcast_fusion = bf16[1,128]{1,0:T(2,128)(2,1)S(1)} fusion(s32[128]{0:T(128)} %param.13), kind=kLoop, calls=%fused_computation.4 | loop fusion | flops 128 | bytes 768 | tf_op jit(solution)/shard_map/convert_element_type | solution.py:373
  1.3 1.2 %pad_add_fusion.rows_ref = bf16[144,1536]{1,0:T(8,128)(2,1)S(1)} fusion(bf16[128,512]{1,0:T(8,128)(2,1)} %param.7, bf16[128,512]{1,0:T(8,128)(2,1)} %param.9, bf16[128,512]{1,0:T(8,128)(2,1)} %param.8, bf16[1,128]{1,0:T(2,128)(2,1)S(1)} %convert_bitcast_fusion), kind=kLoop, calls=%fused_computation.1 | loop fusion | flops 1769472 | bytes 835840 | tf_op jit(solution)/shard_map/add | solution.py:376
  2.5 0.3 tail_states.1
  2.9 3.0 %collective-permute-start = (bf16[800,128]{1,0:T(8,128)(2,1)S(1)}, bf16[800,128]{1,0:T(8,128)(2,1)S(1)}, u32[]{:S(2)}, u32[]{:S(2)}) collective-permute-start(bf16[800,128]{1,0:T(8,128)(2,1)S(1)} %tail_states.1), channel_id=1, source_target_pairs={{0,4},{4,8},{8,12},{12,16},{16,20},{20,24},{24,28},{28,0},{1,5},{5... | collective-permute-start | bytes 614408 | tf_op jit(solution)/shard_map/ppermute | solution.py:360
  5.9 1.6 %collective-permute-start.1 = (bf16[800,128]{1,0:T(8,128)(2,1)S(1)}, bf16[800,128]{1,0:T(8,128)(2,1)S(1)}, u32[]{:S(2)}, u32[]{:S(2)}) collective-permute-start(bf16[800,128]{1,0:T(8,128)(2,1)S(1)} %tail_states.1), channel_id=1, source_target_pairs={{0,8},{4,12},{8,16},{12,20},{16,24},{20,28},{24,0},{28,4},{1,9},{5... | collective-permute-start | bytes 614408 | tf_op jit(solution)/shard_map/ppermute | solution.py:360
  7.5 0.0 collective-permute-start.2
  7.5 1.5 %collective-permute-start.3 = (bf16[128,512]{1,0:T(8,128)(2,1)S(1)}, bf16[128,512]{1,0:T(8,128)(2,1)S(1)}, u32[]{:S(2)}, u32[]{:S(2)}) collective-permute-start(bf16[128,512]{1,0:T(8,128)(2,1)S(1)} %copy-done.1), channel_id=1, source_target_pairs={{0,2},{1,3},{2,0},{3,1},{4,6},{5,7},{6,4},{7,5},{8,10},{9,11},{10,... | collective-permute-start | bytes 393224 | tf_op jit(solution)/shard_map/ppermute | solution.py:365
  9.0 0.4 collective-permute-start.4
  9.4 0.0 collective-permute-done.2.refs_1_
  9.4 4.4 %collective-permute-done.3.refs_2_ = bf16[128,512]{1,0:T(8,128)(2,1)S(1)} collective-permute-done((bf16[128,512]{1,0:T(8,128)(2,1)S(1)}, bf16[128,512]{1,0:T(8,128)(2,1)S(1)}, u32[]{:S(2)}, u32[]{:S(2)}) %collective-permute-start.3) | collective-permute-done | bytes 131104 | tf_op jit(solution)/shard_map/ppermute | solution.py:365
  13.8 2.1 %collective-permute-done.4.refs_3_ = bf16[128,512]{1,0:T(8,128)(2,1)} collective-permute-done((bf16[128,512]{1,0:T(8,128)(2,1)S(1)}, bf16[128,512]{1,0:T(8,128)(2,1)}, u32[]{:S(2)}, u32[]{:S(2)}) %collective-permute-start.4) | collective-permute-done | bytes 131104 | tf_op jit(solution)/shard_map/ppermute | solution.py:365
  15.9 0.0 collective-permute-done.near_ref
  15.9 0.0 collective-permute-done.1.far_ref
  15.9 0.1 join_states.2.near_ref
  16.0 1.6 %collective-permute-start.5 = (bf16[800,128]{1,0:T(8,128)(2,1)S(1)}, bf16[800,128]{1,0:T(8,128)(2,1)S(1)}, u32[]{:S(2)}, u32[]{:S(2)}) collective-permute-start(bf16[800,128]{1,0:T(8,128)(2,1)S(1)} %join_states.2.near_ref), channel_id=1, source_target_pairs={{0,8},{4,12},{8,16},{12,20},{16,24},{20,28},{24,0},{28,4},{1,9},{5... | collective-permute-start | bytes 614408 | tf_op jit(solution)/shard_map/ppermute | solution.py:360
  17.6 0.1 pad_add_fusion.1.place_ref
  17.7 0.8 %collective-permute-start.6 = (bf16[128,512]{1,0:T(8,128)(2,1)S(1)}, bf16[128,512]{1,0:T(8,128)(2,1)S(1)}, u32[]{:S(2)}, u32[]{:S(2)}) collective-permute-start(bf16[128,512]{1,0:T(8,128)(2,1)S(1)} %copy-done.1), channel_id=1, source_target_pairs={{0,0},{1,8},{2,16},{3,24},{4,4},{5,12},{6,20},{7,28},{8,1},{9,9},{... | collective-permute-start | bytes 393224 | tf_op jit(solution)/shard_map/ppermute | solution.py:428
  18.5 1.7 %cotangent.1.cot_ref = bf16[128,512]{1,0:T(8,128)(2,1)S(1)} custom-call(s32[2]{0:T(128)S(1)} %pad_add_fusion.1.place_ref, bf16[128,512]{1,0:T(8,128)(2,1)S(1)} %copy-done.1, bf16[128,512]{1,0:T(8,128)(2,1)S(1)} %collective-permute-done.2.refs_1_, bf16[128,512]{1,0:T(8,128)(2,1)S(1)} %collective-permute-done.3.refs_2_, ...), custom_call_target="tpu_custom_call" | custom-call | flops 1500000000 | bytes 2752520 | tf_op jit(solution)/shard_map/cotangent/pallas_call | solution.py:40
  20.3 4.9 %collective-permute-done.5.far_ref = bf16[800,128]{1,0:T(8,128)(2,1)S(1)} collective-permute-done((bf16[800,128]{1,0:T(8,128)(2,1)S(1)}, bf16[800,128]{1,0:T(8,128)(2,1)S(1)}, u32[]{:S(2)}, u32[]{:S(2)}) %collective-permute-start.5) | collective-permute-done | bytes 204832 | tf_op jit(solution)/shard_map/ppermute | solution.py:360
  25.2 3.8 %solve.1 = (bf16[128,512]{1,0:T(8,128)(2,1)S(1)}, bf16[128,512]{1,0:T(8,128)(2,1)}, bf16[128,512]{1,0:T(8,128)(2,1)S(1)}, bf16[800,128]{1,0:T(8,128)(2,1)S(1)}) custom-call(f32[4]{0:T(128)S(1)} %copy-done.2, bf16[144,1536]{1,0:T(8,128)(2,1)S(1)} %pad_add_fusion.rows_ref, bf16[128,512]{1,0:T(8,128)(2,1)S(1)} %cotangent.1.cot_ref, ...), custom_call_target="tpu_custom_call" | custom-call | flops 5000000000 | bytes 1581072 | tf_op jit(solution)/shard_map/solve/pallas_call | solution.py:40
  29.0 0.0 collective-permute-done.6.refs_0_
  29.0 3.2 %collective-permute-start.7 = (bf16[128,512]{1,0:T(8,128)(2,1)S(1)}, bf16[128,512]{1,0:T(8,128)(2,1)S(1)}, u32[]{:S(2)}, u32[]{:S(2)}) collective-permute-start(bf16[128,512]{1,0:T(8,128)(2,1)S(1)} %collective-permute-done.6.refs_0_), channel_id=1, source_target_pairs={{0,2},{1,3},{2,0},{3,1},{4,6},{5,7},{6,4},{7,5},{8,10},{9,11},{10,... | collective-permute-start | bytes 393224 | tf_op jit(solution)/shard_map/ppermute | solution.py:365
  32.2 2.1 %collective-permute-start.10 = (bf16[800,128]{1,0:T(8,128)(2,1)S(1)}, bf16[800,128]{1,0:T(8,128)(2,1)S(1)}, u32[]{:S(2)}, u32[]{:S(2)}) collective-permute-start(bf16[800,128]{1,0:T(8,128)(2,1)S(1)} %get-tuple-element.45.here_ref), channel_id=1, source_target_pairs={{0,4},{4,0},{8,12},{12,8},{16,20},{20,16},{24,28},{28,24},{1,5},{5... | collective-permute-start | bytes 614408 | tf_op jit(solution)/shard_map/ppermute | solution.py:365
  34.2 0.4 collective-permute-start.8
  34.7 0.1 collective-permute-start.15
  34.7 0.4 collective-permute-done.7.refs_1_
  35.1 1.0 %project.1 = (f32[256,512]{1,0:T(8,128)S(1)}, bf16[512,512]{1,0:T(8,128)(2,1)S(1)}) custom-call(s32[2]{0:T(128)S(1)} %pad_add_fusion.1.place_ref, bf16[128,512]{1,0:T(8,128)(2,1)S(1)} %get-tuple-element.41.mixed_ref.refs_3_, bf16[512,2048]{1,0:T(8,128)(2,1)S(1)} %copy-done, bf16[128,512]{1,0:T(8,128)(2,1)S(1)} %collective-permute-done.6.refs_0_, ...), custom_call_target="tpu_custom_call" | custom-call | flops 1000000000 | bytes 3538952 | tf_op jit(solution)/shard_map/project/pallas_call | solution.py:40
  36.1 0.0 copy-start.3
  36.1 0.1 collective-permute-start.9
  36.2 1.8 %collective-permute-done.10.there_ref = bf16[800,128]{1,0:T(8,128)(2,1)S(1)} collective-permute-done((bf16[800,128]{1,0:T(8,128)(2,1)S(1)}, bf16[800,128]{1,0:T(8,128)(2,1)S(1)}, u32[]{:S(2)}, u32[]{:S(2)}) %collective-permute-start.10) | collective-permute-done | bytes 204832 | tf_op jit(solution)/shard_map/ppermute | solution.py:365
  38.0 0.6 %pair_join.1.refs_0_ = bf16[400,128]{1,0:T(8,128)(2,1)S(1)} custom-call(s32[2]{0:T(128)S(1)} %pad_add_fusion.1.place_ref, bf16[800,128]{1,0:T(8,128)(2,1)S(1)} %get-tuple-element.45.here_ref, bf16[800,128]{1,0:T(8,128)(2,1)S(1)} %collective-permute-done.10.there_ref), custom_call_target="tpu_custom_call" | custom-call | flops 5000000000 | bytes 512008 | tf_op jit(solution)/shard_map/pair_join/pallas_call | solution.py:40
  38.6 1.8 %collective-permute-start.12 = (bf16[400,128]{1,0:T(8,128)(2,1)S(1)}, bf16[400,128]{1,0:T(8,128)(2,1)S(1)}, u32[]{:S(2)}, u32[]{:S(2)}) collective-permute-start(bf16[400,128]{1,0:T(8,128)(2,1)S(1)} %pair_join.1.refs_0_), channel_id=1, source_target_pairs={{0,24},{4,28},{8,0},{12,4},{16,8},{20,12},{24,16},{28,20},{1,25},{... | collective-permute-start | bytes 307208 | tf_op jit(solution)/shard_map/ppermute | solution.py:360
  40.4 0.8 %collective-permute-start.13 = (bf16[400,128]{1,0:T(8,128)(2,1)S(1)}, bf16[400,128]{1,0:T(8,128)(2,1)S(1)}, u32[]{:S(2)}, u32[]{:S(2)}) collective-permute-start(bf16[400,128]{1,0:T(8,128)(2,1)S(1)} %pair_join.1.refs_0_), channel_id=1, source_target_pairs={{0,16},{4,20},{8,24},{12,28},{16,0},{20,4},{24,8},{28,12},{1,17},{... | collective-permute-start | bytes 307208 | tf_op jit(solution)/shard_map/ppermute | solution.py:360
  41.2 1.1 %local_grads.1 = (f32[128,512]{1,0:T(8,128)S(1)}, f32[128,512]{1,0:T(8,128)S(1)}) custom-call(bf16[144,1536]{1,0:T(8,128)(2,1)S(1)} %pad_add_fusion.rows_ref, bf16[128,512]{1,0:T(8,128)(2,1)S(1)} %cotangent.1.cot_ref, bf16[128,512]{1,0:T(8,128)(2,1)S(1)} %get-tuple-element.51.sol_ref, bf16[128,512]{1,0:T(8,128)(2,1)S(1)} %copy-done.3), custom_call_target="tpu_custom_call" | custom-call | flops 1100000000 | bytes 1359872 | tf_op jit(solution)/shard_map/local_grads/pallas_call | solution.py:40
  42.3 0.0 collective-permute-done.9.got_ref.refs_2_
  42.3 0.1 halve.1
  42.3 0.6 collective-permute-start.11
  42.9 1.9 %collective-permute-start.16 = (bf16[128,512]{1,0:T(8,128)(2,1)S(1)}, bf16[128,512]{1,0:T(8,128)(2,1)S(1)}, u32[]{:S(2)}, u32[]{:S(2)}) collective-permute-start(bf16[128,512]{1,0:T(8,128)(2,1)S(1)} %collective-permute-done.8.refs_5_), channel_id=1, source_target_pairs={{0,8},{4,12},{8,0},{12,4},{16,24},{20,28},{24,16},{28,20},{1,9},{5... | collective-permute-start | bytes 393224 | tf_op jit(solution)/shard_map/ppermute | solution.py:365
  44.9 0.0 collective-permute-done.12.near_ref
  44.9 3.3 %collective-permute-done.13.far_ref = bf16[400,128]{1,0:T(8,128)(2,1)S(1)} collective-permute-done((bf16[400,128]{1,0:T(8,128)(2,1)S(1)}, bf16[400,128]{1,0:T(8,128)(2,1)S(1)}, u32[]{:S(2)}, u32[]{:S(2)}) %collective-permute-start.13) | collective-permute-done | bytes 102432 | tf_op jit(solution)/shard_map/ppermute | solution.py:360
  48.3 1.6 %collective-permute-start.14 = (bf16[400,128]{1,0:T(8,128)(2,1)S(1)}, bf16[400,128]{1,0:T(8,128)(2,1)S(1)}, u32[]{:S(2)}, u32[]{:S(2)}) collective-permute-start(bf16[400,128]{1,0:T(8,128)(2,1)S(1)} %join_states.3.mine_ref), channel_id=1, source_target_pairs={{0,4},{4,0},{8,12},{12,8},{16,20},{20,16},{24,28},{28,24},{1,5},{5... | collective-permute-start | bytes 307208 | tf_op jit(solution)/shard_map/ppermute | solution.py:365
  49.8 1.2 %pair_grad.1 = (f32[256,512]{1,0:T(8,128)S(1)}, bf16[256,512]{1,0:T(8,128)(2,1)S(1)}) custom-call(s32[2]{0:T(128)S(1)} %pad_add_fusion.1.place_ref, bf16[128,512]{1,0:T(8,128)(2,1)S(1)} %collective-permute-done.6.refs_0_, bf16[128,512]{1,0:T(8,128)(2,1)S(1)} %collective-permute-done.7.refs_1_, bf16[512,512]{1,0:T(8,128)(2,1)S(1)} %collective-permute-done.9.got_ref.refs_2_, ...), custom_call_target="tpu_custom_call" | custom-call | flops 1500000000 | bytes 2097160 | tf_op jit(solution)/shard_map/pair_grad/pallas_call | solution.py:40
  51.0 1.1 %collective-permute-start.17 = (bf16[256,512]{1,0:T(8,128)(2,1)S(1)}, bf16[256,512]{1,0:T(8,128)(2,1)S(1)}, u32[]{:S(2)}, u32[]{:S(2)}) collective-permute-start(bf16[256,512]{1,0:T(8,128)(2,1)S(1)} %get-tuple-element.58), channel_id=1, source_target_pairs={{0,4},{4,0},{8,12},{12,8},{16,20},{20,16},{24,28},{28,24},{1,5},{5... | collective-permute-start | bytes 786440 | tf_op jit(solution)/shard_map/ppermute | solution.py:365
  52.2 1.3 %collective-permute-done.14.theirs_ref = bf16[400,128]{1,0:T(8,128)(2,1)S(1)} collective-permute-done((bf16[400,128]{1,0:T(8,128)(2,1)S(1)}, bf16[400,128]{1,0:T(8,128)(2,1)S(1)}, u32[]{:S(2)}, u32[]{:S(2)}) %collective-permute-start.14) | collective-permute-done | bytes 102432 | tf_op jit(solution)/shard_map/ppermute | solution.py:365
  53.5 1.6 %final_grads.1 = (bf16[128,512]{1,0:T(8,128)(2,1)}, bf16[128,512]{1,0:T(8,128)(2,1)}) custom-call(s32[2]{0:T(128)S(1)} %pad_add_fusion.1.place_ref, bf16[144,1536]{1,0:T(8,128)(2,1)S(1)} %pad_add_fusion.rows_ref, bf16[800,128]{1,0:T(8,128)(2,1)S(1)} %collective-permute-done.10.there_ref, bf16[400,128]{1,0:T(8,128)(2,1)S(1)} %join_states.3.mine_ref, ...), custom_call_target="tpu_custom_call" | custom-call | flops 1000000000 | bytes 1638408 | tf_op jit(solution)/shard_map/final_grads/pallas_call | solution.py:40
  55.0 0.7 %add_convert_fusion = bf16[128,512]{1,0:T(8,128)(2,1)} fusion(f32[128,512]{1,0:T(8,128)S(1)} %get-tuple-element.47, bf16[128,512]{1,0:T(8,128)(2,1)S(1)} %collective-permute-done.11), kind=kLoop, calls=%fused_computation.2 | loop fusion | flops 196608 | bytes 524288 | tf_op jit(solution)/shard_map/convert_element_type | solution.py:524
  55.7 2.9 %collective-permute-done.17 = bf16[256,512]{1,0:T(8,128)(2,1)S(1)} collective-permute-done((bf16[256,512]{1,0:T(8,128)(2,1)S(1)}, bf16[256,512]{1,0:T(8,128)(2,1)S(1)}, u32[]{:S(2)}, u32[]{:S(2)}) %collective-permute-start.17) | collective-permute-done | bytes 262176 | tf_op jit(solution)/shard_map/ppermute | solution.py:365
  58.6 0.9 %convert_add_fusion = f32[256,512]{1,0:T(8,128)} fusion(f32[256,512]{1,0:T(8,128)S(1)} %get-tuple-element.57, bf16[256,512]{1,0:T(8,128)(2,1)S(1)} %collective-permute-done.17), kind=kLoop, calls=%fused_computation | loop fusion | flops 262144 | bytes 1310720 | tf_op jit(solution)/shard_map/add | solution.py:550
  (12 shorter events, 0.1 us)
Async XLA Ops:
  0.6 6.9 %copy-start.1 = (bf16[128,512]{1,0:T(8,128)(2,1)S(1)}, bf16[128,512]{1,0:T(8,128)(2,1)}, u32[]{:S(2)}) copy-start(bf16[128,512]{1,0:T(8,128)(2,1)} %refs_0_) | copy-start | bytes 393220
  1.3 17.2 %copy-start = (bf16[512,2048]{1,0:T(8,128)(2,1)S(1)}, bf16[512,2048]{1,0:T(8,128)(2,1)}, u32[]{:S(2)}) copy-start(bf16[512,2048]{1,0:T(8,128)(2,1)} %weight_ref.1) | copy-start | bytes 6291460
  2.9 13.0 %collective-permute-start = (bf16[800,128]{1,0:T(8,128)(2,1)S(1)}, bf16[800,128]{1,0:T(8,128)(2,1)S(1)}, u32[]{:S(2)}, u32[]{:S(2)}) collective-permute-start(bf16[800,128]{1,0:T(8,128)(2,1)S(1)} %tail_states.1), channel_id=1, source_target_pairs={{0,4},{4,8},{8,12},{12,16},{16,20},{20,24},{24,28},{28,0},{1,5},{5... | collective-permute-start | bytes 614408 | tf_op jit(solution)/shard_map/ppermute | solution.py:360
  5.9 10.0 %collective-permute-start.1 = (bf16[800,128]{1,0:T(8,128)(2,1)S(1)}, bf16[800,128]{1,0:T(8,128)(2,1)S(1)}, u32[]{:S(2)}, u32[]{:S(2)}) collective-permute-start(bf16[800,128]{1,0:T(8,128)(2,1)S(1)} %tail_states.1), channel_id=1, source_target_pairs={{0,8},{4,12},{8,16},{12,20},{16,24},{20,28},{24,0},{28,4},{1,9},{5... | collective-permute-start | bytes 614408 | tf_op jit(solution)/shard_map/ppermute | solution.py:360
  7.5 1.9 %collective-permute-start.2 = (bf16[128,512]{1,0:T(8,128)(2,1)S(1)}, bf16[128,512]{1,0:T(8,128)(2,1)S(1)}, u32[]{:S(2)}, u32[]{:S(2)}) collective-permute-start(bf16[128,512]{1,0:T(8,128)(2,1)S(1)} %copy-done.1), channel_id=1, source_target_pairs={{0,1},{1,0},{2,3},{3,2},{4,5},{5,4},{6,7},{7,6},{8,9},{9,8},{10,11... | collective-permute-start | bytes 393224 | tf_op jit(solution)/shard_map/ppermute | solution.py:365
  7.5 6.3 %collective-permute-start.3 = (bf16[128,512]{1,0:T(8,128)(2,1)S(1)}, bf16[128,512]{1,0:T(8,128)(2,1)S(1)}, u32[]{:S(2)}, u32[]{:S(2)}) collective-permute-start(bf16[128,512]{1,0:T(8,128)(2,1)S(1)} %copy-done.1), channel_id=1, source_target_pairs={{0,2},{1,3},{2,0},{3,1},{4,6},{5,7},{6,4},{7,5},{8,10},{9,11},{10,... | collective-permute-start | bytes 393224 | tf_op jit(solution)/shard_map/ppermute | solution.py:365
  9.0 6.9 %collective-permute-start.4 = (bf16[128,512]{1,0:T(8,128)(2,1)S(1)}, bf16[128,512]{1,0:T(8,128)(2,1)}, u32[]{:S(2)}, u32[]{:S(2)}) collective-permute-start(bf16[128,512]{1,0:T(8,128)(2,1)S(1)} %copy-done.1), channel_id=1, source_target_pairs={{0,3},{1,2},{2,1},{3,0},{4,7},{5,6},{6,5},{7,4},{8,11},{9,10},{10,... | collective-permute-start | bytes 393224 | tf_op jit(solution)/shard_map/ppermute | solution.py:365
  16.0 9.2 %collective-permute-start.5 = (bf16[800,128]{1,0:T(8,128)(2,1)S(1)}, bf16[800,128]{1,0:T(8,128)(2,1)S(1)}, u32[]{:S(2)}, u32[]{:S(2)}) collective-permute-start(bf16[800,128]{1,0:T(8,128)(2,1)S(1)} %join_states.2.near_ref), channel_id=1, source_target_pairs={{0,8},{4,12},{8,16},{12,20},{16,24},{20,28},{24,0},{28,4},{1,9},{5... | collective-permute-start | bytes 614408 | tf_op jit(solution)/shard_map/ppermute | solution.py:360
  17.7 7.5 %copy-start.2 = (f32[4]{0:T(128)S(1)}, f32[4]{0:T(128)}, u32[]{:S(2)}) copy-start(f32[4]{0:T(128)} %ridge_ref.1) | copy-start | bytes 52
  17.7 11.3 %collective-permute-start.6 = (bf16[128,512]{1,0:T(8,128)(2,1)S(1)}, bf16[128,512]{1,0:T(8,128)(2,1)S(1)}, u32[]{:S(2)}, u32[]{:S(2)}) collective-permute-start(bf16[128,512]{1,0:T(8,128)(2,1)S(1)} %copy-done.1), channel_id=1, source_target_pairs={{0,0},{1,8},{2,16},{3,24},{4,4},{5,12},{6,20},{7,28},{8,1},{9,9},{... | collective-permute-start | bytes 393224 | tf_op jit(solution)/shard_map/ppermute | solution.py:428
  29.0 6.1 %collective-permute-start.7 = (bf16[128,512]{1,0:T(8,128)(2,1)S(1)}, bf16[128,512]{1,0:T(8,128)(2,1)S(1)}, u32[]{:S(2)}, u32[]{:S(2)}) collective-permute-start(bf16[128,512]{1,0:T(8,128)(2,1)S(1)} %collective-permute-done.6.refs_0_), channel_id=1, source_target_pairs={{0,2},{1,3},{2,0},{3,1},{4,6},{5,7},{6,4},{7,5},{8,10},{9,11},{10,... | collective-permute-start | bytes 393224 | tf_op jit(solution)/shard_map/ppermute | solution.py:365
  32.2 5.8 %collective-permute-start.10 = (bf16[800,128]{1,0:T(8,128)(2,1)S(1)}, bf16[800,128]{1,0:T(8,128)(2,1)S(1)}, u32[]{:S(2)}, u32[]{:S(2)}) collective-permute-start(bf16[800,128]{1,0:T(8,128)(2,1)S(1)} %get-tuple-element.45.here_ref), channel_id=1, source_target_pairs={{0,4},{4,0},{8,12},{12,8},{16,20},{20,16},{24,28},{28,24},{1,5},{5... | collective-permute-start | bytes 614408 | tf_op jit(solution)/shard_map/ppermute | solution.py:365
  34.2 8.0 %collective-permute-start.8 = (bf16[128,512]{1,0:T(8,128)(2,1)S(1)}, bf16[128,512]{1,0:T(8,128)(2,1)S(1)}, u32[]{:S(2)}, u32[]{:S(2)}) collective-permute-start(bf16[128,512]{1,0:T(8,128)(2,1)S(1)} %get-tuple-element.41.mixed_ref.refs_3_), channel_id=1, source_target_pairs={{0,16},{4,20},{8,24},{12,28},{16,0},{20,4},{24,8},{28,12},{1,17},{... | collective-permute-start | bytes 393224 | tf_op jit(solution)/shard_map/ppermute | solution.py:365
  34.7 15.2 %collective-permute-start.15 = (bf16[128,512]{1,0:T(8,128)(2,1)S(1)}, bf16[128,512]{1,0:T(8,128)(2,1)S(1)}, u32[]{:S(2)}, u32[]{:S(2)}) collective-permute-start(bf16[128,512]{1,0:T(8,128)(2,1)S(1)} %get-tuple-element.41.mixed_ref.refs_3_), channel_id=1, source_target_pairs={{0,8},{4,12},{8,0},{12,4},{16,24},{20,28},{24,16},{28,20},{1,9},{5... | collective-permute-start | bytes 393224 | tf_op jit(solution)/shard_map/ppermute | solution.py:365
  36.1 5.0 %copy-start.3 = (bf16[128,512]{1,0:T(8,128)(2,1)S(1)}, bf16[128,512]{1,0:T(8,128)(2,1)}, u32[]{:S(2)}) copy-start(bf16[128,512]{1,0:T(8,128)(2,1)} %get-tuple-element.28.dual_ref) | copy-start | bytes 393220
  36.1 6.1 %collective-permute-start.9 = (bf16[512,512]{1,0:T(8,128)(2,1)S(1)}, bf16[512,512]{1,0:T(8,128)(2,1)S(1)}, u32[]{:S(2)}, u32[]{:S(2)}) collective-permute-start(bf16[512,512]{1,0:T(8,128)(2,1)S(1)} %get-tuple-element.44), channel_id=1, source_target_pairs={{0,1},{1,0},{2,3},{3,2},{4,5},{5,4},{6,7},{7,6},{8,9},{9,8},{10,11... | collective-permute-start | bytes 1572872 | tf_op jit(solution)/shard_map/ppermute | solution.py:365
  38.6 6.3 %collective-permute-start.12 = (bf16[400,128]{1,0:T(8,128)(2,1)S(1)}, bf16[400,128]{1,0:T(8,128)(2,1)S(1)}, u32[]{:S(2)}, u32[]{:S(2)}) collective-permute-start(bf16[400,128]{1,0:T(8,128)(2,1)S(1)} %pair_join.1.refs_0_), channel_id=1, source_target_pairs={{0,24},{4,28},{8,0},{12,4},{16,8},{20,12},{24,16},{28,20},{1,25},{... | collective-permute-start | bytes 307208 | tf_op jit(solution)/shard_map/ppermute | solution.py:360
  40.4 7.8 %collective-permute-start.13 = (bf16[400,128]{1,0:T(8,128)(2,1)S(1)}, bf16[400,128]{1,0:T(8,128)(2,1)S(1)}, u32[]{:S(2)}, u32[]{:S(2)}) collective-permute-start(bf16[400,128]{1,0:T(8,128)(2,1)S(1)} %pair_join.1.refs_0_), channel_id=1, source_target_pairs={{0,16},{4,20},{8,24},{12,28},{16,0},{20,4},{24,8},{28,12},{1,17},{... | collective-permute-start | bytes 307208 | tf_op jit(solution)/shard_map/ppermute | solution.py:360
  42.3 12.7 %collective-permute-start.11 = (bf16[128,512]{1,0:T(8,128)(2,1)S(1)}, bf16[128,512]{1,0:T(8,128)(2,1)S(1)}, u32[]{:S(2)}, u32[]{:S(2)}) collective-permute-start(bf16[128,512]{1,0:T(8,128)(2,1)S(1)} %get-tuple-element.48), channel_id=1, source_target_pairs={{0,2},{1,3},{2,0},{3,1},{4,6},{5,7},{6,4},{7,5},{8,10},{9,11},{10,... | collective-permute-start | bytes 393224 | tf_op jit(solution)/shard_map/ppermute | solution.py:365
  42.9 6.9 %collective-permute-start.16 = (bf16[128,512]{1,0:T(8,128)(2,1)S(1)}, bf16[128,512]{1,0:T(8,128)(2,1)S(1)}, u32[]{:S(2)}, u32[]{:S(2)}) collective-permute-start(bf16[128,512]{1,0:T(8,128)(2,1)S(1)} %collective-permute-done.8.refs_5_), channel_id=1, source_target_pairs={{0,8},{4,12},{8,0},{12,4},{16,24},{20,28},{24,16},{28,20},{1,9},{5... | collective-permute-start | bytes 393224 | tf_op jit(solution)/shard_map/ppermute | solution.py:365
  48.3 5.2 %collective-permute-start.14 = (bf16[400,128]{1,0:T(8,128)(2,1)S(1)}, bf16[400,128]{1,0:T(8,128)(2,1)S(1)}, u32[]{:S(2)}, u32[]{:S(2)}) collective-permute-start(bf16[400,128]{1,0:T(8,128)(2,1)S(1)} %join_states.3.mine_ref), channel_id=1, source_target_pairs={{0,4},{4,0},{8,12},{12,8},{16,20},{20,16},{24,28},{28,24},{1,5},{5... | collective-permute-start | bytes 307208 | tf_op jit(solution)/shard_map/ppermute | solution.py:365
  51.0 7.6 %collective-permute-start.17 = (bf16[256,512]{1,0:T(8,128)(2,1)S(1)}, bf16[256,512]{1,0:T(8,128)(2,1)S(1)}, u32[]{:S(2)}, u32[]{:S(2)}) collective-permute-start(bf16[256,512]{1,0:T(8,128)(2,1)S(1)} %get-tuple-element.58), channel_id=1, source_target_pairs={{0,4},{4,0},{8,12},{12,8},{16,20},{20,16},{24,28},{28,24},{1,5},{5... | collective-permute-start | bytes 786440 | tf_op jit(solution)/shard_map/ppermute | solution.py:365

commit v5 on v4

--- a/solution.py
+++ b/solution.py
@@ -17,7 +17,7 @@
 COT_US = 1.5
 FINAL_US = 1.0
 PAIR_JOIN_US = 5.0
-MINE_US = 6.0
+MINE_US = 12.0
 PAIR_US = 1.5
 HALVE_US = 0.5
 
@@ -236,38 +236,41 @@
     out_ref,
 ):
     piece, across, down = label_grids(rows_ref)
-    same = document_mask(across, down).astype(F32)
+    same = document_mask(across, down).astype(F32).astype(BF16)
     same_two = jnp.concatenate([same, same], axis=0)
     first = jnp.min(across, axis=1, keepdims=True)
     head_rows = (down == first)[:, :width].astype(F32).astype(BF16)
     units = join_units(near_ref[...], far_ref[...], width)
     label, value_states, gram_states = unpack_states(units, heads, width)
-    carried = ((down + 1)[:, :width] == label).astype(F32)
+    carried = ((down + 1)[:, :width] == label).astype(F32).astype(BF16)
     carried_two = jnp.concatenate([carried, carried], axis=0)
     every = range(heads)
     keys = [head_rows_of(rows_ref, heads, width, 0, h) for h in every]
     values = [head_rows_of(rows_ref, heads, width, 1, h) for h in every]
     queries = [head_rows_of(rows_ref, heads, width, 2, h).astype(F32) for h in every]
     cots = [cot_ref[:, h * width : (h + 1) * width] for h in every]
-    boths = [
-        mm(cots[h], jnp.concatenate([values[h].T, value_states[h]], axis=1)) for h in every
+    keys_across = [key.T for key in keys]
+    scores = [mm(cots[h], values[h].T).astype(BF16) * same for h in every]
+    targets = [
+        mm(
+            jnp.concatenate([scores[h], cots[h] * carried], axis=1),
+            jnp.concatenate([keys[h], value_states[h]], axis=0),
+        )
+        for h in every
     ]
-    scores = [(both[:, :piece] * same).astype(BF16) for both in boths]
-    targets = [carried * boths[h][:, piece:] + mm(scores[h], keys[h]) for h in every]
-    rhs_keys = [jnp.concatenate([keys[h].T, gram_states[h]], axis=1) for h in every]
+    systems = [jnp.concatenate([keys[h], gram_states[h]], axis=0) for h in every]
     directions = [jnp.concatenate([queries[h], targets[h]], axis=0) for h in every]
     residuals = directions
     solutions = [jnp.zeros_like(start) for start in directions]
     squares = [jnp.sum(start * start, axis=1, keepdims=True) for start in directions]
     for step in range(CG_STEPS):
         ps = directions
-        boths = [mm(ps[h].astype(BF16), rhs_keys[h]) for h in range(heads)]
-        scores = [(both[:, :piece] * same_two).astype(BF16) for both in boths]
-        locals_ = [mm(scores[h], keys[h]) for h in range(heads)]
-        applied = [
-            carried_two * boths[h][:, piece:] + locals_[h] + ridge_ref[h] * ps[h]
-            for h in range(heads)
+        rounded = [p.astype(BF16) for p in ps]
+        scores = [mm(rounded[h], keys_across[h]).astype(BF16) * same_two for h in every]
+        lefts = [
+            jnp.concatenate([scores[h], rounded[h] * carried_two], axis=1) for h in every
         ]
+        applied = [mm(lefts[h], systems[h]) + ridge_ref[h] * ps[h] for h in every]
         sizes = [squares[h] / (jnp.sum(ps[h] * applied[h], axis=1, keepdims=True) + EPSILON) for h in range(heads)]
         solutions = [solutions[h] + sizes[h] * ps[h] for h in range(heads)]
         if step + 1 < CG_STEPS:
@@ -282,12 +285,14 @@
     masked = [sol * head_rows for sol in sols]
     sums = [mm_tn(cots[h], masked[h]) for h in every]
     crosses = [mm_tn(duals[h], masked[h]) for h in every]
-    boths = [
-        mm(sols[h], jnp.concatenate([rhs_keys[h][:, :piece], value_states[h].T], axis=1))
+    scores = [mm(sols[h], keys_across[h]).astype(BF16) * same for h in every]
+    outputs = [
+        mm(
+            jnp.concatenate([scores[h], sols[h] * carried], axis=1),
+            jnp.concatenate([values[h], value_states[h].T], axis=0),
+        )
         for h in every
     ]
-    scores = [(both[:, :piece] * same).astype(BF16) for both in boths]
-    outputs = [carried * boths[h][:, piece:] + mm(scores[h], values[h]) for h in every]
     for h in every:
         cols = slice(h * width, (h + 1) * width)
         mixed_ref[:, cols] = outputs[h].astype(BF16)
@@ -484,7 +489,7 @@
             jax.ShapeDtypeStruct(((blocks + len(even_blocks)) * piece, shard), BF16),
         ],
         (place, ready, out_weight, *even_blocks),
-        1.0,
+        0.05,
         "project",
         smem=(0,),
     )

time: 59.6 us -> 59.7 us (level)
    ppermute x5, starting transfers between devices: 8.79 us -> 6.98 us  [rotated(): lax.ppermute(value, 'seq', [(i, (i + by) % devices) for i in range(device...]
    ppermute x12, starting transfers between devices: 12.9 us -> 14.6 us  [swapped(): return lax.ppermute(value, axis, [(i, i ^ mask) for i in range(devices)])]
where the time goes in v5:
time: 59.7 us; the launch traced here: 59.5 us
  starting transfers between devices  22.4 us (38%)
  waiting for transfers between devices  21.3 us (36%)
  Pallas kernels  11.5 us (19%)
  other arithmetic  3.53 us (6%)
  between operations  0.77 us (1%)
    ppermute x12, starting transfers between devices, swapped(): return lax.ppermute(value, axis, [(i, i ^ mask) for i in range(devices)])  14.6 us
    ppermute x12, waiting for transfers between devices, swapped(): return lax.ppermute(value, axis, [(i, i ^ mask) for i in range(devices)])  13.2 us
    pallas_call x11, Pallas kernels, kernel_call(): pl.pallas_call(body, out_shape=out_shape, in_specs=[pl.BlockSpec(memory_s...  11.5 us
    ppermute x5, waiting for transfers between devices, rotated(): lax.ppermute(value, 'seq', [(i, (i + by) % devices) for i in range(device...  8.08 us
    ppermute x5, starting transfers between devices, rotated(): lax.ppermute(value, 'seq', [(i, (i + by) % devices) for i in range(device...  6.98 us
    add x1, other arithmetic, joined_inputs(): total += jnp.pad(part, ((0, LABEL_ROWS), (i * features, width - (i + 1) *...  1.21 us
  transfers between devices with their start and end apart: 18, of which 8 were waited for; matrix products, arithmetic and copies ran while one was open for 1% of the time, Pallas kernels for 19%

profile of v5, /device:TPU:0, one launch (start us, length us, event | category | flops | bytes accessed | tf_op | source)
XLA Modules:
  0.0 59.5 jit_solution(17452471154626720057)
XLA Ops:
  0.6 0.7 %convert_bitcast_fusion = bf16[1,128]{1,0:T(2,128)(2,1)S(1)} fusion(s32[128]{0:T(128)} %param.13), kind=kLoop, calls=%fused_computation.4 | loop fusion | flops 128 | bytes 768 | tf_op jit(solution)/shard_map/convert_element_type | solution.py:378
  1.3 1.2 %pad_add_fusion.rows_ref = bf16[144,1536]{1,0:T(8,128)(2,1)S(1)} fusion(bf16[128,512]{1,0:T(8,128)(2,1)} %param.7, bf16[128,512]{1,0:T(8,128)(2,1)} %param.9, bf16[128,512]{1,0:T(8,128)(2,1)} %param.8, bf16[1,128]{1,0:T(2,128)(2,1)S(1)} %convert_bitcast_fusion), kind=kLoop, calls=%fused_computation.1 | loop fusion | flops 1769472 | bytes 835840 | tf_op jit(solution)/shard_map/add | solution.py:381
  2.5 0.3 tail_states.1
  2.9 3.0 %collective-permute-start = (bf16[800,128]{1,0:T(8,128)(2,1)S(1)}, bf16[800,128]{1,0:T(8,128)(2,1)S(1)}, u32[]{:S(2)}, u32[]{:S(2)}) collective-permute-start(bf16[800,128]{1,0:T(8,128)(2,1)S(1)} %tail_states.1), channel_id=1, source_target_pairs={{0,4},{4,8},{8,12},{12,16},{16,20},{20,24},{24,28},{28,0},{1,5},{5... | collective-permute-start | bytes 614408 | tf_op jit(solution)/shard_map/ppermute | solution.py:365
  5.9 1.6 %collective-permute-start.1 = (bf16[800,128]{1,0:T(8,128)(2,1)S(1)}, bf16[800,128]{1,0:T(8,128)(2,1)S(1)}, u32[]{:S(2)}, u32[]{:S(2)}) collective-permute-start(bf16[800,128]{1,0:T(8,128)(2,1)S(1)} %tail_states.1), channel_id=1, source_target_pairs={{0,8},{4,12},{8,16},{12,20},{16,24},{20,28},{24,0},{28,4},{1,9},{5... | collective-permute-start | bytes 614408 | tf_op jit(solution)/shard_map/ppermute | solution.py:365
  7.5 0.0 collective-permute-start.2
  7.5 1.5 %collective-permute-start.3 = (bf16[128,512]{1,0:T(8,128)(2,1)S(1)}, bf16[128,512]{1,0:T(8,128)(2,1)S(1)}, u32[]{:S(2)}, u32[]{:S(2)}) collective-permute-start(bf16[128,512]{1,0:T(8,128)(2,1)S(1)} %copy-done.1), channel_id=1, source_target_pairs={{0,2},{1,3},{2,0},{3,1},{4,6},{5,7},{6,4},{7,5},{8,10},{9,11},{10,... | collective-permute-start | bytes 393224 | tf_op jit(solution)/shard_map/ppermute | solution.py:370
  9.0 0.4 collective-permute-start.4
  9.4 0.0 collective-permute-done.2.refs_1_
  9.4 4.4 %collective-permute-done.3.refs_2_ = bf16[128,512]{1,0:T(8,128)(2,1)S(1)} collective-permute-done((bf16[128,512]{1,0:T(8,128)(2,1)S(1)}, bf16[128,512]{1,0:T(8,128)(2,1)S(1)}, u32[]{:S(2)}, u32[]{:S(2)}) %collective-permute-start.3) | collective-permute-done | bytes 131104 | tf_op jit(solution)/shard_map/ppermute | solution.py:370
  13.8 2.1 %collective-permute-done.4.refs_3_ = bf16[128,512]{1,0:T(8,128)(2,1)} collective-permute-done((bf16[128,512]{1,0:T(8,128)(2,1)S(1)}, bf16[128,512]{1,0:T(8,128)(2,1)}, u32[]{:S(2)}, u32[]{:S(2)}) %collective-permute-start.4) | collective-permute-done | bytes 131104 | tf_op jit(solution)/shard_map/ppermute | solution.py:370
  15.9 0.0 collective-permute-done.near_ref
  15.9 0.0 collective-permute-done.1.far_ref
  15.9 0.1 join_states.2.near_ref
  16.0 1.6 %collective-permute-start.5 = (bf16[800,128]{1,0:T(8,128)(2,1)S(1)}, bf16[800,128]{1,0:T(8,128)(2,1)S(1)}, u32[]{:S(2)}, u32[]{:S(2)}) collective-permute-start(bf16[800,128]{1,0:T(8,128)(2,1)S(1)} %join_states.2.near_ref), channel_id=1, source_target_pairs={{0,8},{4,12},{8,16},{12,20},{16,24},{20,28},{24,0},{28,4},{1,9},{5... | collective-permute-start | bytes 614408 | tf_op jit(solution)/shard_map/ppermute | solution.py:365
  17.6 0.1 pad_add_fusion.1.place_ref
  17.7 0.8 %collective-permute-start.6 = (bf16[128,512]{1,0:T(8,128)(2,1)S(1)}, bf16[128,512]{1,0:T(8,128)(2,1)S(1)}, u32[]{:S(2)}, u32[]{:S(2)}) collective-permute-start(bf16[128,512]{1,0:T(8,128)(2,1)S(1)} %copy-done.1), channel_id=1, source_target_pairs={{0,0},{1,8},{2,16},{3,24},{4,4},{5,12},{6,20},{7,28},{8,1},{9,9},{... | collective-permute-start | bytes 393224 | tf_op jit(solution)/shard_map/ppermute | solution.py:433
  18.5 1.7 %cotangent.1.cot_ref = bf16[128,512]{1,0:T(8,128)(2,1)S(1)} custom-call(s32[2]{0:T(128)S(1)} %pad_add_fusion.1.place_ref, bf16[128,512]{1,0:T(8,128)(2,1)S(1)} %copy-done.1, bf16[128,512]{1,0:T(8,128)(2,1)S(1)} %collective-permute-done.2.refs_1_, bf16[128,512]{1,0:T(8,128)(2,1)S(1)} %collective-permute-done.3.refs_2_, ...), custom_call_target="tpu_custom_call" | custom-call | flops 1500000000 | bytes 2752520 | tf_op jit(solution)/shard_map/cotangent/pallas_call | solution.py:40
  20.3 4.9 %collective-permute-done.5.far_ref = bf16[800,128]{1,0:T(8,128)(2,1)S(1)} collective-permute-done((bf16[800,128]{1,0:T(8,128)(2,1)S(1)}, bf16[800,128]{1,0:T(8,128)(2,1)S(1)}, u32[]{:S(2)}, u32[]{:S(2)}) %collective-permute-start.5) | collective-permute-done | bytes 204832 | tf_op jit(solution)/shard_map/ppermute | solution.py:365
  25.2 3.9 %solve.1 = (bf16[128,512]{1,0:T(8,128)(2,1)S(1)}, bf16[128,512]{1,0:T(8,128)(2,1)}, bf16[128,512]{1,0:T(8,128)(2,1)S(1)}, bf16[800,128]{1,0:T(8,128)(2,1)S(1)}) custom-call(f32[4]{0:T(128)S(1)} %copy-done.2, bf16[144,1536]{1,0:T(8,128)(2,1)S(1)} %pad_add_fusion.rows_ref, bf16[128,512]{1,0:T(8,128)(2,1)S(1)} %cotangent.1.cot_ref, ...), custom_call_target="tpu_custom_call" | custom-call | flops 5000000000 | bytes 1581072 | tf_op jit(solution)/shard_map/solve/pallas_call | solution.py:40
  29.0 3.5 %collective-permute-start.10 = (bf16[800,128]{1,0:T(8,128)(2,1)S(1)}, bf16[800,128]{1,0:T(8,128)(2,1)S(1)}, u32[]{:S(2)}, u32[]{:S(2)}) collective-permute-start(bf16[800,128]{1,0:T(8,128)(2,1)S(1)} %get-tuple-element.45.here_ref), channel_id=1, source_target_pairs={{0,4},{4,0},{8,12},{12,8},{16,20},{20,16},{24,28},{28,24},{1,5},{5... | collective-permute-start | bytes 614408 | tf_op jit(solution)/shard_map/ppermute | solution.py:370
  32.5 0.0 collective-permute-done.6.refs_0_
  32.5 0.0 collective-permute-start.7
  32.5 2.2 %collective-permute-start.8 = (bf16[128,512]{1,0:T(8,128)(2,1)S(1)}, bf16[128,512]{1,0:T(8,128)(2,1)S(1)}, u32[]{:S(2)}, u32[]{:S(2)}) collective-permute-start(bf16[128,512]{1,0:T(8,128)(2,1)S(1)} %get-tuple-element.41.mixed_ref.refs_3_), channel_id=1, source_target_pairs={{0,16},{4,20},{8,24},{12,28},{16,0},{20,4},{24,8},{28,12},{1,17},{... | collective-permute-start | bytes 393224 | tf_op jit(solution)/shard_map/ppermute | solution.py:370
  34.7 0.0 collective-permute-start.15
  34.7 2.8 %collective-permute-done.7.refs_1_ = bf16[128,512]{1,0:T(8,128)(2,1)S(1)} collective-permute-done((bf16[128,512]{1,0:T(8,128)(2,1)S(1)}, bf16[128,512]{1,0:T(8,128)(2,1)S(1)}, u32[]{:S(2)}, u32[]{:S(2)}) %collective-permute-start.7) | collective-permute-done | bytes 131104 | tf_op jit(solution)/shard_map/ppermute | solution.py:370
  37.5 1.0 %project.1 = (f32[256,512]{1,0:T(8,128)S(1)}, bf16[512,512]{1,0:T(8,128)(2,1)S(1)}) custom-call(s32[2]{0:T(128)S(1)} %pad_add_fusion.1.place_ref, bf16[128,512]{1,0:T(8,128)(2,1)S(1)} %get-tuple-element.41.mixed_ref.refs_3_, bf16[512,2048]{1,0:T(8,128)(2,1)S(1)} %copy-done, bf16[128,512]{1,0:T(8,128)(2,1)S(1)} %collective-permute-done.6.refs_0_, ...), custom_call_target="tpu_custom_call" | custom-call | flops 50000000 | bytes 3538952 | tf_op jit(solution)/shard_map/project/pallas_call | solution.py:40
  38.5 0.0 copy-start.3
  38.6 0.1 collective-permute-start.9
  38.6 0.0 collective-permute-done.10.there_ref
  38.6 0.6 %pair_join.1.refs_0_ = bf16[400,128]{1,0:T(8,128)(2,1)S(1)} custom-call(s32[2]{0:T(128)S(1)} %pad_add_fusion.1.place_ref, bf16[800,128]{1,0:T(8,128)(2,1)S(1)} %get-tuple-element.45.here_ref, bf16[800,128]{1,0:T(8,128)(2,1)S(1)} %collective-permute-done.10.there_ref), custom_call_target="tpu_custom_call" | custom-call | flops 5000000000 | bytes 512008 | tf_op jit(solution)/shard_map/pair_join/pallas_call | solution.py:40
  39.2 0.3 collective-permute-start.12
  39.6 0.4 collective-permute-start.13
  40.0 1.1 %local_grads.1 = (f32[128,512]{1,0:T(8,128)S(1)}, f32[128,512]{1,0:T(8,128)S(1)}) custom-call(bf16[144,1536]{1,0:T(8,128)(2,1)S(1)} %pad_add_fusion.rows_ref, bf16[128,512]{1,0:T(8,128)(2,1)S(1)} %cotangent.1.cot_ref, bf16[128,512]{1,0:T(8,128)(2,1)S(1)} %get-tuple-element.51.sol_ref, bf16[128,512]{1,0:T(8,128)(2,1)S(1)} %copy-done.3), custom_call_target="tpu_custom_call" | custom-call | flops 1100000000 | bytes 1359872 | tf_op jit(solution)/shard_map/local_grads/pallas_call | solution.py:40
  41.1 0.0 collective-permute-done.9.got_ref.refs_2_
  41.2 1.6 %collective-permute-start.11 = (bf16[128,512]{1,0:T(8,128)(2,1)S(1)}, bf16[128,512]{1,0:T(8,128)(2,1)S(1)}, u32[]{:S(2)}, u32[]{:S(2)}) collective-permute-start(bf16[128,512]{1,0:T(8,128)(2,1)S(1)} %get-tuple-element.48), channel_id=1, source_target_pairs={{0,2},{1,3},{2,0},{3,1},{4,6},{5,7},{6,4},{7,5},{8,10},{9,11},{10,... | collective-permute-start | bytes 393224 | tf_op jit(solution)/shard_map/ppermute | solution.py:370
  42.8 1.9 %collective-permute-start.16 = (bf16[128,512]{1,0:T(8,128)(2,1)S(1)}, bf16[128,512]{1,0:T(8,128)(2,1)S(1)}, u32[]{:S(2)}, u32[]{:S(2)}) collective-permute-start(bf16[128,512]{1,0:T(8,128)(2,1)S(1)} %collective-permute-done.8.refs_5_), channel_id=1, source_target_pairs={{0,8},{4,12},{8,0},{12,4},{16,24},{20,28},{24,16},{28,20},{1,9},{5... | collective-permute-start | bytes 393224 | tf_op jit(solution)/shard_map/ppermute | solution.py:370
  44.7 1.4 %collective-permute-done.12.near_ref = bf16[400,128]{1,0:T(8,128)(2,1)S(1)} collective-permute-done((bf16[400,128]{1,0:T(8,128)(2,1)S(1)}, bf16[400,128]{1,0:T(8,128)(2,1)S(1)}, u32[]{:S(2)}, u32[]{:S(2)}) %collective-permute-start.12) | collective-permute-done | bytes 102432 | tf_op jit(solution)/shard_map/ppermute | solution.py:365
  46.1 1.8 %collective-permute-done.13.far_ref = bf16[400,128]{1,0:T(8,128)(2,1)S(1)} collective-permute-done((bf16[400,128]{1,0:T(8,128)(2,1)S(1)}, bf16[400,128]{1,0:T(8,128)(2,1)S(1)}, u32[]{:S(2)}, u32[]{:S(2)}) %collective-permute-start.13) | collective-permute-done | bytes 102432 | tf_op jit(solution)/shard_map/ppermute | solution.py:365
  47.9 1.9 %collective-permute-start.14 = (bf16[400,128]{1,0:T(8,128)(2,1)S(1)}, bf16[400,128]{1,0:T(8,128)(2,1)S(1)}, u32[]{:S(2)}, u32[]{:S(2)}) collective-permute-start(bf16[400,128]{1,0:T(8,128)(2,1)S(1)} %join_states.3.mine_ref), channel_id=1, source_target_pairs={{0,4},{4,0},{8,12},{12,8},{16,20},{20,16},{24,28},{28,24},{1,5},{5... | collective-permute-start | bytes 307208 | tf_op jit(solution)/shard_map/ppermute | solution.py:370
  49.9 1.2 %pair_grad.1 = (f32[256,512]{1,0:T(8,128)S(1)}, bf16[256,512]{1,0:T(8,128)(2,1)S(1)}) custom-call(s32[2]{0:T(128)S(1)} %pad_add_fusion.1.place_ref, bf16[128,512]{1,0:T(8,128)(2,1)S(1)} %collective-permute-done.6.refs_0_, bf16[128,512]{1,0:T(8,128)(2,1)S(1)} %collective-permute-done.7.refs_1_, bf16[512,512]{1,0:T(8,128)(2,1)S(1)} %collective-permute-done.9.got_ref.refs_2_, ...), custom_call_target="tpu_custom_call" | custom-call | flops 1500000000 | bytes 2097160 | tf_op jit(solution)/shard_map/pair_grad/pallas_call | solution.py:40
  51.1 1.5 %collective-permute-start.17 = (bf16[256,512]{1,0:T(8,128)(2,1)S(1)}, bf16[256,512]{1,0:T(8,128)(2,1)S(1)}, u32[]{:S(2)}, u32[]{:S(2)}) collective-permute-start(bf16[256,512]{1,0:T(8,128)(2,1)S(1)} %get-tuple-element.58), channel_id=1, source_target_pairs={{0,4},{4,0},{8,12},{12,8},{16,20},{20,16},{24,28},{28,24},{1,5},{5... | collective-permute-start | bytes 786440 | tf_op jit(solution)/shard_map/ppermute | solution.py:370
  52.6 0.1 collective-permute-done.14.theirs_ref
  52.7 1.6 %final_grads.1 = (bf16[128,512]{1,0:T(8,128)(2,1)}, bf16[128,512]{1,0:T(8,128)(2,1)}) custom-call(s32[2]{0:T(128)S(1)} %pad_add_fusion.1.place_ref, bf16[144,1536]{1,0:T(8,128)(2,1)S(1)} %pad_add_fusion.rows_ref, bf16[800,128]{1,0:T(8,128)(2,1)S(1)} %collective-permute-done.10.there_ref, bf16[400,128]{1,0:T(8,128)(2,1)S(1)} %join_states.3.mine_ref, ...), custom_call_target="tpu_custom_call" | custom-call | flops 1000000000 | bytes 1638408 | tf_op jit(solution)/shard_map/final_grads/pallas_call | solution.py:40
  54.2 0.0 collective-permute-done.11
  54.2 0.7 %add_convert_fusion = bf16[128,512]{1,0:T(8,128)(2,1)} fusion(f32[128,512]{1,0:T(8,128)S(1)} %get-tuple-element.47, bf16[128,512]{1,0:T(8,128)(2,1)S(1)} %collective-permute-done.11), kind=kLoop, calls=%fused_computation.2 | loop fusion | flops 196608 | bytes 524288 | tf_op jit(solution)/shard_map/convert_element_type | solution.py:529
  54.9 3.7 %collective-permute-done.17 = bf16[256,512]{1,0:T(8,128)(2,1)S(1)} collective-permute-done((bf16[256,512]{1,0:T(8,128)(2,1)S(1)}, bf16[256,512]{1,0:T(8,128)(2,1)S(1)}, u32[]{:S(2)}, u32[]{:S(2)}) %collective-permute-start.17) | collective-permute-done | bytes 262176 | tf_op jit(solution)/shard_map/ppermute | solution.py:370
  58.7 0.9 %convert_add_fusion = f32[256,512]{1,0:T(8,128)} fusion(f32[256,512]{1,0:T(8,128)S(1)} %get-tuple-element.57, bf16[256,512]{1,0:T(8,128)(2,1)S(1)} %collective-permute-done.17), kind=kLoop, calls=%fused_computation | loop fusion | flops 262144 | bytes 1310720 | tf_op jit(solution)/shard_map/add | solution.py:555
  (12 shorter events, 0.1 us)
Async XLA Ops:
  0.6 6.9 %copy-start.1 = (bf16[128,512]{1,0:T(8,128)(2,1)S(1)}, bf16[128,512]{1,0:T(8,128)(2,1)}, u32[]{:S(2)}) copy-start(bf16[128,512]{1,0:T(8,128)(2,1)} %refs_0_) | copy-start | bytes 393220
  1.3 17.2 %copy-start = (bf16[512,2048]{1,0:T(8,128)(2,1)S(1)}, bf16[512,2048]{1,0:T(8,128)(2,1)}, u32[]{:S(2)}) copy-start(bf16[512,2048]{1,0:T(8,128)(2,1)} %weight_ref.1) | copy-start | bytes 6291460
  2.9 13.0 %collective-permute-start = (bf16[800,128]{1,0:T(8,128)(2,1)S(1)}, bf16[800,128]{1,0:T(8,128)(2,1)S(1)}, u32[]{:S(2)}, u32[]{:S(2)}) collective-permute-start(bf16[800,128]{1,0:T(8,128)(2,1)S(1)} %tail_states.1), channel_id=1, source_target_pairs={{0,4},{4,8},{8,12},{12,16},{16,20},{20,24},{24,28},{28,0},{1,5},{5... | collective-permute-start | bytes 614408 | tf_op jit(solution)/shard_map/ppermute | solution.py:365
  5.9 10.0 %collective-permute-start.1 = (bf16[800,128]{1,0:T(8,128)(2,1)S(1)}, bf16[800,128]{1,0:T(8,128)(2,1)S(1)}, u32[]{:S(2)}, u32[]{:S(2)}) collective-permute-start(bf16[800,128]{1,0:T(8,128)(2,1)S(1)} %tail_states.1), channel_id=1, source_target_pairs={{0,8},{4,12},{8,16},{12,20},{16,24},{20,28},{24,0},{28,4},{1,9},{5... | collective-permute-start | bytes 614408 | tf_op jit(solution)/shard_map/ppermute | solution.py:365
  7.5 1.9 %collective-permute-start.2 = (bf16[128,512]{1,0:T(8,128)(2,1)S(1)}, bf16[128,512]{1,0:T(8,128)(2,1)S(1)}, u32[]{:S(2)}, u32[]{:S(2)}) collective-permute-start(bf16[128,512]{1,0:T(8,128)(2,1)S(1)} %copy-done.1), channel_id=1, source_target_pairs={{0,1},{1,0},{2,3},{3,2},{4,5},{5,4},{6,7},{7,6},{8,9},{9,8},{10,11... | collective-permute-start | bytes 393224 | tf_op jit(solution)/shard_map/ppermute | solution.py:370
  7.5 6.3 %collective-permute-start.3 = (bf16[128,512]{1,0:T(8,128)(2,1)S(1)}, bf16[128,512]{1,0:T(8,128)(2,1)S(1)}, u32[]{:S(2)}, u32[]{:S(2)}) collective-permute-start(bf16[128,512]{1,0:T(8,128)(2,1)S(1)} %copy-done.1), channel_id=1, source_target_pairs={{0,2},{1,3},{2,0},{3,1},{4,6},{5,7},{6,4},{7,5},{8,10},{9,11},{10,... | collective-permute-start | bytes 393224 | tf_op jit(solution)/shard_map/ppermute | solution.py:370
  9.0 6.9 %collective-permute-start.4 = (bf16[128,512]{1,0:T(8,128)(2,1)S(1)}, bf16[128,512]{1,0:T(8,128)(2,1)}, u32[]{:S(2)}, u32[]{:S(2)}) collective-permute-start(bf16[128,512]{1,0:T(8,128)(2,1)S(1)} %copy-done.1), channel_id=1, source_target_pairs={{0,3},{1,2},{2,1},{3,0},{4,7},{5,6},{6,5},{7,4},{8,11},{9,10},{10,... | collective-permute-start | bytes 393224 | tf_op jit(solution)/shard_map/ppermute | solution.py:370
  16.0 9.2 %collective-permute-start.5 = (bf16[800,128]{1,0:T(8,128)(2,1)S(1)}, bf16[800,128]{1,0:T(8,128)(2,1)S(1)}, u32[]{:S(2)}, u32[]{:S(2)}) collective-permute-start(bf16[800,128]{1,0:T(8,128)(2,1)S(1)} %join_states.2.near_ref), channel_id=1, source_target_pairs={{0,8},{4,12},{8,16},{12,20},{16,24},{20,28},{24,0},{28,4},{1,9},{5... | collective-permute-start | bytes 614408 | tf_op jit(solution)/shard_map/ppermute | solution.py:365
  17.7 7.5 %copy-start.2 = (f32[4]{0:T(128)S(1)}, f32[4]{0:T(128)}, u32[]{:S(2)}) copy-start(f32[4]{0:T(128)} %ridge_ref.1) | copy-start | bytes 52
  17.7 14.8 %collective-permute-start.6 = (bf16[128,512]{1,0:T(8,128)(2,1)S(1)}, bf16[128,512]{1,0:T(8,128)(2,1)S(1)}, u32[]{:S(2)}, u32[]{:S(2)}) collective-permute-start(bf16[128,512]{1,0:T(8,128)(2,1)S(1)} %copy-done.1), channel_id=1, source_target_pairs={{0,0},{1,8},{2,16},{3,24},{4,4},{5,12},{6,20},{7,28},{8,1},{9,9},{... | collective-permute-start | bytes 393224 | tf_op jit(solution)/shard_map/ppermute | solution.py:433
  29.0 9.6 %collective-permute-start.10 = (bf16[800,128]{1,0:T(8,128)(2,1)S(1)}, bf16[800,128]{1,0:T(8,128)(2,1)S(1)}, u32[]{:S(2)}, u32[]{:S(2)}) collective-permute-start(bf16[800,128]{1,0:T(8,128)(2,1)S(1)} %get-tuple-element.45.here_ref), channel_id=1, source_target_pairs={{0,4},{4,0},{8,12},{12,8},{16,20},{20,16},{24,28},{28,24},{1,5},{5... | collective-permute-start | bytes 614408 | tf_op jit(solution)/shard_map/ppermute | solution.py:370
  32.5 5.0 %collective-permute-start.7 = (bf16[128,512]{1,0:T(8,128)(2,1)S(1)}, bf16[128,512]{1,0:T(8,128)(2,1)S(1)}, u32[]{:S(2)}, u32[]{:S(2)}) collective-permute-start(bf16[128,512]{1,0:T(8,128)(2,1)S(1)} %collective-permute-done.6.refs_0_), channel_id=1, source_target_pairs={{0,2},{1,3},{2,0},{3,1},{4,6},{5,7},{6,4},{7,5},{8,10},{9,11},{10,... | collective-permute-start | bytes 393224 | tf_op jit(solution)/shard_map/ppermute | solution.py:370
  32.5 8.6 %collective-permute-start.8 = (bf16[128,512]{1,0:T(8,128)(2,1)S(1)}, bf16[128,512]{1,0:T(8,128)(2,1)S(1)}, u32[]{:S(2)}, u32[]{:S(2)}) collective-permute-start(bf16[128,512]{1,0:T(8,128)(2,1)S(1)} %get-tuple-element.41.mixed_ref.refs_3_), channel_id=1, source_target_pairs={{0,16},{4,20},{8,24},{12,28},{16,0},{20,4},{24,8},{28,12},{1,17},{... | collective-permute-start | bytes 393224 | tf_op jit(solution)/shard_map/ppermute | solution.py:370
  34.7 15.2 %collective-permute-start.15 = (bf16[128,512]{1,0:T(8,128)(2,1)S(1)}, bf16[128,512]{1,0:T(8,128)(2,1)S(1)}, u32[]{:S(2)}, u32[]{:S(2)}) collective-permute-start(bf16[128,512]{1,0:T(8,128)(2,1)S(1)} %get-tuple-element.41.mixed_ref.refs_3_), channel_id=1, source_target_pairs={{0,8},{4,12},{8,0},{12,4},{16,24},{20,28},{24,16},{28,20},{1,9},{5... | collective-permute-start | bytes 393224 | tf_op jit(solution)/shard_map/ppermute | solution.py:370
  38.5 1.5 %copy-start.3 = (bf16[128,512]{1,0:T(8,128)(2,1)S(1)}, bf16[128,512]{1,0:T(8,128)(2,1)}, u32[]{:S(2)}) copy-start(bf16[128,512]{1,0:T(8,128)(2,1)} %get-tuple-element.28.dual_ref) | copy-start | bytes 393220
  38.6 2.6 %collective-permute-start.9 = (bf16[512,512]{1,0:T(8,128)(2,1)S(1)}, bf16[512,512]{1,0:T(8,128)(2,1)S(1)}, u32[]{:S(2)}, u32[]{:S(2)}) collective-permute-start(bf16[512,512]{1,0:T(8,128)(2,1)S(1)} %get-tuple-element.44), channel_id=1, source_target_pairs={{0,1},{1,0},{2,3},{3,2},{4,5},{5,4},{6,7},{7,6},{8,9},{9,8},{10,11... | collective-permute-start | bytes 1572872 | tf_op jit(solution)/shard_map/ppermute | solution.py:370
  39.2 6.9 %collective-permute-start.12 = (bf16[400,128]{1,0:T(8,128)(2,1)S(1)}, bf16[400,128]{1,0:T(8,128)(2,1)S(1)}, u32[]{:S(2)}, u32[]{:S(2)}) collective-permute-start(bf16[400,128]{1,0:T(8,128)(2,1)S(1)} %pair_join.1.refs_0_), channel_id=1, source_target_pairs={{0,24},{4,28},{8,0},{12,4},{16,8},{20,12},{24,16},{28,20},{1,25},{... | collective-permute-start | bytes 307208 | tf_op jit(solution)/shard_map/ppermute | solution.py:365
  39.6 8.3 %collective-permute-start.13 = (bf16[400,128]{1,0:T(8,128)(2,1)S(1)}, bf16[400,128]{1,0:T(8,128)(2,1)S(1)}, u32[]{:S(2)}, u32[]{:S(2)}) collective-permute-start(bf16[400,128]{1,0:T(8,128)(2,1)S(1)} %pair_join.1.refs_0_), channel_id=1, source_target_pairs={{0,16},{4,20},{8,24},{12,28},{16,0},{20,4},{24,8},{28,12},{1,17},{... | collective-permute-start | bytes 307208 | tf_op jit(solution)/shard_map/ppermute | solution.py:365
  41.2 13.1 %collective-permute-start.11 = (bf16[128,512]{1,0:T(8,128)(2,1)S(1)}, bf16[128,512]{1,0:T(8,128)(2,1)S(1)}, u32[]{:S(2)}, u32[]{:S(2)}) collective-permute-start(bf16[128,512]{1,0:T(8,128)(2,1)S(1)} %get-tuple-element.48), channel_id=1, source_target_pairs={{0,2},{1,3},{2,0},{3,1},{4,6},{5,7},{6,4},{7,5},{8,10},{9,11},{10,... | collective-permute-start | bytes 393224 | tf_op jit(solution)/shard_map/ppermute | solution.py:370
  42.8 7.1 %collective-permute-start.16 = (bf16[128,512]{1,0:T(8,128)(2,1)S(1)}, bf16[128,512]{1,0:T(8,128)(2,1)S(1)}, u32[]{:S(2)}, u32[]{:S(2)}) collective-permute-start(bf16[128,512]{1,0:T(8,128)(2,1)S(1)} %collective-permute-done.8.refs_5_), channel_id=1, source_target_pairs={{0,8},{4,12},{8,0},{12,4},{16,24},{20,28},{24,16},{28,20},{1,9},{5... | collective-permute-start | bytes 393224 | tf_op jit(solution)/shard_map/ppermute | solution.py:370
  47.9 4.7 %collective-permute-start.14 = (bf16[400,128]{1,0:T(8,128)(2,1)S(1)}, bf16[400,128]{1,0:T(8,128)(2,1)S(1)}, u32[]{:S(2)}, u32[]{:S(2)}) collective-permute-start(bf16[400,128]{1,0:T(8,128)(2,1)S(1)} %join_states.3.mine_ref), channel_id=1, source_target_pairs={{0,4},{4,0},{8,12},{12,8},{16,20},{20,16},{24,28},{28,24},{1,5},{5... | collective-permute-start | bytes 307208 | tf_op jit(solution)/shard_map/ppermute | solution.py:370
  51.1 7.6 %collective-permute-start.17 = (bf16[256,512]{1,0:T(8,128)(2,1)S(1)}, bf16[256,512]{1,0:T(8,128)(2,1)S(1)}, u32[]{:S(2)}, u32[]{:S(2)}) collective-permute-start(bf16[256,512]{1,0:T(8,128)(2,1)S(1)} %get-tuple-element.58), channel_id=1, source_target_pairs={{0,4},{4,0},{8,12},{12,8},{16,20},{20,16},{24,28},{28,24},{1,5},{5... | collective-permute-start | bytes 786440 | tf_op jit(solution)/shard_map/ppermute | solution.py:370
